TPU v7x, 32 devices: a whole 2x2x4 slice. The times are simulated.
32 devices in a mesh: section: 2 (over core), seq: 4 (over y, x), dp: 4 (over z).
Axes of the slice: x: 2, y: 2, z: 4, core: 2. Of those that a mesh axis runs over, the one named last changes fastest.
Arguments:
- section_inputs: bfloat16 [2, 2, 8, 736, 1152], P('section', None, 'dp', 'seq'), may hold values from -6 to 6
- key_mask: int32 [2, 8, 736], P(None, 'dp'), may hold values from 0 to 1, as said below
- attention_in: bfloat16 [2, 1152, 3456], P('section', 'dp'), may hold values from -0.25 to 0.25
- attention_out: bfloat16 [2, 1152, 1152], P('section', 'dp'), may hold values from -0.5 to 0.5
- expand_weight: bfloat16 [2, 1152, 4304], P('section', 'dp'), may hold values from -0.1875 to 0.1875
- contract_weight: bfloat16 [2, 4304, 1152], P('section', 'dp'), may hold values from -0.125 to 0.125
- norm_gains: bfloat16 [2, 2, 1152], P('section', None, 'dp'), may hold values from 0.099609375 to 1.8984375
- biases: bfloat16 [2, 6, 1152], P('section', None, 'dp'), may hold values from -1.796875 to 1.796875
- expand_bias: bfloat16 [2, 4304], P('section', 'dp'), may hold values from -1.796875 to 1.796875
Outputs:
- section_results: float32 [2, 2, 8, 736, 1152], P('section', None, 'dp', 'seq')
- attention_in_grad: float32 [2, 1152, 3456], P('section', 'dp')
- attention_out_grad: float32 [2, 1152, 1152], P('section', 'dp')
- expand_weight_grad: float32 [2, 1152, 4304], P('section', 'dp')
- contract_weight_grad: float32 [2, 4304, 1152], P('section', 'dp')
- norm_gains_grad: float32 [2, 2, 1152], P('section', None, 'dp')
- biases_grad: float32 [2, 6, 1152], P('section', None, 'dp')
- expand_bias_grad: float32 [2, 4304], P('section', 'dp')
Inputs may be any that keep to these rules, and one draw needn't show every extreme that they name: `key_mask`: each image has exactly 7 padding positions (zeros), placed anywhere among its 736 positions.
All inputs are finite; a program needn't handle non-finite values.
Results may differ from a plain program's by a relative error of at most 0.025.
Values may be sent and summed in bfloat16 or wider, within the bound.
No kernel may reach another device: no remote copies, remote signals or barrier semaphores. Data moves between devices by JAX's collectives and lax.ppermute only.
A program may use at most 384 MiB of HBM per device.

v0:
```python
import jax
import jax.numpy as jnp
from jax import lax
from jax.sharding import PartitionSpec as P

HEAD_DIM = 72
MB = 2


def passed_along(value, axis, steps):
    count = lax.axis_size(axis)
    initial, last = (max(0, -steps), min(count, count - steps))
    return lax.ppermute(value, axis, [(source, source + steps) for source in range(initial, last)])


def layer_norm(stream, gain, shift):
    centre = jnp.mean(stream, axis=-1, keepdims=True)
    offset = stream - centre
    spread = jnp.mean(offset * offset, axis=-1, keepdims=True)
    return offset * lax.rsqrt(spread + 1e-06) * gain + shift


def matmul(left, right):
    return jnp.dot(left, right, preferred_element_type=jnp.float32)


def left_matmul(left, right):
    return lax.dot_general(
        left, right, (((0,), (0,)), ((), ())), preferred_element_type=jnp.float32
    )


def right_matmul(left, right):
    return lax.dot_general(
        left, right, (((1,), (1,)), ((), ())), preferred_element_type=jnp.float32
    )


def gather_once(local):
    whole = (
        lax.all_gather(local[0], "dp", axis=1, tiled=True),
        lax.all_gather(local[1], "dp", axis=1, tiled=True),
        lax.all_gather(local[2], "dp", axis=1, tiled=True),
        lax.all_gather(local[3], "dp", axis=1, tiled=True),
        lax.all_gather(local[4], "dp", axis=2, tiled=True),
        lax.all_gather(local[5], "dp", axis=2, tiled=True),
        lax.all_gather(local[6], "dp", axis=1, tiled=True),
    )
    return tuple((piece[0] for piece in whole))


def split_heads(heads):
    images, length, _, width = heads.shape
    count = width // HEAD_DIM
    queries = heads[:, :, 0].reshape(images, length, count, HEAD_DIM)
    key_rows = heads[:, :, 1].reshape(images, length, count, HEAD_DIM)
    value_rows = heads[:, :, 2].reshape(images, length, count, HEAD_DIM)
    return (queries, key_rows, value_rows)


def head_scores(queries, key_rows, visible):
    scores = jnp.einsum(
        "nqhd,nkhd->nhqk", queries, key_rows, preferred_element_type=jnp.float32
    ) * HEAD_DIM ** (-0.5)
    return jnp.where(visible[:, None, None, :], scores, -1000000000.0)


def attend(heads, visible):
    images, length, _, width = heads.shape
    queries, key_rows, value_rows = split_heads(heads)
    scores = head_scores(queries, key_rows, visible)
    row_max = jnp.max(scores, axis=-1, keepdims=True)
    expon = jnp.exp(scores - row_max)
    total = jnp.sum(expon, axis=-1, keepdims=True)
    softmaxed = (expon / total).astype(jnp.bfloat16)
    log_total = (row_max + jnp.log(total))[..., 0]
    mixture = jnp.einsum(
        "nhqk,nkhd->nqhd", softmaxed, value_rows, preferred_element_type=jnp.float32
    )
    return (mixture.astype(jnp.bfloat16).reshape(images, length, width), log_total)


def attend_back(heads, log_total, visible, d_mixture):
    images, length, _, width = heads.shape
    queries, key_rows, value_rows = split_heads(heads)
    d_rows = d_mixture.reshape(queries.shape)
    scores = head_scores(queries, key_rows, visible)
    softmaxed = jnp.exp(scores - log_total[..., None])
    d_soft = jnp.einsum("nqhd,nkhd->nhqk", d_rows, value_rows, preferred_element_type=jnp.float32)
    inner = jnp.sum(softmaxed * d_soft, axis=-1, keepdims=True)
    d_scores = (softmaxed * (d_soft - inner)).astype(jnp.bfloat16)
    scale = HEAD_DIM ** (-0.5)
    d_queries = (
        jnp.einsum("nhqk,nkhd->nqhd", d_scores, key_rows, preferred_element_type=jnp.float32)
        * scale
    ).astype(jnp.bfloat16)
    d_keys = (
        jnp.einsum("nhqk,nqhd->nkhd", d_scores, queries, preferred_element_type=jnp.float32) * scale
    ).astype(jnp.bfloat16)
    d_values = jnp.einsum(
        "nhqk,nqhd->nkhd",
        softmaxed.astype(jnp.bfloat16),
        d_rows,
        preferred_element_type=jnp.float32,
    ).astype(jnp.bfloat16)
    return jnp.stack([d_queries, d_keys, d_values], axis=2).reshape(images, length, 3, width)


def forward_layer(stream_in, visible, params):
    attn_in, attn_out, expand, contract, gains, shifts, expand_shift = params
    images, rows_seq, width = stream_in.shape
    stream = stream_in.astype(jnp.float32).reshape(-1, width)
    gains32 = gains.astype(jnp.float32)
    shifts32 = shifts.astype(jnp.float32)
    normed = layer_norm(stream, gains32[0], shifts32[0]).astype(jnp.bfloat16)
    qkv_shift = jnp.stack([shifts32[2], jnp.zeros_like(shifts32[2]), shifts32[3]])
    projected = (matmul(normed, attn_in).reshape(images, rows_seq, 3, width) + qkv_shift).astype(
        jnp.bfloat16
    )
    heads = lax.all_to_all(projected, "seq", split_axis=3, concat_axis=1, tiled=True)
    mixture, log_total = attend(heads, visible)
    mixed_rows = lax.all_to_all(mixture, "seq", split_axis=1, concat_axis=2, tiled=True).reshape(
        -1, width
    )
    middle = stream + matmul(mixed_rows, attn_out) + shifts32[4]
    normed_mid = layer_norm(middle, gains32[1], shifts32[1]).astype(jnp.bfloat16)
    hidden_pre = matmul(normed_mid, expand) + expand_shift.astype(jnp.float32)
    hidden = jax.nn.gelu(hidden_pre, approximate=True).astype(jnp.bfloat16)
    result = middle + matmul(hidden, contract) + shifts32[5]
    saved = (
        stream_in,
        normed,
        heads,
        log_total,
        mixed_rows,
        middle,
        normed_mid,
        hidden_pre,
        hidden,
        visible,
    )
    return (result.reshape(images, rows_seq, width), saved)


def backward_layer(d_result, saved, params):
    attn_in, attn_out, expand, contract, gains, shifts, expand_shift = params
    (
        stream_in,
        normed,
        heads,
        log_total,
        mixed_rows,
        middle,
        normed_mid,
        hidden_pre,
        hidden,
        visible,
    ) = saved
    images, rows_seq, width = d_result.shape
    gains32 = gains.astype(jnp.float32)
    shifts32 = shifts.astype(jnp.float32)
    d_flat = d_result.reshape(-1, width)
    d_wide = d_flat.astype(jnp.float32)
    grad_contract = left_matmul(hidden, d_flat)
    grad_last_bias = jnp.sum(d_wide, axis=0)
    d_hidden = right_matmul(d_flat, contract)
    _, gelu_back = jax.vjp(lambda inner: jax.nn.gelu(inner, approximate=True), hidden_pre)
    d_pre = gelu_back(d_hidden)[0].astype(jnp.bfloat16)
    grad_expand = left_matmul(normed_mid, d_pre)
    grad_expand_bias = jnp.sum(d_pre.astype(jnp.float32), axis=0)
    d_normed_mid = right_matmul(d_pre, expand)
    _, norm_back_mid = jax.vjp(layer_norm, middle, gains32[1], shifts32[1])
    d_middle_part, grad_gain_mid, grad_shift_mid = norm_back_mid(d_normed_mid)
    d_middle = d_wide + d_middle_part
    d_branch = d_middle.astype(jnp.bfloat16)
    grad_out_bias = jnp.sum(d_branch.astype(jnp.float32), axis=0)
    grad_attn_out = left_matmul(mixed_rows, d_branch)
    d_mixture = (
        right_matmul(d_branch, attn_out).astype(jnp.bfloat16).reshape(images, rows_seq, width)
    )
    d_heads = lax.all_to_all(d_mixture, "seq", split_axis=2, concat_axis=1, tiled=True)
    d_projected_heads = attend_back(heads, log_total, visible, d_heads)
    d_projected = lax.all_to_all(
        d_projected_heads, "seq", split_axis=1, concat_axis=3, tiled=True
    ).reshape(-1, 3 * width)
    grad_attn_in = left_matmul(normed, d_projected)
    column_sums = jnp.sum(d_projected.astype(jnp.float32), axis=0).reshape(3, width)
    d_normed = right_matmul(d_projected, attn_in)
    stream = stream_in.astype(jnp.float32).reshape(-1, width)
    _, norm_back_in = jax.vjp(layer_norm, stream, gains32[0], shifts32[0])
    d_stream_part, grad_gain_in, grad_shift_in = norm_back_in(d_normed)
    d_stream = d_middle + d_stream_part
    grad_gains = jnp.stack([grad_gain_in, grad_gain_mid])
    grad_shifts = jnp.stack(
        [
            grad_shift_in,
            grad_shift_mid,
            column_sums[0],
            column_sums[2],
            grad_out_bias,
            grad_last_bias,
        ]
    )
    grads = (
        grad_attn_in,
        grad_attn_out,
        grad_expand,
        grad_contract,
        grad_gains,
        grad_shifts,
        grad_expand_bias,
    )
    return (d_stream.reshape(images, rows_seq, width), grads)


def send_forward(values):
    return passed_along(values, "section", 1)


def send_backward(values):
    return passed_along(values, "section", -1)


def on_device(
    section_inputs,
    key_mask,
    attention_in,
    attention_out,
    expand_weight,
    contract_weight,
    norm_gains,
    biases,
    expand_bias,
):
    leading = lax.axis_index("section") == 0
    local = (
        attention_in,
        attention_out,
        expand_weight,
        contract_weight,
        norm_gains,
        biases,
        expand_bias,
    )
    sources = section_inputs[0]
    visible_all = key_mask > 0
    blank = jnp.zeros_like(sources[0])
    recv_forward = blank
    recv_backward = blank
    saves = {}
    outputs = [None] * MB
    input_grads = [None] * MB
    totals = None
    params = gather_once(local)
    for tick in range(MB + 2):
        if tick <= MB:
            source = sources[tick] if tick < MB else blank
            stream_now = jnp.where(leading, source, recv_forward)
            visible_now = jnp.where(
                leading, visible_all[min(tick, MB - 1)], visible_all[max(tick - 1, 0)]
            )
            result, saved = forward_layer(stream_now, visible_now, params)
            saves[tick] = saved
            if tick >= 1:
                outputs[tick - 1] = result
            sent_forward = send_forward(result.astype(jnp.bfloat16))
        if tick >= 1:
            early = saves[tick - 2] if tick - 2 in saves else saves[tick]
            later = saves[tick] if tick in saves else saves[tick - 2]
            chosen = jax.tree.map(
                lambda left_one, right_one: jnp.where(leading, left_one, right_one), early, later
            )
            cotangent = sources[tick - 1] if tick <= MB else blank
            d_result = jnp.where(leading, recv_backward, cotangent)
            d_stream, grads = backward_layer(d_result, chosen, params)
            active = jnp.where(leading, tick >= 2, tick <= MB)
            grads = tuple((jnp.where(active, piece, 0.0) for piece in grads))
            if tick >= 2:
                input_grads[tick - 2] = d_stream
            totals = (
                grads if totals is None else tuple((old + new for old, new in zip(totals, grads)))
            )
            recv_backward = send_backward(d_stream.astype(jnp.bfloat16))
        if tick <= MB:
            recv_forward = sent_forward
    totals = (
        lax.psum_scatter(
            totals[0].astype(jnp.bfloat16), "dp", scatter_dimension=0, tiled=True
        ).astype(jnp.float32),
        lax.psum_scatter(
            totals[1].astype(jnp.bfloat16), "dp", scatter_dimension=0, tiled=True
        ).astype(jnp.float32),
        lax.psum_scatter(
            totals[2].astype(jnp.bfloat16), "dp", scatter_dimension=0, tiled=True
        ).astype(jnp.float32),
        lax.psum_scatter(
            totals[3].astype(jnp.bfloat16), "dp", scatter_dimension=0, tiled=True
        ).astype(jnp.float32),
        lax.psum_scatter(
            totals[4].astype(jnp.bfloat16), "dp", scatter_dimension=1, tiled=True
        ).astype(jnp.float32),
        lax.psum_scatter(
            totals[5].astype(jnp.bfloat16), "dp", scatter_dimension=1, tiled=True
        ).astype(jnp.float32),
        lax.psum_scatter(
            totals[6].astype(jnp.bfloat16), "dp", scatter_dimension=0, tiled=True
        ).astype(jnp.float32),
    )
    totals = (
        lax.psum(totals[0].astype(jnp.bfloat16), "seq").astype(jnp.float32),
        lax.psum(totals[1].astype(jnp.bfloat16), "seq").astype(jnp.float32),
        lax.psum(totals[2].astype(jnp.bfloat16), "seq").astype(jnp.float32),
        lax.psum(totals[3].astype(jnp.bfloat16), "seq").astype(jnp.float32),
        lax.psum(totals[4].astype(jnp.bfloat16), "seq").astype(jnp.float32),
        lax.psum(totals[5].astype(jnp.bfloat16), "seq").astype(jnp.float32),
        lax.psum(totals[6].astype(jnp.bfloat16), "seq").astype(jnp.float32),
    )
    results = jnp.stack(
        [jnp.where(leading, input_grads[index], outputs[index]) for index in range(MB)]
    )[None]
    return (
        results,
        totals[0][None],
        totals[1][None],
        totals[2][None],
        totals[3][None],
        totals[4][None],
        totals[5][None],
        totals[6][None],
    )


def solution(mesh):
    in_specs = (
        P("section", None, "dp", "seq", None),
        P(None, "dp", None),
        P("section", "dp", None),
        P("section", "dp", None),
        P("section", "dp", None),
        P("section", "dp", None),
        P("section", None, "dp"),
        P("section", None, "dp"),
        P("section", "dp"),
    )
    out_specs = (
        P("section", None, "dp", "seq", None),
        P("section", "dp", None),
        P("section", "dp", None),
        P("section", "dp", None),
        P("section", "dp", None),
        P("section", None, "dp"),
        P("section", None, "dp"),
        P("section", "dp"),
    )
    return jax.shard_map(
        on_device, mesh=mesh, in_specs=in_specs, out_specs=out_specs, check_vma=False
    )
```

profile of v0, /device:TPU:0, one launch (start us, length us, event | category | flops | bytes accessed | tf_op | source)
XLA Modules:
  0.0 2401.7 jit_solution(12540566179387140181)
XLA Ops:
  8.9 27.3 %copy.222 = bf16[1,1076,1152]{2,0,1:T(2,128)(2,1)} copy(bf16[1,1076,1152]{2,1,0:T(8,128)(2,1)S(1)} %copy-done.63) | data formatting | bytes 4958208 | tf_op args[5]
  37.0 26.0 %all_gather.23 = bf16[1,6,1152]{1,0,2:T(2,128)(2,1)S(1)} all-gather(bf16[1,6,288]{1,0,2:T(2,128)(2,1)S(1)} %copy.224), channel_id=1, replica_groups=mesh['section'=2,'seq'=4,'dp'=4] {'dp'}, dimensions={2}, use_global_device_ids=true | all-gather | bytes 17280 | tf_op jit(solution)/shard_map/all_gather | solution.py:46
  63.6 20.0 slice_reduce_fusion.1
  83.8 27.6 %all_gather.22 = bf16[1,2,1152]{1,0,2:T(2,128)(2,1)S(1)} all-gather(bf16[1,2,288]{1,0,2:T(2,128)(2,1)S(1)} %copy.223), channel_id=1, replica_groups=mesh['section'=2,'seq'=4,'dp'=4] {'dp'}, dimensions={2}, use_global_device_ids=true | all-gather | bytes 5760 | tf_op jit(solution)/shard_map/all_gather | solution.py:45
  114.4 18.9 slice_reduce_fusion.2
  133.4 40.5 %all-gather.7.cloned.1.call-done = bf16[1,1152,3456]{2,1,0:T(8,128)(2,1)} async-done(((bf16[1,288,3456]{2,1,0:T(8,128)(2,1)}), bf16[1,1152,3456]{2,1,0:T(8,128)(2,1)}) %all-gather.7.cloned.1.call-update) | async-done | bytes 7962640 | tf_op jit(solution)/shard_map/all_gather | solution.py:41
  173.9 11.5 copy.225
  185.4 10.6 add_convert_fusion.4
  212.4 38.9 %all-to-all-done = bf16[2,184,3,1152]{1,0,2,3:T(2,128)(2,1)S(1)} async-done(((bf16[2,184,3,1152]{1,0,2,3:T(2,128)(2,1)}), bf16[2,184,3,1152]{1,0,2,3:T(2,128)(2,1)S(1)}, u32[]{:S(2)}, u32[]{:S(2)}) %all-to-all-start) | async-done | bytes 2543648 | tf_op jit(solution)/shard_map/all_to_all | solution.py:120
  284.2 22.1 all-reduce
  316.2 252.5 %all-gather.5.cloned.1.call-done = bf16[1,4304,1152]{2,0,1:T(2,128)(2,1)} async-done(((bf16[1,1076,1152]{2,0,1:T(2,128)(2,1)}), bf16[1,4304,1152]{2,0,1:T(2,128)(2,1)}) %all-gather.5.cloned.1.call-update) | async-done | bytes 9916432 | tf_op jit(solution)/shard_map/all_gather | solution.py:44
  568.7 15.1 copy.322
  583.9 161.5 %all-gather.11.cloned.1.call-done = bf16[1,1152,4304]{2,1,0:T(8,128)(2,1)} async-done(((bf16[1,288,4304]{2,1,0:T(8,128)(2,1)}), bf16[1,1152,4304]{2,1,0:T(8,128)(2,1)}) %all-gather.11.cloned.1.call-update) | async-done | bytes 9916432 | tf_op jit(solution)/shard_map/all_gather | solution.py:43
  787.0 40.6 %all-to-all-done.2 = bf16[2,184,3,1152]{1,0,2,3:T(2,128)(2,1)} async-done(((bf16[2,184,3,1152]{1,0,2,3:T(2,128)(2,1)}), bf16[2,184,3,1152]{1,0,2,3:T(2,128)(2,1)}, u32[]{:S(2)}, u32[]{:S(2)}) %all-to-all-start.2) | async-done | bytes 2543648 | tf_op jit(solution)/shard_map/all_to_all | solution.py:120
  863.1 17.7 all_to_all.189
  887.0 10.6 fusion.55
  897.6 11.0 convert_reduce_fusion.5
  932.9 13.6 all-to-all-done.4
  953.0 13.7 multiply_reduce_fusion.2
  966.7 17.1 multiply_convert_fusion.2
  1031.7 11.8 fusion.198
  1045.8 22.9 all-to-all-done.5
  1119.3 40.5 %all-to-all-done.6 = bf16[2,184,3,1152]{1,0,2,3:T(2,128)(2,1)S(1)} async-done(((bf16[2,184,3,1152]{1,0,2,3:T(2,128)(2,1)}), bf16[2,184,3,1152]{1,0,2,3:T(2,128)(2,1)S(1)}, u32[]{:S(2)}, u32[]{:S(2)}) %all-to-all-start.6) | async-done | bytes 2543648 | tf_op jit(solution)/shard_map/all_to_all | solution.py:120
  1195.0 12.5 all-to-all-done.7
  1223.9 14.2 convert_reduce_fusion.4
  1279.3 13.7 multiply_reduce_fusion.1
  1293.1 17.3 multiply_convert_fusion.1
  1353.6 36.3 %all-to-all-done.9 = bf16[2,736,3,288]{3,0,2,1:T(2,128)(2,1)S(1)} async-done(((bf16[2,736,3,288]{3,0,2,1:T(2,128)(2,1)}), bf16[2,736,3,288]{3,0,2,1:T(2,128)(2,1)S(1)}, u32[]{:S(2)}, u32[]{:S(2)}) %all-to-all-start.9) | async-done | bytes 2543648 | tf_op jit(solution)/shard_map/all_to_all | solution.py:183
  1418.2 11.7 convert_reduce_fusion.3
  1479.6 12.8 multiply_reduce_fusion
  1492.5 17.3 multiply_convert_fusion
  1565.2 28.8 %all-to-all-done.11 = bf16[2,736,3,288]{3,0,2,1:T(2,128)(2,1)} async-done(((bf16[2,736,3,288]{3,0,2,1:T(2,128)(2,1)}), bf16[2,736,3,288]{3,0,2,1:T(2,128)(2,1)}, u32[]{:S(2)}, u32[]{:S(2)}) %all-to-all-start.11) | async-done | bytes 2543648 | tf_op jit(solution)/shard_map/all_to_all | solution.py:183
  1614.9 15.9 fusion.9
  1634.6 11.8 convolution_select_fusion.1
  1646.5 18.4 convolution_add_fusion
  1665.0 15.1 fusion.3
  1681.2 14.6 convolution_select_fusion.3
  1695.8 12.9 copy.306
  1737.2 14.8 convolution_select_fusion.2
  1752.0 28.2 %fusion.4 = bf16[4304,1152]{1,0:T(8,128)(2,1)} fusion(f32[4304,1152]{1,0:T(8,128)} %convolution_select_fusion.2, f32[4304,1152]{1,0:T(8,128)} %convolution_select_fusion.3, bf16[368,1152]{1,0:T(8,128)(2,1)S(1)} %bitcast.421, pred[]{:T(512)S(6)} %eq.3, f32[368,4304]{1,0:T(8,128)} %copy-done.23, f32[368,4304]{1,0:T(8,128)} %copy-done.22), kind=kOutput, calls=%fused_computation.12 | convolution fusion | flops 3694209280 | bytes 63100928 | tf_op jit(solution)/shard_map/dot_general | solution.py:28
  1780.2 322.1 %fusion = bf16[1088,1152]{1,0:T(8,128)(2,1)S(1)} fusion(bf16[4304,1152]{1,0:T(8,128)(2,1)} %fusion.4), kind=kCustom, calls=%all-reduce-scatter | all-reduce-scatter fusion | flops 5013505 | bytes 12423680
  2109.2 11.4 concatenate.3
  2120.6 13.0 copy.316
  2162.2 16.1 all-reduce.2
  2183.1 11.6 add_select_fusion
  2198.8 16.7 all-reduce.4
  2217.3 142.6 %all-reduce.8.cloned.1.call-done = (bf16[1,1076,1152]{2,1,0:T(8,128)(2,1)}, bf16[1,288,3456]{2,1,0:T(8,128)(2,1)}, bf16[1,288,1152]{2,1,0:T(8,128)(2,1)}, bf16[1,288,4304]{2,1,0:T(8,128)(2,1)}) async-done(((bf16[1,1076,1152]{2,1,0:T(8,128)(2,1)}, bf16[1,288,3456]{2,1,0:T(8,128)(2,1)}, bf16[1,288,1152]{2,1,0:T(8,128)(2,1)}, bf16[1,288,4304]{2,1,0:T(8,128)(2,1)}), (bf16[1,1076,1152]{2,1,0:T(8,128)(2,1)}, ...) | async-done | bytes 7612432 | tf_op jit(solution)/shard_map/psum | solution.py:313
  2364.4 26.9 %copy.283 = f32[1,1076,1152]{2,0,1:T(1,128)} copy(bf16[1,1076,1152]{2,1,0:T(8,128)(2,1)S(1)} %copy-done.64) | data formatting | bytes 7437312
  (680 shorter events, 654.0 us)
Async XLA Ops:
  7.2 166.7 %all-gather.7.cloned.1.call-start = ((), (), s32[]{:S(2)}) async-start(), calls=%async_computation.18 | async-start | bytes 9953280 | tf_op jit(solution)/shard_map/all_gather | solution.py:41
  7.9 304.0 %all-gather.9.cloned.1.call-start = ((), (), s32[]{:S(2)}) async-start(), calls=%async_computation.19 | async-start | bytes 3317760 | tf_op jit(solution)/shard_map/all_gather | solution.py:42
  8.7 560.1 %all-gather.5.cloned.1.call-start = ((), (), s32[]{:S(2)}) async-start(), calls=%async_computation.17 | async-start | bytes 24791040 | tf_op jit(solution)/shard_map/all_gather | solution.py:44
  36.2 709.2 %all-gather.11.cloned.1.call-start = ((), (), s32[]{:S(2)}) async-start(), calls=%async_computation.20 | async-start | bytes 12533760 | tf_op jit(solution)/shard_map/all_gather | solution.py:43
  83.6 101.8 %copy-start.92 = (f32[1152]{0:T(1024)}, f32[1152]{0:T(1024)S(1)}, u32[]{:S(2)}) copy-start(f32[1152]{0:T(1024)S(1)} %get-tuple-element.82) | copy-start | bytes 13828
  112.4 73.0 %copy-start.130 = (f32[2,184]{1,0:T(2,128)}, f32[2,184]{1,0:T(2,128)S(1)}, u32[]{:S(2)}) copy-start(f32[2,184]{1,0:T(2,128)S(1)} %broadcast_multiply_fusion.7) | copy-start | bytes 4420
  114.4 70.9 %copy-start.156 = (f32[2,184]{1,0:T(2,128)}, f32[2,184]{1,0:T(2,128)S(1)}, u32[]{:S(2)}) copy-start(f32[2,184]{1,0:T(2,128)S(1)} %add_rsqrt_fusion.3) | copy-start | bytes 4420
  133.3 629.5 %copy-start.71 = (f32[1152]{0:T(1024)}, f32[1152]{0:T(1024)S(1)}, u32[]{:S(2)}) copy-start(f32[1152]{0:T(1024)S(1)} %get-tuple-element.76) | copy-start | bytes 13828
  133.4 52.0 %copy-start.144 = (f32[3,1152]{1,0:T(4,128)}, f32[3,1152]{1,0:T(4,128)S(1)}, u32[]{:S(2)}) copy-start(f32[3,1152]{1,0:T(4,128)S(1)} %pad_maximum_fusion.3) | copy-start | bytes 41476
  206.3 45.0 %all-to-all-start = ((bf16[2,184,3,1152]{1,0,2,3:T(2,128)(2,1)}), bf16[2,184,3,1152]{1,0,2,3:T(2,128)(2,1)S(1)}, u32[]{:S(2)}, u32[]{:S(2)}) async-start(bf16[2,184,3,1152]{1,0,2,3:T(2,128)(2,1)} %copy.226), calls=%async_computation | async-start | bytes 7077888 | tf_op jit(solution)/shard_map/all_to_all | solution.py:120
  278.9 28.7 %all-to-all-start.1 = ((bf16[2,736,288]{2,0,1:T(2,128)(2,1)}), bf16[2,736,288]{2,0,1:T(2,128)(2,1)S(1)}, u32[]{:S(2)}, u32[]{:S(2)}) async-start(bf16[2,736,288]{2,0,1:T(2,128)(2,1)} %copy.229), calls=%async_computation.1 | async-start | bytes 2260992 | tf_op jit(solution)/shard_map/all_to_all | solution.py:122
  306.3 580.7 %copy-start.121 = (f32[4304]{0:T(1024)}, f32[4304]{0:T(1024)S(1)}, u32[]{:S(2)}) copy-start(f32[4304]{0:T(1024)S(1)} %add.486) | copy-start | bytes 51652
  315.9 437.3 %copy-start.16 = (f32[368,1152]{1,0:T(8,128)}, f32[368,1152]{1,0:T(8,128)S(1)}, u32[]{:S(2)}) copy-start(f32[368,1152]{1,0:T(8,128)S(1)} %get-tuple-element.153) | copy-start | bytes 5087236
  315.9 429.5 %copy-start.105 = (f32[368]{0:T(512)}, f32[368]{0:T(512)S(1)}, u32[]{:S(2)}) copy-start(f32[368]{0:T(512)S(1)} %broadcast_multiply_fusion.3) | copy-start | bytes 4420
  316.2 429.1 %copy-start.132 = (f32[368]{0:T(512)}, f32[368]{0:T(512)S(1)}, u32[]{:S(2)}) copy-start(f32[368]{0:T(512)S(1)} %add_rsqrt_fusion.2) | copy-start | bytes 4420
  316.2 429.1 %copy-start.74 = (f32[1152]{0:T(1024)S(1)}, f32[1152]{0:T(1024)}, u32[]{:S(2)}) copy-start(f32[1152]{0:T(1024)} %get-tuple-element.77) | copy-start | bytes 13828
  758.0 4.1 collective-permute-start
  762.4 326.1 %copy-start.5 = (bf16[2,184,1152]{2,1,0:T(8,128)(2,1)}, bf16[2,184,1152]{2,1,0:T(8,128)(2,1)S(1)}, u32[]{:S(2)}) copy-start(bf16[2,184,1152]{2,1,0:T(8,128)(2,1)S(1)} %get-tuple-element.115) | copy-start | bytes 2543620
  781.5 46.1 %all-to-all-start.2 = ((bf16[2,184,3,1152]{1,0,2,3:T(2,128)(2,1)}), bf16[2,184,3,1152]{1,0,2,3:T(2,128)(2,1)}, u32[]{:S(2)}, u32[]{:S(2)}) async-start(bf16[2,184,3,1152]{1,0,2,3:T(2,128)(2,1)} %copy.232), calls=%async_computation.2 | async-start | bytes 7077888 | tf_op jit(solution)/shard_map/all_to_all | solution.py:120
  787.0 211.1 %copy-start.77 = (pred[2,736]{1,0:T(4,128)(4,1)}, pred[2,736]{1,0:T(4,128)(4,1)S(1)}, u32[]{:S(2)}) copy-start(pred[2,736]{1,0:T(4,128)(4,1)S(1)} %get-tuple-element.140) | copy-start | bytes 4420
  843.2 140.6 %copy-start.10 = (bf16[2,736,1,288]{1,3,2,0:T(8,128)(2,1)}, bf16[2,736,1,288]{1,3,2,0:T(8,128)(2,1)S(1)}, u32[]{:S(2)}) copy-start(bf16[2,736,1,288]{1,3,2,0:T(8,128)(2,1)S(1)} %get-tuple-element.122) | copy-start | bytes 2543620
  886.6 145.1 %copy-start.1 = (f32[368,1152]{1,0:T(8,128)}, f32[368,1152]{1,0:T(8,128)S(1)}, u32[]{:S(2)}) copy-start(f32[368,1152]{1,0:T(8,128)S(1)} %get-tuple-element.157) | copy-start | bytes 5087236
  928.0 18.5 all-to-all-start.4
  932.8 155.7 %copy-start.119 = (f32[368]{0:T(512)}, f32[368]{0:T(512)S(1)}, u32[]{:S(2)}) copy-start(f32[368]{0:T(512)S(1)} %div.165) | copy-start | bytes 4420
  932.9 155.6 %copy-start.117 = (f32[368]{0:T(512)}, f32[368]{0:T(512)S(1)}, u32[]{:S(2)}) copy-start(f32[368]{0:T(512)S(1)} %add.442) | copy-start | bytes 4420
  932.9 155.6 %copy-start.128 = (f32[368]{0:T(512)}, f32[368]{0:T(512)S(1)}, u32[]{:S(2)}) copy-start(f32[368]{0:T(512)S(1)} %rsqrt.91) | copy-start | bytes 4420
  932.9 65.2 %copy-start.69 = (f32[1,8,736]{2,1,0:T(8,128)}, f32[1,8,736]{2,1,0:T(8,128)S(1)}, u32[]{:S(2)}) copy-start(f32[1,8,736]{2,1,0:T(8,128)S(1)} %log_add_fusion) | copy-start | bytes 70660
  1025.5 43.1 %all-to-all-start.5 = ((bf16[2,736,3,288]{3,0,2,1:T(2,128)(2,1)}), bf16[2,736,3,288]{3,0,2,1:T(2,128)(2,1)}, u32[]{:S(2)}, u32[]{:S(2)}) async-start(bf16[2,736,3,288]{3,0,2,1:T(2,128)(2,1)} %pad_maximum_fusion), calls=%async_computation.5 | async-start | bytes 6782976 | tf_op jit(solution)/shard_map/all_to_all | solution.py:183
  1043.5 51.9 %collective-permute-start.2 = (bf16[2,184,1152]{2,1,0:T(8,128)(2,1)}, bf16[2,184,1152]{2,1,0:T(8,128)(2,1)}, u32[]{:S(2)}, u32[]{:S(2)}) collective-permute-start(bf16[2,184,1152]{2,1,0:T(8,128)(2,1)} %bitcast.55), channel_id=1, source_target_pairs={{0,16},{1,17},{2,18},{3,19},{4,20},{5,21},{6,22},{7,23},{8,24},{9,... | collective-permute-start | bytes 2543624 | tf_op jit(solution)/shard_map/ppermute | solution.py:13
  1093.8 4.4 collective-permute-start.1
  1114.9 44.9 %all-to-all-start.6 = ((bf16[2,184,3,1152]{1,0,2,3:T(2,128)(2,1)}), bf16[2,184,3,1152]{1,0,2,3:T(2,128)(2,1)S(1)}, u32[]{:S(2)}, u32[]{:S(2)}) async-start(bf16[2,184,3,1152]{1,0,2,3:T(2,128)(2,1)} %copy.249), calls=%async_computation.6 | async-start | bytes 7077888 | tf_op jit(solution)/shard_map/all_to_all | solution.py:120
  1187.4 20.0 all-to-all-start.7
  1255.9 18.9 all-to-all-start.8
  1347.4 42.5 %all-to-all-start.9 = ((bf16[2,736,3,288]{3,0,2,1:T(2,128)(2,1)}), bf16[2,736,3,288]{3,0,2,1:T(2,128)(2,1)S(1)}, u32[]{:S(2)}, u32[]{:S(2)}) async-start(bf16[2,736,3,288]{3,0,2,1:T(2,128)(2,1)} %pad_maximum_fusion.1), calls=%async_computation.9 | async-start | bytes 6782976 | tf_op jit(solution)/shard_map/all_to_all | solution.py:183
  1411.9 5.5 collective-permute-start.3
  1453.3 20.6 all-to-all-start.10
  1457.6 703.6 %reduce-scatter.14.cloned.1.call-start = ((), (), s32[]{:S(2)}) async-start(), calls=%async_computation.22 | async-start | bytes 3317760 | tf_op jit(solution)/shard_map/reduce_scatter | solution.py:290
  1549.7 44.4 %all-to-all-start.11 = ((bf16[2,736,3,288]{3,0,2,1:T(2,128)(2,1)}), bf16[2,736,3,288]{3,0,2,1:T(2,128)(2,1)}, u32[]{:S(2)}, u32[]{:S(2)}) async-start(bf16[2,736,3,288]{3,0,2,1:T(2,128)(2,1)} %pad_maximum_fusion.2), calls=%async_computation.11 | async-start | bytes 6782976 | tf_op jit(solution)/shard_map/all_to_all | solution.py:183
  1554.6 606.7 %reduce-scatter.12.cloned.1.call-start = ((), (), s32[]{:S(2)}) async-start(), calls=%async_computation.21 | async-start | bytes 9953280 | tf_op jit(solution)/shard_map/reduce_scatter | solution.py:287
  1630.9 530.3 %reduce-scatter.16.cloned.1.call-start = ((), (), s32[]{:S(2)}) async-start(), calls=%async_computation.23 | async-start | bytes 12533760 | tf_op jit(solution)/shard_map/reduce_scatter | solution.py:293
  1680.1 516.8 %reduce-scatter.18.cloned.1.call-start = ((), (), s32[]{:S(2)}) async-start(), calls=%async_computation.24 | async-start | bytes 368640
  1780.2 323.5 %copy-start.113 = (f32[1152]{0:T(1024)S(1)}, f32[1152]{0:T(1024)}, u32[]{:S(2)}) copy-start(f32[1152]{0:T(1024)} %get-tuple-element.58) | copy-start | bytes 13828
  1780.2 324.1 %copy-start.165 = (f32[1152]{0:T(1024)S(1)}, f32[1152]{0:T(1024)}, u32[]{:S(2)}) copy-start(f32[1152]{0:T(1024)} %get-tuple-element.69) | copy-start | bytes 13828
  1780.2 326.6 %copy-start.114 = (f32[1152]{0:T(1024)S(1)}, f32[1152]{0:T(1024)}, u32[]{:S(2)}) copy-start(f32[1152]{0:T(1024)} %get-tuple-element.100) | copy-start | bytes 13828
  1780.2 328.4 %copy-start.112 = (f32[1152]{0:T(1024)S(1)}, f32[1152]{0:T(1024)}, u32[]{:S(2)}) copy-start(f32[1152]{0:T(1024)} %get-tuple-element.98) | copy-start | bytes 13828
  2102.4 6.9 collective-permute-start.4
  2154.6 43.2 %reduce-scatter.20.cloned.1.call-start = ((), (), s32[]{:S(2)}) async-start(), calls=%async_computation.25 | async-start | bytes 368640
  2159.1 200.9 %all-reduce.8.cloned.1.call-start = ((), (), s32[]{:S(2)}) async-start(), calls=%async_computation.26 | async-start | bytes 15298560 | tf_op jit(solution)/shard_map/psum | solution.py:313
  (175 other events, 1852.0 us)
Sparse Core Ops, SparseCore 0:
  9.6 164.2 all-gather.6
  175.4 53.5 all-gather.8
  231.2 337.5 all-gather.4
  570.2 175.1 all-gather.10
  1465.6 51.7 reduce-scatter.13
  1631.0 135.2 reduce-scatter.11
  1768.8 320.9 reduce-scatter.15
  2154.7 19.0 reduce-scatter.17
  2176.8 18.0 reduce-scatter.19
  2199.7 160.1 all-reduce.7
where the time goes:
time: 2410 us; the launch traced here: 2400 us
  waiting for transfers between devices  852 us (35%)
  matrix products  479 us (20%)
  blocking collectives  448 us (19%)
  local copies, waits for them, and re-layouts  394 us (16%)
  other arithmetic  152 us (6%)
  starting transfers between devices  57.4 us (2%)
    unnamed x3, blocking collectives  360 us
    all_gather x1, waiting for transfers between devices, gather_once(): lax.all_gather(local[3], 'dp', axis=1, tiled=True)  253 us
    all_gather x1, waiting for transfers between devices, gather_once(): lax.all_gather(local[2], 'dp', axis=1, tiled=True)  161 us
    dot_general x12, matrix products, left_matmul(): lax.dot_general(left, right, (((0,), (0,)), ((), ())), preferred_element_...  154 us
    psum x1, waiting for transfers between devices, on_device(): lax.psum(totals[3].astype(jnp.bfloat16), 'seq').astype(jnp.float32)  143 us
    all_to_all x3, waiting for transfers between devices, forward_layer(): lax.all_to_all(projected, 'seq', split_axis=3, concat_axis=1, tiled=True)  120 us
    unnamed x410, local copies, waits for them, and re-layouts  99.9 us
    dot_general x12, matrix products, right_matmul(): lax.dot_general(left, right, (((1,), (1,)), ((), ())), preferred_element_...  99.3 us
  transfers between devices with their start and end apart: 26, of which 16 were waited for; matrix products, arithmetic and copies ran while one was open for 37% of the time, Pallas kernels for 0%

commit v1 on v0

v1 whole, which is shorter than its diff:
```python
import jax
import jax.numpy as jnp
from jax import lax
from jax.experimental import pallas as pl
from jax.experimental.pallas import tpu as pltpu
from jax.sharding import PartitionSpec as P

HEAD_DIM = 72
SCALE = HEAD_DIM**-0.5
VMEM_LIMIT = 56 * 1024 * 1024
F32 = jnp.float32
BF16 = jnp.bfloat16
LIGHT = pl.CostEstimate(flops=1, bytes_accessed=1, transcendentals=0)


def round_up(value, step):
    return -(-value // step) * step


def pick(array, index, axis=0):
    return lax.dynamic_index_in_dim(array, index, axis, keepdims=False)


def swap_cores(value):
    swap = [(0, 1), (1, 0)]
    return jax.tree.map(lambda array: lax.ppermute(array, "section", swap), value)


def swap_seq(value, bit):
    count = lax.axis_size("seq")
    return lax.ppermute(value, "seq", [(index, index ^ bit) for index in range(count)])


def dot(left, right, left_axis, right_axis):
    return lax.dot_general(
        left, right, (((left_axis,), (right_axis,)), ((), ())), preferred_element_type=F32
    )


def params_of(limit=VMEM_LIMIT):
    return pltpu.CompilerParams(vmem_limit_bytes=limit)


def whole_vmem(count):
    return [pl.BlockSpec(memory_space=pltpu.VMEM)] * count


def half_runs(total, parts, half, width):
    size = total // parts
    runs = [[], []]
    for part in range(parts):
        runs[0].append((part * size, half, part * width))
        runs[1].append((part * size + half, size - half, part * width))
    return runs


def split_columns(weight, runs, width, core):
    rows = weight.shape[0]

    def kernel(core_ref, whole_ref, keep_ref, send_ref):
        def write(ref, pieces):
            if sum(size for _, size, _ in pieces) < width:
                ref[...] = jnp.zeros_like(ref)
            for start, size, place in pieces:
                ref[:, place : place + size] = whole_ref[:, start : start + size]

        @pl.when(core_ref[0] == 0)
        def _():
            write(keep_ref, runs[0])
            write(send_ref, runs[1])

        @pl.when(core_ref[0] == 1)
        def _():
            write(keep_ref, runs[1])
            write(send_ref, runs[0])

    shape = jax.ShapeDtypeStruct((rows, width), weight.dtype)
    return pl.pallas_call(
        kernel,
        out_shape=(shape, shape),
        in_specs=[pl.BlockSpec(memory_space=pltpu.SMEM)] + whole_vmem(1),
        out_specs=tuple(whole_vmem(2)),
        compiler_params=params_of(),
        cost_estimate=LIGHT,
        name="split_columns",
    )(core, weight)


def join_columns(mine, other, runs, total, place):
    count, rows, width = mine.shape

    def kernel(place_ref, mine_ref, other_ref, out_ref):
        def write(first, second):
            for ref, pieces in ((first, runs[0]), (second, runs[1])):
                for start, size, at in pieces:
                    out_ref[0, :, start : start + size] = ref[0, :, at : at + size].astype(F32)

        @pl.when(place_ref[0] == 0)
        def _():
            write(mine_ref, other_ref)

        @pl.when(place_ref[0] == 1)
        def _():
            write(other_ref, mine_ref)

    block = pl.BlockSpec((1, rows, width), lambda j, place: (j, 0, 0))
    out = pl.pallas_call(
        kernel,
        out_shape=jax.ShapeDtypeStruct((count, rows, total), F32),
        grid_spec=pltpu.PrefetchScalarGridSpec(
            num_scalar_prefetch=1,
            grid=(count,),
            in_specs=[block, block],
            out_specs=pl.BlockSpec((1, rows, total), lambda j, place: (j ^ place[1], 0, 0)),
        ),
        compiler_params=params_of(),
        cost_estimate=LIGHT,
        name="join_columns",
    )(place, mine, other)
    return out.reshape(count * rows, total)


def join_rows(mine, other, total, place):
    count, rows, width = mine.shape

    def kernel(place_ref, mine_ref, other_ref, out_ref):
        half = pl.program_id(0) // count

        @pl.when(half == place_ref[0])
        def _():
            out_ref[...] = mine_ref[0].astype(F32)

        @pl.when(half != place_ref[0])
        def _():
            out_ref[...] = other_ref[0].astype(F32)

    def quarter(step):
        return lax.rem(step, count)

    return pl.pallas_call(
        kernel,
        out_shape=jax.ShapeDtypeStruct((total, width), F32),
        grid_spec=pltpu.PrefetchScalarGridSpec(
            num_scalar_prefetch=1,
            grid=(2 * count,),
            in_specs=[
                pl.BlockSpec((1, rows, width), lambda t, place: (quarter(t), 0, 0)),
                pl.BlockSpec((1, rows, width), lambda t, place: (quarter(t), 0, 0)),
            ],
            out_specs=pl.BlockSpec(
                (rows, width),
                lambda t, place: (lax.div(t, count) * count + (quarter(t) ^ place[1]), 0),
            ),
        ),
        compiler_params=params_of(),
        cost_estimate=LIGHT,
        name="join_rows",
    )(place, mine, other)


def assemble(own, near, side, front, across):
    parts, rows, columns = near.shape
    count = parts + 1
    place = jnp.stack([lax.axis_index("dp"), lax.axis_index("seq")]).astype(jnp.int32)

    def kernel(place_ref, own_ref, near_ref, side_ref, front_ref, across_ref, out_ref, sem):
        along, here = place_ref[0], place_ref[1]
        copies = [pltpu.make_async_copy(own_ref, out_ref.at[along], sem.at[0])]
        for step in range(parts):
            there = lax.rem(along + step + 1, count)
            for bits, ref in enumerate((near_ref, side_ref, front_ref, across_ref)):
                copies.append(
                    pltpu.make_async_copy(
                        ref.at[step], out_ref.at[there, here ^ bits], sem.at[len(copies)]
                    )
                )
        for copy in copies:
            copy.start()
        for copy in copies:
            copy.wait()

    return pl.pallas_call(
        kernel,
        out_shape=jax.ShapeDtypeStruct((count, 4, rows, columns), own.dtype),
        in_specs=[pl.BlockSpec(memory_space=pltpu.SMEM)]
        + [pl.BlockSpec(memory_space=pl.ANY)] * 5,
        out_specs=pl.BlockSpec(memory_space=pltpu.VMEM),
        scratch_shapes=[pltpu.SemaphoreType.DMA((1 + 4 * parts,))],
        compiler_params=params_of(),
        cost_estimate=LIGHT,
        name="assemble",
    )(place, own, near, side, front, across)


def line_shifts(value):
    count = lax.axis_size("dp")
    return jnp.stack(
        [
            lax.ppermute(value, "dp", [((to + step) % count, to) for to in range(count)])
            for step in range(1, count)
        ]
    )


def line_gather(value):
    count = lax.axis_size("dp")
    line = lax.all_gather(value, "dp", axis=0)
    return lax.dynamic_slice_in_dim(
        jnp.concatenate([line, line], 0), lax.axis_index("dp") + 1, count - 1, 0
    )


def quarters_of(shard):
    return shard.reshape(4, shard.shape[0] // 4, shard.shape[1])


def spread(near):
    return swap_seq(near, 1), swap_seq(near, 2)


def spread_on(neighbours, by_side):
    side, front = neighbours
    return swap_seq(front, 1) if by_side else swap_seq(side, 2)


def bits_of_place():
    here = lax.axis_index("seq")
    return lax.rem(here, 2), lax.div(here, 2)


def grad_halves(left, right, count, by_side, start, end):
    length, depth = left.shape
    columns = end - start
    rows = depth // count
    quarter = round_up(rows, 32) // 4
    x, y = bits_of_place()
    bit = (x if by_side else y).astype(jnp.int32).reshape(1)

    def kernel(bit_ref, left_ref, right_ref, keep_ref, send_ref, turned):
        block = pl.program_id(0)

        @pl.when(block == 0)
        def _():
            turned[...] = left_ref[...].astype(F32).T.astype(BF16).reshape(turned.shape)

        grad = dot(turned[block], right_ref[:, start:end], 1, 0)
        if 4 * quarter > rows:
            empty = jnp.zeros((4 * quarter - rows, columns), F32)
            grad = jnp.concatenate([grad, empty], axis=0)
        parts = [grad[at * quarter : (at + 1) * quarter].astype(BF16) for at in range(4)]
        zeros, ones = ((0, 2), (1, 3)) if by_side else ((0, 1), (2, 3))

        def write(ref, which):
            for index, at in enumerate(which):
                ref[0, index] = parts[at]

        @pl.when(bit_ref[0] == 0)
        def _():
            write(keep_ref, zeros)
            write(send_ref, ones)

        @pl.when(bit_ref[0] == 1)
        def _():
            write(keep_ref, ones)
            write(send_ref, zeros)

    out = pl.BlockSpec((1, 2, quarter, columns), lambda z, bit: (z, 0, 0, 0))
    shape = jax.ShapeDtypeStruct((count, 2, quarter, columns), BF16)
    return pl.pallas_call(
        kernel,
        out_shape=(shape, shape),
        grid_spec=pltpu.PrefetchScalarGridSpec(
            num_scalar_prefetch=1,
            grid=(count,),
            in_specs=[
                pl.BlockSpec((length, depth), lambda z, bit: (0, 0)),
                pl.BlockSpec(right.shape, lambda z, bit: (0, 0)),
            ],
            out_specs=(out, out),
            scratch_shapes=[pltpu.VMEM((count, rows, length), BF16)],
        ),
        compiler_params=params_of(),
        cost_estimate=LIGHT,
        name="grad_halves",
    )(bit, left, right)


def add_half(held, moved, by_side):
    count, _, rows, columns = held.shape
    x, y = bits_of_place()
    bit = (y if by_side else x).astype(jnp.int32).reshape(1)

    def kernel(bit_ref, held_ref, moved_ref, keep_ref, send_ref):
        def total(index):
            return (held_ref[0, index].astype(F32) + moved_ref[0, index].astype(F32)).astype(BF16)

        keep_ref[0] = total(bit_ref[0])
        send_ref[0] = total(1 - bit_ref[0])

    both = pl.BlockSpec((1, 2, rows, columns), lambda z, bit: (z, 0, 0, 0))
    out = pl.BlockSpec((1, rows, columns), lambda z, bit: (z, 0, 0))
    shape = jax.ShapeDtypeStruct((count, rows, columns), BF16)
    return pl.pallas_call(
        kernel,
        out_shape=(shape, shape),
        grid_spec=pltpu.PrefetchScalarGridSpec(
            num_scalar_prefetch=1, grid=(count,), in_specs=[both, both], out_specs=(out, out)
        ),
        compiler_params=params_of(),
        cost_estimate=LIGHT,
        name="add_half",
    )(bit, held, moved)


def add_low(left, right):
    return (left.astype(F32) + right.astype(F32)).astype(BF16)


class Sum:
    def __init__(self, left, right, count, by_side, columns=None):
        self.by_side = by_side
        start, end = columns or (0, right.shape[1])
        self.keep, self.send = grad_halves(left, right, count, by_side, start, end)

    def first(self):
        self.moved = swap_seq(self.send, 1 if self.by_side else 2)

    def add(self):
        self.keep, self.send = add_half(self.keep, self.moved, self.by_side)

    def second(self):
        self.moved = swap_seq(self.send, 2 if self.by_side else 1)

    def over_line(self, gate):
        part = gate(add_low(self.keep, self.moved))
        self.line = lax.psum_scatter(part, "dp", scatter_dimension=0, tiled=True)[0]

    def over_line_shifts(self):
        line, count = lax.axis_index("dp"), lax.axis_size("dp")
        part = self.keep.astype(F32) + self.moved.astype(F32)
        total = pick(part, line)
        for step in range(1, count):
            moved = lax.ppermute(
                pick(part, lax.rem(line + step, count)).astype(BF16),
                "dp",
                [(source, (source + step) % count) for source in range(count)],
            )
            total = total + moved.astype(F32)
        self.line = total.astype(BF16)


def plain_grad(left, right):
    depth, columns = left.shape[1], right.shape[1]

    def kernel(left_ref, right_ref, out_ref):
        turned = left_ref[...].astype(F32).T.astype(BF16)
        for start, end in tiles(columns):
            out_ref[:, start:end] = dot(turned, right_ref[:, start:end], 1, 0).astype(BF16)

    return whole_call(kernel, "plain_grad", [((depth, columns), BF16)], left, right)[0]


class Order:
    def __init__(self, token):
        self.token = token

    def __call__(self, *values):
        values, self.token = lax.optimization_barrier((values, self.token))
        return values if len(values) > 1 else values[0]

    def sent(self, *sums):
        for each in sums:
            each.send = self(each.send)

    def summed(self, *sums):
        for each in sums:
            each.line = self(each.line)

    def arrived(self, *sums):
        for each in sums:
            each.moved = self(each.moved)


def in_order(pieces):
    here = lax.axis_index("seq")
    return jnp.stack([pick(pieces, here ^ index) for index in range(4)])


def attention_forward(qkv, hidden_keys):
    length, width = qkv.shape
    width //= 3
    heads = width // HEAD_DIM

    def kernel(qkv_ref, hidden_ref, out_ref, lse_ref, q_s, k_s, v_s, o_s):
        head = pl.program_id(0)

        @pl.when(head == 0)
        def _():
            for index in range(heads):
                at = index * HEAD_DIM
                q_s[index] = qkv_ref[:, at : at + HEAD_DIM]
                k_s[index] = qkv_ref[:, width + at : width + at + HEAD_DIM]
                v_s[index] = qkv_ref[:, 2 * width + at : 2 * width + at + HEAD_DIM]

        scores = dot(k_s[head], q_s[head], 1, 1) * SCALE
        scores = jnp.where(hidden_ref[...] > 0, -1e9, scores)
        top = jnp.max(scores, axis=0, keepdims=True)
        expon = jnp.exp(scores - top)
        total = jnp.sum(expon, axis=0, keepdims=True)
        lse_ref[0] = top + jnp.log(total)
        mixed = dot(v_s[head], expon.astype(BF16), 0, 0) / total
        o_s[head] = mixed.T.astype(BF16)

        @pl.when(head == heads - 1)
        def _():
            for index in range(heads):
                out_ref[:, index * HEAD_DIM : (index + 1) * HEAD_DIM] = o_s[index]

    slab = pltpu.VMEM((heads, length, HEAD_DIM), BF16)
    return pl.pallas_call(
        kernel,
        grid=(heads,),
        out_shape=(
            jax.ShapeDtypeStruct((length, width), BF16),
            jax.ShapeDtypeStruct((heads, 1, length), F32),
        ),
        in_specs=[
            pl.BlockSpec((length, 3 * width), lambda h: (0, 0)),
            pl.BlockSpec((length, 1), lambda h: (0, 0)),
        ],
        out_specs=(
            pl.BlockSpec((length, width), lambda h: (0, 0)),
            pl.BlockSpec((1, 1, length), lambda h: (h, 0, 0)),
        ),
        scratch_shapes=[slab, slab, slab, slab],
        compiler_params=params_of(),
        cost_estimate=LIGHT,
        name="attention_forward",
    )(qkv, hidden_keys)


def attention_backward(qkv, d_out, lse, hidden_keys):
    length, width = d_out.shape
    heads = width // HEAD_DIM

    def kernel(qkv_ref, do_ref, lse_ref, hidden_ref, out_ref, q_s, k_s, v_s, do_s, dq_s, dk_s, dv_s):
        head = pl.program_id(0)

        @pl.when(head == 0)
        def _():
            for index in range(heads):
                at = index * HEAD_DIM
                q_s[index] = qkv_ref[:, at : at + HEAD_DIM]
                k_s[index] = qkv_ref[:, width + at : width + at + HEAD_DIM]
                v_s[index] = qkv_ref[:, 2 * width + at : 2 * width + at + HEAD_DIM]
                do_s[index] = do_ref[:, at : at + HEAD_DIM]

        queries, keys, values, d_rows = q_s[head], k_s[head], v_s[head], do_s[head]
        scores = dot(keys, queries, 1, 1) * SCALE
        scores = jnp.where(hidden_ref[...] > 0, -1e9, scores)
        soft = jnp.exp(scores - lse_ref[0])
        d_soft = dot(values, d_rows, 1, 1)
        inner = jnp.sum(soft * d_soft, axis=0, keepdims=True)
        d_scores = (soft * (d_soft - inner)).astype(BF16)
        dv_s[head] = dot(soft.astype(BF16), d_rows, 1, 0).astype(BF16)
        dk_s[head] = (dot(d_scores, queries, 1, 0) * SCALE).astype(BF16)
        dq_s[head] = (dot(keys, d_scores, 0, 0) * SCALE).T.astype(BF16)

        @pl.when(head == heads - 1)
        def _():
            for index in range(heads):
                at = index * HEAD_DIM
                out_ref[:, at : at + HEAD_DIM] = dq_s[index]
                out_ref[:, width + at : width + at + HEAD_DIM] = dk_s[index]
                out_ref[:, 2 * width + at : 2 * width + at + HEAD_DIM] = dv_s[index]

    slab = pltpu.VMEM((heads, length, HEAD_DIM), BF16)
    return pl.pallas_call(
        kernel,
        grid=(heads,),
        out_shape=jax.ShapeDtypeStruct((length, 3 * width), BF16),
        in_specs=[
            pl.BlockSpec((length, 3 * width), lambda h: (0, 0)),
            pl.BlockSpec((length, width), lambda h: (0, 0)),
            pl.BlockSpec((1, 1, length), lambda h: (h, 0, 0)),
            pl.BlockSpec((length, 1), lambda h: (0, 0)),
        ],
        out_specs=pl.BlockSpec((length, 3 * width), lambda h: (0, 0)),
        scratch_shapes=[slab] * 7,
        compiler_params=params_of(),
        cost_estimate=LIGHT,
        name="attention_backward",
    )(qkv, d_out, lse, hidden_keys)


def norm_parts(stream):
    centre = jnp.mean(stream, axis=-1, keepdims=True)
    offset = stream - centre
    spread = jnp.mean(offset * offset, axis=-1, keepdims=True)
    inverse = lax.rsqrt(spread + 1e-06)
    return offset * inverse, inverse


def tiles(total, step=256):
    return [(at, min(at + step, total)) for at in range(0, total, step)]


def whole_call(kernel, name, out_shapes, *arrays):
    shapes = tuple(jax.ShapeDtypeStruct(shape, dtype) for shape, dtype in out_shapes)
    return pl.pallas_call(
        kernel,
        out_shape=shapes,
        in_specs=whole_vmem(len(arrays)),
        out_specs=tuple(whole_vmem(len(shapes))),
        compiler_params=params_of(),
        cost_estimate=LIGHT,
        name=name,
    )(*arrays)


PIECES = 3


def join_pieces(refs):
    return jnp.concatenate([ref[...] for ref in refs], axis=1).astype(F32)


def partial_product(left, weight, turned, name):
    length = left.shape[0]
    columns = weight.shape[0 if turned else 1]
    piece = columns // PIECES

    def kernel(left_ref, weight_ref, *out_refs):
        for start, end in tiles(columns):
            if turned:
                product = dot(left_ref[...], weight_ref[start:end, :], 1, 1)
            else:
                product = dot(left_ref[...], weight_ref[:, start:end], 1, 0)
            product = product.astype(BF16)
            for index, ref in enumerate(out_refs):
                low, high = max(start, index * piece), min(end, (index + 1) * piece)
                if low < high:
                    ref[:, low - index * piece : high - index * piece] = product[
                        :, low - start : high - start
                    ]

    return whole_call(kernel, name, [((length, piece), BF16)] * PIECES, left, weight)


def project_in(base, partials, vectors, weight, shift):
    length, width = base.shape
    columns = weight.shape[1]

    def kernel(*refs):
        if partials is None:
            base_ref, vectors_ref, weight_ref, shift_ref, normed_ref, qkv_ref = refs
            stream = base_ref[...].astype(F32)
        else:
            base_ref, *refs = refs
            own_refs, other_refs = refs[:PIECES], refs[PIECES : 2 * PIECES]
            bias_ref, vectors_ref, weight_ref, shift_ref = refs[2 * PIECES : 2 * PIECES + 4]
            normed_ref, qkv_ref, stream_ref = refs[2 * PIECES + 4 :]
            stream = base_ref[...] + join_pieces(own_refs) + join_pieces(other_refs)
            stream_ref[...] = (stream + bias_ref[...]).astype(BF16)
            stream = stream_ref[...].astype(F32)
        normed = norm_parts(stream)[0] * vectors_ref[0:1, :] + vectors_ref[2:3, :]
        normed_ref[...] = normed.astype(BF16)
        for start, end in tiles(columns):
            product = dot(normed_ref[...], weight_ref[:, start:end], 1, 0)
            qkv_ref[:, start:end] = (product + shift_ref[:, start:end]).astype(BF16)

    shapes = [((length, width), BF16), ((length, columns), BF16)]
    if partials is None:
        normed, qkv = whole_call(kernel, "project_in", shapes, base, vectors, weight, shift)
        return base, normed, qkv
    shapes.append(((length, width), BF16))
    normed, qkv, stream = whole_call(
        kernel,
        "project_in",
        shapes,
        base,
        *partials[0],
        *partials[1],
        partials[2],
        vectors,
        weight,
        shift,
    )
    return stream, normed, qkv


def expand_hidden(stream, own, other, vectors, weight, shift):
    length, width = stream.shape
    columns = weight.shape[1]
    root = 0.7978845608028654

    def kernel(stream_ref, *refs):
        own_refs, other_refs, refs = refs[:PIECES], refs[PIECES : 2 * PIECES], refs[2 * PIECES :]
        vectors_ref, weight_ref, shift_ref, mid_ref, normed_ref, hidden_ref, slope_ref = refs
        middle = stream_ref[...].astype(F32) + join_pieces(own_refs)
        middle = middle + join_pieces(other_refs) + vectors_ref[6:7, :]
        mid_ref[...] = middle
        normed = norm_parts(middle)[0] * vectors_ref[1:2, :] + vectors_ref[3:4, :]
        normed_ref[...] = normed.astype(BF16)
        for start, end in tiles(columns):
            inner = dot(normed_ref[...], weight_ref[:, start:end], 1, 0) + shift_ref[:, start:end]
            square = inner * inner
            half_tanh = 0.5 * jnp.tanh(root * (inner + 0.044715 * square * inner))
            hidden_ref[:, start:end] = (inner * (0.5 + half_tanh)).astype(BF16)
            bend = (0.5 - 2.0 * half_tanh * half_tanh) * (root + 3 * 0.044715 * root * square)
            slope_ref[:, start:end] = (0.5 + half_tanh + inner * bend).astype(BF16)

    return whole_call(
        kernel,
        "expand_hidden",
        [
            ((length, width), F32),
            ((length, width), BF16),
            ((length, columns), BF16),
            ((length, columns), BF16),
        ],
        stream, *own, *other, vectors, weight, shift,
    )


def back_hidden(d_result, weight, slope):
    length, columns = slope.shape

    def kernel(d_ref, weight_ref, slope_ref, out_ref, sums_ref):
        for start, end in tiles(columns):
            d_hidden = dot(d_ref[...], weight_ref[start:end, :], 1, 1)
            d_pre = (d_hidden * slope_ref[:, start:end].astype(F32)).astype(BF16)
            out_ref[:, start:end] = d_pre
            sums_ref[:, start:end] = jnp.sum(d_pre.astype(F32), axis=0, keepdims=True)

    return whole_call(
        kernel,
        "back_hidden",
        [((length, columns), BF16), ((1, columns), F32)],
        d_result, weight, slope,
    )


def back_norm(base, own, other, stream, gain, weight):
    length, width = base.shape

    def kernel(*refs):
        base_ref, *refs = refs
        own_refs, other_refs, refs = refs[:PIECES], refs[PIECES : 2 * PIECES], refs[2 * PIECES :]
        stream_ref, gain_ref, *refs = refs
        unit, inverse = norm_parts(stream_ref[...].astype(F32))
        d_normed = join_pieces(own_refs) + join_pieces(other_refs)
        d_unit = d_normed * gain_ref[...]
        mean_d = jnp.mean(d_unit, axis=-1, keepdims=True)
        mean_du = jnp.mean(d_unit * unit, axis=-1, keepdims=True)
        base_wide = base_ref[...].astype(F32)
        total = base_wide + inverse * (d_unit - mean_d - unit * mean_du)
        if weight is None:
            low_ref, sums_ref = refs
        else:
            weight_ref, low_ref, sums_ref, wide_ref, product_ref = refs
            wide_ref[...] = total
        low_ref[...] = total.astype(BF16)
        sums_ref[0:1, :] = jnp.sum(d_normed * unit, axis=0, keepdims=True)
        sums_ref[1:2, :] = jnp.sum(d_normed, axis=0, keepdims=True)
        sums_ref[2:3, :] = jnp.sum(low_ref[...].astype(F32), axis=0, keepdims=True)
        sums_ref[3:4, :] = jnp.sum(base_wide, axis=0, keepdims=True)
        if weight is not None:
            for start, end in tiles(weight.shape[0]):
                product = dot(low_ref[...], weight_ref[start:end, :], 1, 1)
                product_ref[:, start:end] = product.astype(BF16)

    shapes = [((length, width), BF16), ((4, width), F32)]
    arrays = [base, *own, *other, stream, gain]
    if weight is not None:
        arrays.append(weight)
        shapes += [((length, width), F32), ((length, weight.shape[0]), BF16)]
    return whole_call(kernel, "back_norm", shapes, *arrays)


def column_sums(array):
    return jnp.sum(array.astype(F32), axis=0)


def on_device(
    section_inputs,
    key_mask,
    attention_in,
    attention_out,
    expand_weight,
    contract_weight,
    norm_gains,
    biases,
    expand_bias,
):
    core = lax.axis_index("section")
    here = lax.axis_index("seq")
    line = lax.axis_index("dp")
    count = lax.axis_size("dp")
    first = core == 0
    core_ref = core.astype(jnp.int32).reshape(1)
    place_ref = jnp.stack([core, here]).astype(jnp.int32)

    width = attention_out.shape[2]
    own_rows = attention_out.shape[1]
    half_heads = own_rows // 2
    own_hidden = contract_weight.shape[1]
    half_hidden = round_up(round_up(own_hidden, 2) // 2, 16)
    in_runs = half_runs(3 * count * own_rows, 3 * count, half_heads, half_heads)
    hidden_runs = half_runs(count * own_hidden, count, half_hidden, half_hidden)
    in_width = 3 * count * half_heads
    hidden_width = count * half_hidden

    gate = Order(core)

    def both_layers(keep, send):
        received = swap_cores(send)
        return jnp.where(first, keep, received), jnp.where(first, received, keep)

    def pad_rows(array, step=32):
        extra = round_up(array.shape[-2], step) - array.shape[-2]
        if extra == 0:
            return array
        spec = [(0, 0)] * (array.ndim - 2) + [(0, extra), (0, 0)]
        return jnp.pad(array, spec)

    def prepared(halves):
        quarters = [quarters_of(pad_rows(half)) for half in halves]
        return quarters, [pick(quarter, here) for quarter in quarters]

    def built(own, near, others, rows):
        whole = assemble(own, near, *others)
        whole = whole.reshape(count, -1, whole.shape[3])[:, :rows]
        return whole.reshape(count * rows, whole.shape[2])

    in_own, in_mine = prepared(
        both_layers(*split_columns(attention_in[0], in_runs, in_width, core_ref))
    )
    in_mine, attention_out, expand_weight, contract_weight, norm_gains, biases, expand_bias = gate(
        in_mine, attention_out, expand_weight, contract_weight, norm_gains, biases, expand_bias
    )

    near_in_0 = line_shifts(in_mine[0])
    hidden_shift = jnp.pad(expand_bias[0], (0, 2 * half_hidden - own_hidden))
    packed = jnp.concatenate([norm_gains[0].reshape(-1), biases[0].reshape(-1), hidden_shift])
    packed = both_layers(packed, packed)
    packed_rows = round_up(packed[0].size, width) // width
    out_parts = attention_out[0].reshape(2, half_heads, width)
    out_halves = both_layers(pick(out_parts, core), pick(out_parts, 1 - core))
    out_whole = []
    for half, vector in zip(out_halves, packed):
        vector = jnp.pad(vector, (0, packed_rows * width - vector.size)).reshape(-1, width)
        out_whole.append(pad_rows(jnp.concatenate([half, vector], axis=0)))
    out_0 = lax.all_gather(out_whole[0], "dp", axis=0)
    expand_own, expand_mine = prepared(
        both_layers(*split_columns(expand_weight[0], hidden_runs, hidden_width, core_ref))
    )
    near_expand_0 = line_gather(expand_mine[0])
    near_in_0, expand_mine, out_whole, contract_weight, section_inputs = gate(
        near_in_0, expand_mine, out_whole, contract_weight, section_inputs
    )

    beside_in_0 = spread(near_in_0)
    contract_parts = jnp.pad(
        contract_weight[0], ((0, 2 * half_hidden - own_hidden), (0, 0))
    ).reshape(2, half_hidden, width)
    contract_own, contract_mine = prepared(
        both_layers(pick(contract_parts, core), pick(contract_parts, 1 - core))
    )
    near_contract_0 = line_gather(contract_mine[0])
    beside_in_0, out_0, near_expand_0, contract_mine, in_mine, section_inputs = gate(
        beside_in_0, out_0, near_expand_0, contract_mine, in_mine, section_inputs
    )

    across_in_0 = spread_on(beside_in_0, False)
    micro, images, block, _ = section_inputs.shape[1:]
    tokens = section_inputs[0].reshape(micro * images, block, width)
    pieces = [pick(tokens, here)]
    pieces += [swap_seq(pick(tokens, here ^ bits), bits) for bits in range(1, 4)]
    in_padded = jnp.pad(in_mine[1], ((0, 8), (0, 0)))
    near_in_1 = line_gather(in_padded)[:, : in_mine[1].shape[0]]
    mask = pick(key_mask.reshape(micro * images, 4, block), here)
    mask = jnp.concatenate([pick(mask, here ^ bits) for bits in range(4)])
    hidden_keys = jnp.where(mask > 0, 0.0, 1.0).astype(F32)[:, None]

    def small_of(gathered):
        packed = gathered[:, half_heads : half_heads + packed_rows].reshape(count, -1)
        packed = packed.astype(F32)
        vectors = packed[:, : 8 * own_rows].reshape(count, 8, own_rows)
        hidden = packed[:, 8 * own_rows :][:, : 2 * half_hidden].reshape(count, 2, half_hidden)
        heads_part = pick(vectors.reshape(count, 8, 2, half_heads), core, 2)
        vectors = vectors.transpose(1, 0, 2).reshape(8, width)
        query, value = heads_part[:, 4].reshape(-1), heads_part[:, 5].reshape(-1)
        qkv_shift = jnp.concatenate([query, jnp.zeros_like(query), value])
        hidden_shift = pick(hidden, core, 1).reshape(1, -1)
        return vectors, qkv_shift.reshape(1, -1), hidden_shift

    def heads_of(gathered):
        return gathered[:, :half_heads].reshape(count * half_heads, width)

    vectors_0, qkv_shift_0, hidden_shift_0 = small_of(out_0)
    attn_out_0 = heads_of(out_0)
    pieces, across_in_0, near_expand_0, out_whole, qkv_shift_0 = gate(
        pieces, across_in_0, near_expand_0, out_whole, qkv_shift_0
    )
    beside_expand_0 = spread(near_expand_0)
    image = jnp.concatenate(pieces, axis=0)
    other = swap_cores(image)
    start = jnp.where(first, image, other)
    cotangent = jnp.where(first, other, image)
    attn_in_0 = built(in_own[0], near_in_0, (*beside_in_0, across_in_0), own_rows)
    out_1 = lax.all_gather(out_whole[1], "dp", axis=0)
    beside_expand_0, near_contract_0, start, attn_in_0, hidden_keys, expand_mine = gate(
        beside_expand_0, near_contract_0, start, attn_in_0, hidden_keys, expand_mine
    )

    across_expand_0 = spread_on(beside_expand_0, True)
    beside_contract_0 = spread(near_contract_0)
    near_expand_1 = line_gather(expand_mine[1])
    stream_0, normed_0, qkv_0 = project_in(start, None, vectors_0, attn_in_0, qkv_shift_0)
    mixed_0, lse_0 = attention_forward(qkv_0, hidden_keys)
    own = partial_product(mixed_0, attn_out_0, False, "project_heads")
    across_expand_0, beside_contract_0, contract_mine, own = gate(
        across_expand_0, beside_contract_0, contract_mine, own
    )
    expand_0 = built(expand_own[0], near_expand_0, (*beside_expand_0, across_expand_0), own_rows)
    own, other, expand_0, near_in_1 = gate(own, swap_cores(own), expand_0, near_in_1)

    across_contract_0 = spread_on(beside_contract_0, False)
    beside_in_1 = spread(near_in_1)
    near_contract_1 = line_gather(contract_mine[1])
    middle_0, normed_mid_0, hidden_0, slope_0 = expand_hidden(
        stream_0, own, other, vectors_0, expand_0, hidden_shift_0
    )
    across_contract_0, beside_in_1, near_expand_1, hidden_0 = gate(
        across_contract_0, beside_in_1, near_expand_1, hidden_0
    )

    across_in_1 = spread_on(beside_in_1, True)
    beside_expand_1 = spread(near_expand_1)
    contract_0 = built(
        contract_own[0], near_contract_0, (*beside_contract_0, across_contract_0), half_hidden
    )
    own = partial_product(hidden_0, contract_0, False, "contract_hidden")
    vectors_1, qkv_shift_1, hidden_shift_1 = small_of(out_1)
    attn_out_1 = heads_of(out_1)
    own, across_in_1, beside_expand_1, qkv_shift_1, attn_out_1 = gate(
        own, across_in_1, beside_expand_1, qkv_shift_1, attn_out_1
    )
    attn_in_1 = built(in_own[1], near_in_1, (*beside_in_1, across_in_1), own_rows)
    own, other, attn_in_1, near_contract_1 = gate(own, swap_cores(own), attn_in_1, near_contract_1)

    across_expand_1 = spread_on(beside_expand_1, False)
    beside_contract_1 = spread(near_contract_1)
    partials = (own, other, vectors_0[7:8])
    stream_1, normed_1, qkv_1 = project_in(middle_0, partials, vectors_1, attn_in_1, qkv_shift_1)
    mixed_1, lse_1 = attention_forward(qkv_1, hidden_keys)
    own = partial_product(mixed_1, attn_out_1, False, "project_heads")
    across_expand_1, beside_contract_1, own = gate(across_expand_1, beside_contract_1, own)
    expand_1 = built(expand_own[1], near_expand_1, (*beside_expand_1, across_expand_1), own_rows)
    own, other, expand_1 = gate(own, swap_cores(own), expand_1)

    across_contract_1 = spread_on(beside_contract_1, True)
    middle_1, normed_mid_1, hidden_1, slope_1 = expand_hidden(
        stream_1, own, other, vectors_1, expand_1, hidden_shift_1
    )
    hidden_1, across_contract_1, cotangent = gate(hidden_1, across_contract_1, cotangent)
    contract_1 = built(
        contract_own[1], near_contract_1, (*beside_contract_1, across_contract_1), half_hidden
    )

    def rows_of(pieces, rows, total):
        mine, other = jnp.stack(pieces, axis=1)
        if 4 * mine.shape[1] == rows:
            return join_rows(mine, other, total, place_ref)
        halves = [jnp.where(first, mine, other), jnp.where(first, other, mine)]
        halves = [in_order(half).reshape(-1, width)[:rows] for half in halves]
        return jnp.concatenate(halves, axis=0).astype(F32)[:total]

    def columns_of(pieces, runs, total, place):
        mine, other = jnp.stack(pieces, axis=1)
        return join_columns(mine, other, runs, total, place)[:own_rows]

    contract_sum_1 = Sum(hidden_1, cotangent, count, True)
    gate.sent(contract_sum_1)
    contract_sum_1.first()
    own_out = partial_product(hidden_1, contract_1, False, "contract_hidden")
    d_pre_1, hidden_sums_1 = back_hidden(cotangent, contract_1, slope_1)
    d_pre_1 = gate(d_pre_1)
    expand_sum_1 = Sum(normed_mid_1, d_pre_1, count, False)
    gate.sent(expand_sum_1)
    expand_sum_1.first()
    own = partial_product(d_pre_1, expand_1, True, "back_expand")
    own, other, other_out = gate(own, swap_cores(own), swap_cores(own_out))
    own_out, other_out = jnp.concatenate(own_out, axis=1), jnp.concatenate(other_out, axis=1)
    output = middle_1 + own_out.astype(F32) + other_out.astype(F32) + vectors_1[7:8]
    output = output.astype(BF16)
    d_branch_1, mid_sums_1, d_middle_1, d_mixed_1 = back_norm(
        cotangent, own, other, middle_1, vectors_1[1:2], attn_out_1
    )
    d_branch_1, d_mixed_1 = gate(d_branch_1, d_mixed_1)
    out_grad_1 = gate(plain_grad(mixed_1, d_branch_1))
    out_line_1 = lax.psum_scatter(out_grad_1, "dp", scatter_dimension=0, tiled=True)
    gate.arrived(contract_sum_1)
    contract_sum_1.add()
    gate.sent(contract_sum_1)
    contract_sum_1.second()
    d_qkv_1 = attention_backward(qkv_1, gate(d_mixed_1), lse_1, hidden_keys)
    d_qkv_1 = gate(d_qkv_1)
    in_sum_1 = Sum(normed_1, d_qkv_1, count, False)
    gate.sent(in_sum_1)
    in_sum_1.first()
    gate.arrived(expand_sum_1)
    expand_sum_1.add()
    gate.sent(expand_sum_1)
    expand_sum_1.second()
    own = partial_product(gate(d_qkv_1), attn_in_1, True, "back_in")
    gate.arrived(contract_sum_1)
    own = gate(own)
    own, other, output = gate(own, swap_cores(own), output)
    d_result_0, in_sums_1 = back_norm(d_middle_1, own, other, stream_1, vectors_1[0:1], None)
    d_result_0 = gate(d_result_0)
    contract_sum_0 = Sum(hidden_0, d_result_0, count, True)
    gate.sent(contract_sum_0)
    contract_sum_0.first()
    contract_sum_1.over_line(gate)
    d_pre_0, hidden_sums_0 = back_hidden(gate(d_result_0), contract_0, slope_0)
    d_pre_0 = gate(d_pre_0)
    expand_sum_0 = Sum(normed_mid_0, d_pre_0, count, False)
    gate.sent(expand_sum_0)
    gate.arrived(expand_sum_1)
    expand_sum_0.first()
    expand_sum_1.over_line(gate)
    own = partial_product(gate(d_pre_0), expand_0, True, "back_expand")
    gate.arrived(in_sum_1)
    in_sum_1.add()
    gate.sent(in_sum_1)
    own = gate(own)
    own, other, out_line_1 = gate(own, swap_cores(own), out_line_1)
    in_sum_1.second()
    d_branch_0, mid_sums_0, d_middle_0, d_mixed_0 = back_norm(
        d_result_0, own, other, middle_0, vectors_0[1:2], attn_out_0
    )
    d_branch_0, d_mixed_0 = gate(d_branch_0, d_mixed_0)
    out_grad_0 = gate(plain_grad(mixed_0, d_branch_0))
    out_line_0 = lax.psum_scatter(out_grad_0, "dp", scatter_dimension=0, tiled=True)
    gate.summed(contract_sum_1)
    d_qkv_0 = gate(attention_backward(qkv_0, gate(d_mixed_0), lse_0, hidden_keys))
    gate.arrived(contract_sum_0)
    contract_sum_0.add()
    gate.sent(contract_sum_0)
    contract_sum_0.second()
    cut = round_up(in_width // 2, 128)
    in_sums_a = Sum(normed_0, gate(d_qkv_0), count, True, (0, cut))
    gate.sent(in_sums_a)
    gate.arrived(in_sum_1)
    in_sums_a.first()
    in_sum_1.over_line(gate)
    in_sums_b = Sum(normed_0, gate(d_qkv_0), count, False, (cut, in_width))
    gate.sent(in_sums_b)
    gate.arrived(expand_sum_0)
    in_sums_b.first()
    expand_sum_0.add()
    gate.sent(expand_sum_0)
    own = partial_product(gate(d_qkv_0), attn_in_0, True, "back_in")
    own = gate(own)
    gate.summed(expand_sum_1)
    gate.arrived(contract_sum_0)
    own, other = gate(own, swap_cores(own))
    expand_sum_0.second()
    contract_sum_0.over_line(gate)
    d_input_0, in_sums_0 = back_norm(d_middle_0, gate(own), other, stream_0, vectors_0[0:1], None)
    d_input_0 = gate(d_input_0)
    gate.arrived(in_sums_a, in_sums_b)
    in_sums_a.add()
    in_sums_b.add()
    gate.sent(in_sums_a, in_sums_b)
    in_sums_a.second()
    in_sums_b.second()
    gate.summed(in_sum_1)
    gate.arrived(expand_sum_0)
    expand_sum_0.over_line(gate)

    def own_layer(low, high):
        return jnp.stack([jnp.where(first, low, high), swap_cores(jnp.where(first, high, low))])

    out_line_0 = gate(out_line_0)
    out_near = gate(own_layer(out_line_0, out_line_1))
    gate.arrived(in_sums_a, in_sums_b)
    in_sums_a.over_line_shifts()
    in_sums_b.over_line_shifts()
    gate.summed(contract_sum_0)
    contract_near = gate(own_layer(contract_sum_0.line, contract_sum_1.line))
    contract_beside = gate(spread(contract_near))
    contract_across = spread_on(contract_beside, True)
    out_moved = swap_seq(out_near, 2)
    gate.summed(in_sums_a, in_sums_b)
    contract_across, out_moved = gate(contract_across, out_moved)
    out_near = add_low(out_near, out_moved)
    in_line_0 = jnp.concatenate([in_sums_a.line, in_sums_b.line], axis=1)
    in_near = gate(own_layer(in_line_0, in_sum_1.line))
    in_beside = spread(in_near)
    grad_contract = rows_of(
        [contract_near, *contract_beside, contract_across], half_hidden, own_hidden
    )
    gate.summed(expand_sum_0)
    expand_near = gate(own_layer(expand_sum_0.line, expand_sum_1.line))
    in_beside, grad_contract = gate(in_beside, grad_contract)
    in_across = spread_on(in_beside, True)
    expand_beside = spread(expand_near)
    in_across, expand_beside = gate(in_across, expand_beside)
    expand_across = spread_on(expand_beside, False)
    out_moved = swap_seq(out_near, 1)
    last_place = jnp.stack([gate.token, here]).astype(jnp.int32)
    grad_in = columns_of([in_near, *in_beside, in_across], in_runs, 3 * width, last_place)
    expand_across, out_moved, grad_in = gate(expand_across, out_moved, grad_in)
    out_near = add_low(out_near, out_moved).astype(F32)
    grad_out = jnp.concatenate(
        [jnp.where(first, out_near[0], out_near[1]), jnp.where(first, out_near[1], out_near[0])]
    )
    last_place = jnp.stack([gate.token, here]).astype(jnp.int32)
    grad_expand = columns_of(
        [expand_near, *expand_beside, expand_across],
        hidden_runs,
        count * own_hidden,
        last_place,
    )

    def small_sums(in_sums, mid_sums, hidden_sums, d_qkv):
        heads = column_sums(d_qkv).reshape(3, -1)
        shared = jnp.stack(
            [in_sums[0], mid_sums[0], in_sums[1], mid_sums[1], mid_sums[2], mid_sums[3]]
        )
        return shared, heads[0], heads[2], hidden_sums[0]

    small_0 = small_sums(in_sums_0, mid_sums_0, hidden_sums_0, d_qkv_0)
    small_1 = small_sums(in_sums_1, mid_sums_1, hidden_sums_1, d_qkv_1)

    def pack_small(small):
        shared, query, value, hidden = small
        shared = jnp.where(first, shared, 0.0)
        none = jnp.zeros((count, half_heads), F32)

        def spread(vector, size):
            vector = vector.reshape(count, size)
            nothing = jnp.zeros_like(vector)
            return jnp.concatenate(
                [jnp.where(first, vector, nothing), jnp.where(first, nothing, vector)], axis=1
            )

        shared = shared.reshape(6, count, own_rows)
        return jnp.concatenate(
            [
                shared[0],
                shared[1],
                shared[2],
                shared[3],
                spread(query, half_heads),
                spread(value, half_heads),
                shared[4],
                shared[5],
                spread(hidden, half_hidden),
            ],
            axis=1,
        )

    low_sums, high_sums = pack_small(small_0), pack_small(small_1)
    sums = jnp.where(first, low_sums, high_sums)
    sums = sums + swap_cores(jnp.where(first, high_sums, low_sums))
    sums = sums + swap_seq(sums, 1)
    sums = sums + swap_seq(sums, 2)
    total = pick(sums, line)
    for step in range(1, count):
        total = total + lax.ppermute(
            pick(sums, lax.rem(line + step, count)),
            "dp",
            [(source, (source + step) % count) for source in range(count)],
        )
    sums = total

    result = jnp.where(first, d_input_0, output).reshape(4, block, width)
    returned = jnp.stack([result[0]] + [swap_seq(result[bits], bits) for bits in range(1, 4)])
    results = in_order(returned).astype(F32).reshape(1, micro, images, block, width)

    return (
        results,
        grad_in[None],
        grad_out[None],
        grad_expand[None],
        grad_contract[None],
        sums[: 2 * own_rows].reshape(1, 2, own_rows),
        sums[2 * own_rows : 8 * own_rows].reshape(1, 6, own_rows),
        sums[8 * own_rows : 8 * own_rows + own_hidden][None],
    )


def plain_passed_along(value, axis, steps):
    count = lax.axis_size(axis)
    initial, last = (max(0, -steps), min(count, count - steps))
    return lax.ppermute(value, axis, [(source, source + steps) for source in range(initial, last)])


def plain_layer_norm(stream, gain, shift):
    centre = jnp.mean(stream, axis=-1, keepdims=True)
    offset = stream - centre
    spread = jnp.mean(offset * offset, axis=-1, keepdims=True)
    return offset * lax.rsqrt(spread + 1e-06) * gain + shift


def plain_matmul(left, right):
    return jnp.dot(left, right, preferred_element_type=F32)


def plain_left_matmul(left, right):
    return lax.dot_general(
        left, right, (((0,), (0,)), ((), ())), preferred_element_type=F32
    )


def plain_right_matmul(left, right):
    return lax.dot_general(
        left, right, (((1,), (1,)), ((), ())), preferred_element_type=F32
    )


def plain_gather_once(local):
    whole = (
        lax.all_gather(local[0], "dp", axis=1, tiled=True),
        lax.all_gather(local[1], "dp", axis=1, tiled=True),
        lax.all_gather(local[2], "dp", axis=1, tiled=True),
        lax.all_gather(local[3], "dp", axis=1, tiled=True),
        lax.all_gather(local[4], "dp", axis=2, tiled=True),
        lax.all_gather(local[5], "dp", axis=2, tiled=True),
        lax.all_gather(local[6], "dp", axis=1, tiled=True),
    )
    return tuple((piece[0] for piece in whole))


def plain_split_heads(heads):
    images, length, _, width = heads.shape
    count = width // HEAD_DIM
    queries = heads[:, :, 0].reshape(images, length, count, HEAD_DIM)
    key_rows = heads[:, :, 1].reshape(images, length, count, HEAD_DIM)
    value_rows = heads[:, :, 2].reshape(images, length, count, HEAD_DIM)
    return (queries, key_rows, value_rows)


def plain_head_scores(queries, key_rows, visible):
    scores = jnp.einsum(
        "nqhd,nkhd->nhqk", queries, key_rows, preferred_element_type=F32
    ) * HEAD_DIM ** (-0.5)
    return jnp.where(visible[:, None, None, :], scores, -1000000000.0)


def plain_attend(heads, visible):
    images, length, _, width = heads.shape
    queries, key_rows, value_rows = plain_split_heads(heads)
    scores = plain_head_scores(queries, key_rows, visible)
    row_max = jnp.max(scores, axis=-1, keepdims=True)
    expon = jnp.exp(scores - row_max)
    total = jnp.sum(expon, axis=-1, keepdims=True)
    softmaxed = (expon / total).astype(BF16)
    log_total = (row_max + jnp.log(total))[..., 0]
    mixture = jnp.einsum(
        "nhqk,nkhd->nqhd", softmaxed, value_rows, preferred_element_type=F32
    )
    return (mixture.astype(BF16).reshape(images, length, width), log_total)


def plain_attend_back(heads, log_total, visible, d_mixture):
    images, length, _, width = heads.shape
    queries, key_rows, value_rows = plain_split_heads(heads)
    d_rows = d_mixture.reshape(queries.shape)
    scores = plain_head_scores(queries, key_rows, visible)
    softmaxed = jnp.exp(scores - log_total[..., None])
    d_soft = jnp.einsum("nqhd,nkhd->nhqk", d_rows, value_rows, preferred_element_type=F32)
    inner = jnp.sum(softmaxed * d_soft, axis=-1, keepdims=True)
    d_scores = (softmaxed * (d_soft - inner)).astype(BF16)
    scale = HEAD_DIM ** (-0.5)
    d_queries = (
        jnp.einsum("nhqk,nkhd->nqhd", d_scores, key_rows, preferred_element_type=F32)
        * scale
    ).astype(BF16)
    d_keys = (
        jnp.einsum("nhqk,nqhd->nkhd", d_scores, queries, preferred_element_type=F32) * scale
    ).astype(BF16)
    d_values = jnp.einsum(
        "nhqk,nqhd->nkhd",
        softmaxed.astype(BF16),
        d_rows,
        preferred_element_type=F32,
    ).astype(BF16)
    return jnp.stack([d_queries, d_keys, d_values], axis=2).reshape(images, length, 3, width)


def plain_forward_layer(stream_in, visible, params):
    attn_in, attn_out, expand, contract, gains, shifts, expand_shift = params
    images, rows_seq, width = stream_in.shape
    stream = stream_in.astype(F32).reshape(-1, width)
    gains32 = gains.astype(F32)
    shifts32 = shifts.astype(F32)
    normed = plain_layer_norm(stream, gains32[0], shifts32[0]).astype(BF16)
    qkv_shift = jnp.stack([shifts32[2], jnp.zeros_like(shifts32[2]), shifts32[3]])
    projected = (plain_matmul(normed, attn_in).reshape(images, rows_seq, 3, width) + qkv_shift).astype(
        BF16
    )
    heads = lax.all_to_all(projected, "seq", split_axis=3, concat_axis=1, tiled=True)
    mixture, log_total = plain_attend(heads, visible)
    mixed_rows = lax.all_to_all(mixture, "seq", split_axis=1, concat_axis=2, tiled=True).reshape(
        -1, width
    )
    middle = stream + plain_matmul(mixed_rows, attn_out) + shifts32[4]
    normed_mid = plain_layer_norm(middle, gains32[1], shifts32[1]).astype(BF16)
    hidden_pre = plain_matmul(normed_mid, expand) + expand_shift.astype(F32)
    hidden = jax.nn.gelu(hidden_pre, approximate=True).astype(BF16)
    result = middle + plain_matmul(hidden, contract) + shifts32[5]
    saved = (
        stream_in,
        normed,
        heads,
        log_total,
        mixed_rows,
        middle,
        normed_mid,
        hidden_pre,
        hidden,
        visible,
    )
    return (result.reshape(images, rows_seq, width), saved)


def plain_backward_layer(d_result, saved, params):
    attn_in, attn_out, expand, contract, gains, shifts, expand_shift = params
    (
        stream_in,
        normed,
        heads,
        log_total,
        mixed_rows,
        middle,
        normed_mid,
        hidden_pre,
        hidden,
        visible,
    ) = saved
    images, rows_seq, width = d_result.shape
    gains32 = gains.astype(F32)
    shifts32 = shifts.astype(F32)
    d_flat = d_result.reshape(-1, width)
    d_wide = d_flat.astype(F32)
    grad_contract = plain_left_matmul(hidden, d_flat)
    grad_last_bias = jnp.sum(d_wide, axis=0)
    d_hidden = plain_right_matmul(d_flat, contract)
    _, gelu_back = jax.vjp(lambda inner: jax.nn.gelu(inner, approximate=True), hidden_pre)
    d_pre = gelu_back(d_hidden)[0].astype(BF16)
    grad_expand = plain_left_matmul(normed_mid, d_pre)
    grad_expand_bias = jnp.sum(d_pre.astype(F32), axis=0)
    d_normed_mid = plain_right_matmul(d_pre, expand)
    _, norm_back_mid = jax.vjp(plain_layer_norm, middle, gains32[1], shifts32[1])
    d_middle_part, grad_gain_mid, grad_shift_mid = norm_back_mid(d_normed_mid)
    d_middle = d_wide + d_middle_part
    d_branch = d_middle.astype(BF16)
    grad_out_bias = jnp.sum(d_branch.astype(F32), axis=0)
    grad_attn_out = plain_left_matmul(mixed_rows, d_branch)
    d_mixture = (
        plain_right_matmul(d_branch, attn_out).astype(BF16).reshape(images, rows_seq, width)
    )
    d_heads = lax.all_to_all(d_mixture, "seq", split_axis=2, concat_axis=1, tiled=True)
    d_projected_heads = plain_attend_back(heads, log_total, visible, d_heads)
    d_projected = lax.all_to_all(
        d_projected_heads, "seq", split_axis=1, concat_axis=3, tiled=True
    ).reshape(-1, 3 * width)
    grad_attn_in = plain_left_matmul(normed, d_projected)
    column_sums = jnp.sum(d_projected.astype(F32), axis=0).reshape(3, width)
    d_normed = plain_right_matmul(d_projected, attn_in)
    stream = stream_in.astype(F32).reshape(-1, width)
    _, norm_back_in = jax.vjp(plain_layer_norm, stream, gains32[0], shifts32[0])
    d_stream_part, grad_gain_in, grad_shift_in = norm_back_in(d_normed)
    d_stream = d_middle + d_stream_part
    grad_gains = jnp.stack([grad_gain_in, grad_gain_mid])
    grad_shifts = jnp.stack(
        [
            grad_shift_in,
            grad_shift_mid,
            column_sums[0],
            column_sums[2],
            grad_out_bias,
            grad_last_bias,
        ]
    )
    grads = (
        grad_attn_in,
        grad_attn_out,
        grad_expand,
        grad_contract,
        grad_gains,
        grad_shifts,
        grad_expand_bias,
    )
    return (d_stream.reshape(images, rows_seq, width), grads)


def plain_send_forward(values):
    return plain_passed_along(values, "section", 1)


def plain_send_backward(values):
    return plain_passed_along(values, "section", -1)


def on_device_any(
    section_inputs,
    key_mask,
    attention_in,
    attention_out,
    expand_weight,
    contract_weight,
    norm_gains,
    biases,
    expand_bias,
):
    micro = section_inputs.shape[1]
    leading = lax.axis_index("section") == 0
    local = (
        attention_in,
        attention_out,
        expand_weight,
        contract_weight,
        norm_gains,
        biases,
        expand_bias,
    )
    sources = section_inputs[0]
    visible_all = key_mask > 0
    blank = jnp.zeros_like(sources[0])
    recv_forward = blank
    recv_backward = blank
    saves = {}
    outputs = [None] * micro
    input_grads = [None] * micro
    totals = None
    params = plain_gather_once(local)
    for tick in range(micro + 2):
        if tick <= micro:
            source = sources[tick] if tick < micro else blank
            stream_now = jnp.where(leading, source, recv_forward)
            visible_now = jnp.where(
                leading, visible_all[min(tick, micro - 1)], visible_all[max(tick - 1, 0)]
            )
            result, saved = plain_forward_layer(stream_now, visible_now, params)
            saves[tick] = saved
            if tick >= 1:
                outputs[tick - 1] = result
            sent_forward = plain_send_forward(result.astype(BF16))
        if tick >= 1:
            early = saves[tick - 2] if tick - 2 in saves else saves[tick]
            later = saves[tick] if tick in saves else saves[tick - 2]
            chosen = jax.tree.map(
                lambda left_one, right_one: jnp.where(leading, left_one, right_one), early, later
            )
            cotangent = sources[tick - 1] if tick <= micro else blank
            d_result = jnp.where(leading, recv_backward, cotangent)
            d_stream, grads = plain_backward_layer(d_result, chosen, params)
            active = jnp.where(leading, tick >= 2, tick <= micro)
            grads = tuple((jnp.where(active, piece, 0.0) for piece in grads))
            if tick >= 2:
                input_grads[tick - 2] = d_stream
            totals = (
                grads if totals is None else tuple((old + new for old, new in zip(totals, grads)))
            )
            recv_backward = plain_send_backward(d_stream.astype(BF16))
        if tick <= micro:
            recv_forward = sent_forward
    totals = (
        lax.psum_scatter(
            totals[0].astype(BF16), "dp", scatter_dimension=0, tiled=True
        ).astype(F32),
        lax.psum_scatter(
            totals[1].astype(BF16), "dp", scatter_dimension=0, tiled=True
        ).astype(F32),
        lax.psum_scatter(
            totals[2].astype(BF16), "dp", scatter_dimension=0, tiled=True
        ).astype(F32),
        lax.psum_scatter(
            totals[3].astype(BF16), "dp", scatter_dimension=0, tiled=True
        ).astype(F32),
        lax.psum_scatter(
            totals[4].astype(BF16), "dp", scatter_dimension=1, tiled=True
        ).astype(F32),
        lax.psum_scatter(
            totals[5].astype(BF16), "dp", scatter_dimension=1, tiled=True
        ).astype(F32),
        lax.psum_scatter(
            totals[6].astype(BF16), "dp", scatter_dimension=0, tiled=True
        ).astype(F32),
    )
    totals = (
        lax.psum(totals[0].astype(BF16), "seq").astype(F32),
        lax.psum(totals[1].astype(BF16), "seq").astype(F32),
        lax.psum(totals[2].astype(BF16), "seq").astype(F32),
        lax.psum(totals[3].astype(BF16), "seq").astype(F32),
        lax.psum(totals[4].astype(BF16), "seq").astype(F32),
        lax.psum(totals[5].astype(BF16), "seq").astype(F32),
        lax.psum(totals[6].astype(BF16), "seq").astype(F32),
    )
    results = jnp.stack(
        [jnp.where(leading, input_grads[index], outputs[index]) for index in range(micro)]
    )[None]
    return (
        results,
        totals[0][None],
        totals[1][None],
        totals[2][None],
        totals[3][None],
        totals[4][None],
        totals[5][None],
        totals[6][None],
    )


def solution(mesh):
    in_specs = (
        P("section", None, "dp", "seq", None),
        P(None, "dp", None),
        P("section", "dp", None),
        P("section", "dp", None),
        P("section", "dp", None),
        P("section", "dp", None),
        P("section", None, "dp"),
        P("section", None, "dp"),
        P("section", "dp"),
    )
    out_specs = (
        P("section", None, "dp", "seq", None),
        P("section", "dp", None),
        P("section", "dp", None),
        P("section", "dp", None),
        P("section", "dp", None),
        P("section", None, "dp"),
        P("section", None, "dp"),
        P("section", "dp"),
    )

    def by_size(section_inputs, *others):
        _, micro, images, _, _ = section_inputs.shape
        one_image_each = micro * images == lax.axis_size("seq") == 4
        plan = on_device if one_image_each else on_device_any
        return plan(section_inputs, *others)

    return jax.shard_map(
        by_size, mesh=mesh, in_specs=in_specs, out_specs=out_specs, check_vma=False
    )
```

time: 2410 us -> 916 us (0.38)
  waiting for transfers between devices: 852 us -> 274 us
  matrix products: 479 us -> 0 us
  blocking collectives: 448 us -> 0 us
  Pallas kernels: 0 us -> 404 us
  local copies, waits for them, and re-layouts: 394 us -> 67.8 us
  other arithmetic: 152 us -> 58.3 us
  starting transfers between devices: 57.4 us -> 87 us
    dot_general x55 -> x0, matrix products: 479 us -> none  [the longest x12 154 us: left_matmul(): lax.dot_general(left, right, (((0,), (0,)), ((), ())), preferred_element_...]
    all_gather x4 -> x7, waiting for transfers between devices: 454 us -> 41.1 us  [the longest x1 32.3 us: on_device(): out_0 = lax.all_gather(out_whole[0], 'dp', axis=0)]
    pallas_call x0 -> x49, Pallas kernels: none -> 404 us  [the longest x20 172 us: whole_call(): pl.pallas_call(kernel, out_shape=shapes, in_specs=whole_vmem(len(arrays))...]
    unnamed x3 -> x0, blocking collectives: 360 us -> none
    all_to_all x11 -> x0, waiting for transfers between devices: 249 us -> none  [the longest x3 120 us: forward_layer(): lax.all_to_all(projected, 'seq', split_axis=3, concat_axis=1, tiled=True)]
    ppermute x4 -> x98, waiting for transfers between devices: 4 us -> 232 us  [the longest x51 190 us: swap_seq(): lax.ppermute(value, 'seq', [(index, index ^ bit) for index in range(count)])]
    psum x1 -> x0, waiting for transfers between devices: 143 us -> none  [on_device(): lax.psum(totals[3].astype(jnp.bfloat16), 'seq').astype(jnp.float32)]
    all_to_all x18 -> x0, local copies, waits for them, and re-layouts: 96 us -> none  [the longest x6 49.3 us: backward_layer(): lax.all_to_all(d_projected_heads, 'seq', split_axis=1, concat_axis=3, til...]
  transfers between devices with their start and end apart: 26 -> 112, of which waited for: 16 -> 38; matrix products, arithmetic and copies ran while one was open for 37% -> 12% of each run, Pallas kernels for 0% -> 42%
where the time goes in v1:
time: 916 us; the launch traced here: 907 us
  Pallas kernels  404 us (44%)
  waiting for transfers between devices  274 us (30%)
  starting transfers between devices  87 us (9%)
  local copies, waits for them, and re-layouts  67.8 us (7%)
  other arithmetic  58.3 us (6%)
  between operations  15.5 us (2%)
    ppermute x51, waiting for transfers between devices, swap_seq(): lax.ppermute(value, 'seq', [(index, index ^ bit) for index in range(count)])  190 us
    pallas_call x20, Pallas kernels, whole_call(): pl.pallas_call(kernel, out_shape=shapes, in_specs=whole_vmem(len(arrays))...  172 us
    pallas_call x7, Pallas kernels, grad_halves(): pl.pallas_call(kernel, out_shape=(shape, shape), grid_spec=pltpu.Prefetch...  61.7 us
    ppermute x51, starting transfers between devices, swap_seq(): lax.ppermute(value, 'seq', [(index, index ^ bit) for index in range(count)])  60.1 us
    pallas_call x2, Pallas kernels, attention_backward(): pl.pallas_call(kernel, grid=(heads,), out_shape=jax.ShapeDtypeStruct((len...  49.4 us
    all_gather x1, waiting for transfers between devices, on_device(): out_0 = lax.all_gather(out_whole[0], 'dp', axis=0)  32.3 us
    pallas_call x2, Pallas kernels, attention_forward(): pl.pallas_call(kernel, grid=(heads,), out_shape=(jax.ShapeDtypeStruct((le...  32.3 us
    pallas_call x6, Pallas kernels, assemble(): pl.pallas_call(kernel, out_shape=jax.ShapeDtypeStruct((count, 4, rows, co...  31.8 us
  transfers between devices with their start and end apart: 112, of which 38 were waited for; matrix products, arithmetic and copies ran while one was open for 12% of the time, Pallas kernels for 42%

profile of v1, /device:TPU:0, one launch (start us, length us, event | category | flops | bytes accessed | tf_op | source)
XLA Modules:
  0.0 906.6 jit_solution(7981773313512897373)
XLA Ops:
  33.7 12.1 %collective-permute-done.2 = bf16[72,1728]{1,0:T(8,128)(2,1)} collective-permute-done((bf16[72,1728]{1,0:T(8,128)(2,1)}, bf16[72,1728]{1,0:T(8,128)(2,1)}, u32[]{:S(2)}, u32[]{:S(2)}) %collective-permute-start.2) | collective-permute-done | bytes 248864 | tf_op jit(solution)/shard_map/ppermute | solution.py:199
  61.5 8.7 all-gather.13.cloned.1.call-done
  75.1 32.3 %all-gather.17.cloned.1.call-done = bf16[640,1152]{1,0:T(8,128)(2,1)} async-done(((bf16[160,1152]{1,0:T(8,128)(2,1)}), bf16[640,1152]{1,0:T(8,128)(2,1)}) %all-gather.17.cloned.1.call-update) | async-done | bytes 1474576 | tf_op jit(solution)/shard_map/all_gather | solution.py:754
  125.3 18.9 %collective-permute-done.11 = bf16[184,1152]{1,0:T(8,128)(2,1)} collective-permute-done((bf16[184,1152]{1,0:T(8,128)(2,1)}, bf16[184,1152]{1,0:T(8,128)(2,1)}, u32[]{:S(2)}, u32[]{:S(2)}) %collective-permute-start.11) | collective-permute-done | bytes 423968 | tf_op jit(solution)/shard_map/ppermute | solution.py:31
  165.9 9.4 %collective-permute-done.15.front_ref = bf16[3,72,2176]{2,1,0:T(8,128)(2,1)} collective-permute-done((bf16[3,72,2176]{2,1,0:T(8,128)(2,1)S(1)}, bf16[3,72,2176]{2,1,0:T(8,128)(2,1)}, u32[]{:S(2)}, u32[]{:S(2)}) %collective-permute-start.15) | collective-permute-done | bytes 940064 | tf_op jit(solution)/shard_map/ppermute | solution.py:31
  182.0 8.6 project_in.2
  190.6 16.1 %attention_forward.2 = (bf16[736,576]{1,0:T(8,128)(2,1)}, f32[8,1,736]{2,1,0:T(1,128)}) custom-call(bf16[736,1728]{1,0:T(8,128)(2,1)} %get-tuple-element.430.qkv_ref, f32[736,1]{1,0:T(8,128)} %broadcast_select_fusion.11.hidden_ref), custom_call_target="tpu_custom_call" | custom-call | flops 1 | bytes 1 | tf_op jit(solution)/shard_map/attention_forward/pallas_call | solution.py:420
  210.7 9.3 %collective-permute-done.18.side_ref = bf16[3,136,1152]{2,1,0:T(8,128)(2,1)} collective-permute-done((bf16[3,136,1152]{2,1,0:T(8,128)(2,1)S(1)}, bf16[3,136,1152]{2,1,0:T(8,128)(2,1)}, u32[]{:S(2)}, u32[]{:S(2)}) %collective-permute-start.18) | collective-permute-done | bytes 940064 | tf_op jit(solution)/shard_map/ppermute | solution.py:31
  222.6 5.6 assemble.7
  232.4 14.5 %expand_hidden.2 = (f32[736,1152]{1,0:T(8,128)}, bf16[736,1152]{1,0:T(8,128)(2,1)}, bf16[736,2176]{1,0:T(8,128)(2,1)}, bf16[736,2176]{1,0:T(8,128)(2,1)}) custom-call(bf16[736,1152]{1,0:T(8,128)(2,1)} %get-tuple-element.424.refs_0_.stream_ref.refs_7_, bf16[736,384]{1,0:T(8,128)(2,1)} %get-tuple-element.444.refs_0_, ...), custom_call_target="tpu_custom_call" | custom-call | flops 1 | bytes 1 | tf_op jit(solution)/shard_map/expand_hidden/pallas_call | solution.py:510
  248.5 12.2 %collective-permute-done.25.front_ref = bf16[3,72,1728]{2,1,0:T(8,128)(2,1)} collective-permute-done((bf16[3,72,1728]{2,1,0:T(8,128)(2,1)S(1)}, bf16[3,72,1728]{2,1,0:T(8,128)(2,1)}, u32[]{:S(2)}, u32[]{:S(2)}) %collective-permute-start.25) | collective-permute-done | bytes 746528 | tf_op jit(solution)/shard_map/ppermute | solution.py:31
  273.4 8.7 contract_hidden.2
  282.1 18.1 %collective-permute-done.26.across_ref = bf16[3,72,1728]{2,1,0:T(8,128)(2,1)} collective-permute-done((bf16[3,72,1728]{2,1,0:T(8,128)(2,1)}, bf16[3,72,1728]{2,1,0:T(8,128)(2,1)}, u32[]{:S(2)}, u32[]{:S(2)}) %collective-permute-start.26) | collective-permute-done | bytes 746528 | tf_op jit(solution)/shard_map/ppermute | solution.py:31
  312.9 11.5 %project_in.3 = (bf16[736,1152]{1,0:T(8,128)(2,1)}, bf16[736,1728]{1,0:T(8,128)(2,1)}, bf16[736,1152]{1,0:T(8,128)(2,1)}) custom-call(f32[736,1152]{1,0:T(8,128)} %get-tuple-element.451.refs_0_.refs_7_, bf16[736,384]{1,0:T(8,128)(2,1)} %get-tuple-element.474.refs_1_, bf16[736,384]{1,0:T(8,128)(2,1)} %get-tuple-element.475.refs_2_, ...), custom_call_target="tpu_custom_call" | custom-call | flops 1 | bytes 1 | tf_op jit(solution)/shard_map/project_in/pallas_call | solution.py:510
  324.4 16.2 %attention_forward.3 = (bf16[736,576]{1,0:T(8,128)(2,1)}, f32[8,1,736]{2,1,0:T(1,128)}) custom-call(bf16[736,1728]{1,0:T(8,128)(2,1)} %get-tuple-element.485.qkv_ref, f32[736,1]{1,0:T(8,128)} %broadcast_select_fusion.11.hidden_ref), custom_call_target="tpu_custom_call" | custom-call | flops 1 | bytes 1 | tf_op jit(solution)/shard_map/attention_forward/pallas_call | solution.py:420
  355.5 14.5 %expand_hidden.3 = (f32[736,1152]{1,0:T(8,128)}, bf16[736,1152]{1,0:T(8,128)(2,1)}, bf16[736,2176]{1,0:T(8,128)(2,1)}, bf16[736,2176]{1,0:T(8,128)(2,1)}) custom-call(bf16[736,1152]{1,0:T(8,128)(2,1)} %get-tuple-element.482.stream_ref.refs_7_, bf16[736,384]{1,0:T(8,128)(2,1)} %get-tuple-element.498.refs_0_, bf16[736,384]{1,0:T(8,128)(2,1)} %get-tuple-element.499.refs_1_, ...), custom_call_target="tpu_custom_call" | custom-call | flops 1 | bytes 1 | tf_op jit(solution)/shard_map/expand_hidden/pallas_call | solution.py:510
  370.0 10.8 %grad_halves.7 = (bf16[4,2,136,1152]{3,2,1,0:T(8,128)(2,1)}, bf16[4,2,136,1152]{3,2,1,0:T(8,128)(2,1)}) custom-call(s32[1]{0:T(128)} %bitcast.53.bit_ref, bf16[736,2176]{1,0:T(8,128)(2,1)} %get-tuple-element.513.left_ref, bf16[736,1152]{1,0:T(8,128)(2,1)} %get-tuple-element.508.d_ref.right_ref.refs_0_), custom_call_target="tpu_custom_call" | custom-call | flops 1 | bytes 1 | tf_op jit(solution)/shard_map/grad_halves/pallas_call | solution.py:269
  386.9 8.8 contract_hidden.3
  396.4 10.1 %back_hidden.2 = (bf16[736,2176]{1,0:T(8,128)(2,1)}, f32[1,2176]{1,0:T(1,128)}) custom-call(bf16[736,1152]{1,0:T(8,128)(2,1)} %get-tuple-element.508.d_ref.right_ref.refs_0_, bf16[2176,1152]{1,0:T(8,128)(2,1)} %bitcast.193, bf16[736,2176]{1,0:T(8,128)(2,1)} %get-tuple-element.511.slope_ref), custom_call_target="tpu_custom_call" | custom-call | flops 1 | bytes 1 | tf_op jit(solution)/shard_map/back_hidden/pallas_call | solution.py:510
  406.5 8.8 back_expand.2
  416.1 9.6 %grad_halves.8 = (bf16[4,2,72,2176]{3,2,1,0:T(8,128)(2,1)}, bf16[4,2,72,2176]{3,2,1,0:T(8,128)(2,1)}) custom-call(s32[1]{0:T(128)} %bitcast.54.bit_ref, bf16[736,1152]{1,0:T(8,128)(2,1)} %get-tuple-element.524.left_ref, bf16[736,2176]{1,0:T(8,128)(2,1)} %get-tuple-element.517.left_ref.right_ref), custom_call_target="tpu_custom_call" | custom-call | flops 1 | bytes 1 | tf_op jit(solution)/shard_map/grad_halves/pallas_call | solution.py:269
  427.9 10.2 %back_norm.4 = (bf16[736,1152]{1,0:T(8,128)(2,1)}, f32[4,1152]{1,0:T(4,128)}, f32[736,1152]{1,0:T(8,128)}, bf16[736,576]{1,0:T(8,128)(2,1)}) custom-call(bf16[736,1152]{1,0:T(8,128)(2,1)} %get-tuple-element.508.d_ref.right_ref.refs_0_, bf16[736,384]{1,0:T(8,128)(2,1)} %get-tuple-element.528.refs_1_, bf16[736,384]{1,0:T(8,128)(2,1)} %get-tuple-element.529.refs_2_, ...), custom_call_target="tpu_custom_call" | custom-call | flops 1 | bytes 1 | tf_op jit(solution)/shard_map/back_norm/pallas_call | solution.py:510
  453.3 24.6 %attention_backward.2.right_ref.left_ref = bf16[736,1728]{1,0:T(8,128)(2,1)} custom-call(bf16[736,1728]{1,0:T(8,128)(2,1)} %get-tuple-element.485.qkv_ref, bf16[736,576]{1,0:T(8,128)(2,1)} %get-tuple-element.549.do_ref, f32[8,1,736]{2,1,0:T(1,128)} %get-tuple-element.550.lse_ref, f32[736,1]{1,0:T(8,128)} %broadcast_select_fusion.11.hidden_ref), custom_call_target="tpu_custom_call" | custom-call | flops 1 | bytes 1 | tf_op jit(solution)/shard_map/attention_backward/pallas_call | solution.py:478
  477.9 8.2 grad_halves.9
  491.0 7.5 back_in.2
  498.4 11.0 %collective-permute-done.47 = bf16[4,136,1152]{2,1,0:T(8,128)(2,1)} collective-permute-done((bf16[4,136,1152]{2,1,0:T(8,128)(2,1)}, bf16[4,136,1152]{2,1,0:T(8,128)(2,1)}, u32[]{:S(2)}, u32[]{:S(2)}) %collective-permute-start.47) | collective-permute-done | bytes 1253408 | tf_op jit(solution)/shard_map/ppermute | solution.py:31
  514.1 7.7 back_norm.5
  521.8 10.0 %grad_halves.10 = (bf16[4,2,136,1152]{3,2,1,0:T(8,128)(2,1)}, bf16[4,2,136,1152]{3,2,1,0:T(8,128)(2,1)}) custom-call(s32[1]{0:T(128)} %bitcast.53.bit_ref, bf16[736,2176]{1,0:T(8,128)(2,1)} %get-tuple-element.457.left_ref, bf16[736,1152]{1,0:T(8,128)(2,1)} %get-tuple-element.592.right_ref.d_ref.refs_0_), custom_call_target="tpu_custom_call" | custom-call | flops 1 | bytes 1 | tf_op jit(solution)/shard_map/grad_halves/pallas_call | solution.py:269
  534.8 10.4 %back_hidden.3 = (bf16[736,2176]{1,0:T(8,128)(2,1)}, f32[1,2176]{1,0:T(1,128)}) custom-call(bf16[736,1152]{1,0:T(8,128)(2,1)} %get-tuple-element.592.right_ref.d_ref.refs_0_, bf16[2176,1152]{1,0:T(8,128)(2,1)} %bitcast.189, bf16[736,2176]{1,0:T(8,128)(2,1)} %get-tuple-element.593.slope_ref), custom_call_target="tpu_custom_call" | custom-call | flops 1 | bytes 1 | tf_op jit(solution)/shard_map/back_hidden/pallas_call | solution.py:510
  545.5 9.7 %grad_halves.11 = (bf16[4,2,72,2176]{3,2,1,0:T(8,128)(2,1)}, bf16[4,2,72,2176]{3,2,1,0:T(8,128)(2,1)}) custom-call(s32[1]{0:T(128)} %bitcast.54.bit_ref, bf16[736,1152]{1,0:T(8,128)(2,1)} %get-tuple-element.599.left_ref, bf16[736,2176]{1,0:T(8,128)(2,1)} %get-tuple-element.606.right_ref.left_ref), custom_call_target="tpu_custom_call" | custom-call | flops 1 | bytes 1 | tf_op jit(solution)/shard_map/grad_halves/pallas_call | solution.py:269
  555.2 7.3 collective-permute-done.51
  564.0 16.5 %collective-permute-done.52.moved_ref = bf16[4,2,72,1728]{3,2,1,0:T(8,128)(2,1)} collective-permute-done((bf16[4,2,72,1728]{3,2,1,0:T(8,128)(2,1)}, bf16[4,2,72,1728]{3,2,1,0:T(8,128)(2,1)}, u32[]{:S(2)}, u32[]{:S(2)}) %collective-permute-start.52) | collective-permute-done | bytes 1990688 | tf_op jit(solution)/shard_map/ppermute | solution.py:31
  585.3 8.7 back_expand.3
  598.4 10.2 %back_norm.6 = (bf16[736,1152]{1,0:T(8,128)(2,1)}, f32[4,1152]{1,0:T(4,128)}, f32[736,1152]{1,0:T(8,128)}, bf16[736,576]{1,0:T(8,128)(2,1)}) custom-call(bf16[736,1152]{1,0:T(8,128)(2,1)} %get-tuple-element.592.right_ref.d_ref.refs_0_, bf16[736,384]{1,0:T(8,128)(2,1)} %get-tuple-element.622.refs_1_, bf16[736,384]{1,0:T(8,128)(2,1)} %get-tuple-element.623.refs_2_, ...), custom_call_target="tpu_custom_call" | custom-call | flops 1 | bytes 1 | tf_op jit(solution)/shard_map/back_norm/pallas_call | solution.py:510
  612.9 24.8 %attention_backward.3.right_ref.left_ref = bf16[736,1728]{1,0:T(8,128)(2,1)} custom-call(bf16[736,1728]{1,0:T(8,128)(2,1)} %get-tuple-element.430.qkv_ref, bf16[736,576]{1,0:T(8,128)(2,1)} %get-tuple-element.638.do_ref, f32[8,1,736]{2,1,0:T(1,128)} %get-tuple-element.639.lse_ref, f32[736,1]{1,0:T(8,128)} %broadcast_select_fusion.11.hidden_ref), custom_call_target="tpu_custom_call" | custom-call | flops 1 | bytes 1 | tf_op jit(solution)/shard_map/attention_backward/pallas_call | solution.py:478
  643.5 6.6 grad_halves.12
  655.9 6.9 grad_halves.13
  667.3 7.6 back_in.3
  677.0 7.1 collective-permute-done.62
  687.4 7.9 back_norm.7
  703.2 21.5 %collective-permute-done.93 = f32[4,3392]{1,0:T(4,128)S(1)} collective-permute-done((f32[4,3392]{1,0:T(4,128)S(1)}, f32[4,3392]{1,0:T(4,128)S(1)}, u32[]{:S(2)}, u32[]{:S(2)}) %collective-permute-start.93) | collective-permute-done | bytes 54304 | tf_op jit(solution)/shard_map/ppermute | solution.py:31
  773.9 6.6 collective-permute-done.74
  800.7 12.4 %collective-permute-done.79 = bf16[72,832]{1,0:T(8,128)(2,1)S(1)} collective-permute-done((bf16[72,832]{1,0:T(8,128)(2,1)S(1)}, bf16[72,832]{1,0:T(8,128)(2,1)S(1)}, u32[]{:S(2)}, u32[]{:S(2)}) %collective-permute-start.79) | collective-permute-done | bytes 119840 | tf_op jit(solution)/shard_map/ppermute | solution.py:343
  814.7 6.6 collective-permute-done.72
  830.0 7.6 collective-permute-done.82
  846.6 7.9 join_rows.1
  856.8 11.3 %copy.75 = f32[1,1076,1152]{2,0,1:T(1,128)} copy(f32[1,1076,1152]{2,1,0:T(8,128)} %bitcast.198) | data formatting | bytes 9916416
  868.1 10.2 %collective-permute-done.87 = bf16[2,72,1728]{2,1,0:T(8,128)(2,1)S(1)} collective-permute-done((bf16[2,72,1728]{2,1,0:T(8,128)(2,1)S(1)}, bf16[2,72,1728]{2,1,0:T(8,128)(2,1)S(1)}, u32[]{:S(2)}, u32[]{:S(2)}) %collective-permute-start.87) | collective-permute-done | bytes 497696 | tf_op jit(solution)/shard_map/ppermute | solution.py:31
  (551 shorter events, 339.5 us)
Async XLA Ops:
  7.2 63.1 %all-gather.13.cloned.1.call-start = ((), (), s32[]{:S(2)}) async-start(), calls=%async_computation.7 | async-start | bytes 1566720 | tf_op jit(solution)/shard_map/all_gather | solution.py:207
  33.7 73.7 %all-gather.17.cloned.1.call-start = ((), (), s32[]{:S(2)}) async-start(), calls=%async_computation.12 | async-start | bytes 1843200 | tf_op jit(solution)/shard_map/all_gather | solution.py:754
  53.9 106.1 %all-gather.15.cloned.1.call-start = ((), (), s32[]{:S(2)}) async-start(), calls=%async_computation.8 | async-start | bytes 1566720 | tf_op jit(solution)/shard_map/all_gather | solution.py:207
  107.4 36.8 %collective-permute-start.13 = (bf16[3,72,1728]{2,1,0:T(8,128)(2,1)}, bf16[3,72,1728]{2,1,0:T(8,128)(2,1)}, u32[]{:S(2)}, u32[]{:S(2)}) collective-permute-start(bf16[3,72,1728]{2,1,0:T(8,128)(2,1)} %collective-permute-done.7.side_ref), channel_id=1, source_target_pairs={{0,8},{4,12},{8,0},{12,4},{1,9},{5,13},{9,1},{13,5},{2,10},{6,14},... | collective-permute-start | bytes 2239496 | tf_op jit(solution)/shard_map/ppermute | solution.py:31
  112.9 31.2 %collective-permute-start.11 = (bf16[184,1152]{1,0:T(8,128)(2,1)}, bf16[184,1152]{1,0:T(8,128)(2,1)}, u32[]{:S(2)}, u32[]{:S(2)}) collective-permute-start(bf16[184,1152]{1,0:T(8,128)(2,1)} %get-tuple-element.861), channel_id=1, source_target_pairs={{0,8},{4,12},{8,0},{12,4},{1,9},{5,13},{9,1},{13,5},{2,10},{6,14},... | collective-permute-start | bytes 1271816 | tf_op jit(solution)/shard_map/ppermute | solution.py:31
  114.4 29.8 %collective-permute-start.10 = (bf16[184,1152]{1,0:T(8,128)(2,1)}, bf16[184,1152]{1,0:T(8,128)(2,1)}, u32[]{:S(2)}, u32[]{:S(2)}) collective-permute-start(bf16[184,1152]{1,0:T(8,128)(2,1)} %get-tuple-element.862), channel_id=1, source_target_pairs={{0,4},{4,0},{8,12},{12,8},{1,5},{5,1},{9,13},{13,9},{2,6},{6,2},{1... | collective-permute-start | bytes 1271816 | tf_op jit(solution)/shard_map/ppermute | solution.py:31
  116.7 104.5 %all-gather.19.cloned.1.call-start = ((), (), s32[]{:S(2)}) async-start(), calls=%async_computation.13 | async-start | bytes 1433600 | tf_op jit(solution)/shard_map/all_gather | solution.py:207
  150.1 96.8 %all-gather.21.cloned.1.call-start = ((), (), s32[]{:S(2)}) async-start(), calls=%async_computation.14 | async-start | bytes 1566720 | tf_op jit(solution)/shard_map/all_gather | solution.py:207
  176.6 86.8 %all-gather.23.cloned.1.call-start = ((), (), s32[]{:S(2)}) async-start(), calls=%async_computation.15 | async-start | bytes 1843200 | tf_op jit(solution)/shard_map/all_gather | solution.py:812
  177.2 123.7 %all-gather.25.cloned.1.call-start = ((), (), s32[]{:S(2)}) async-start(), calls=%async_computation.16 | async-start | bytes 1566720 | tf_op jit(solution)/shard_map/all_gather | solution.py:207
  177.4 33.4 %collective-permute-start.17 = (bf16[3,72,2176]{2,1,0:T(8,128)(2,1)}, bf16[3,72,2176]{2,1,0:T(8,128)(2,1)}, u32[]{:S(2)}, u32[]{:S(2)}) collective-permute-start(bf16[3,72,2176]{2,1,0:T(8,128)(2,1)} %collective-permute-done.15.front_ref), channel_id=1, source_target_pairs={{0,4},{4,0},{8,12},{12,8},{1,5},{5,1},{9,13},{13,9},{2,6},{6,2},{1... | collective-permute-start | bytes 2820104 | tf_op jit(solution)/shard_map/ppermute | solution.py:31
  178.9 31.8 %collective-permute-start.19 = (bf16[3,136,1152]{2,1,0:T(8,128)(2,1)S(1)}, bf16[3,136,1152]{2,1,0:T(8,128)(2,1)S(1)}, u32[]{:S(2)}, u32[]{:S(2)}) collective-permute-start(bf16[3,136,1152]{2,1,0:T(8,128)(2,1)S(1)} %fusion.2.near_ref), channel_id=1, source_target_pairs={{0,8},{4,12},{8,0},{12,4},{1,9},{5,13},{9,1},{13,5},{2,10},{6,14},... | collective-permute-start | bytes 2820104 | tf_op jit(solution)/shard_map/ppermute | solution.py:31
  179.5 40.6 %collective-permute-start.18 = (bf16[3,136,1152]{2,1,0:T(8,128)(2,1)S(1)}, bf16[3,136,1152]{2,1,0:T(8,128)(2,1)}, u32[]{:S(2)}, u32[]{:S(2)}) collective-permute-start(bf16[3,136,1152]{2,1,0:T(8,128)(2,1)S(1)} %fusion.2.near_ref), channel_id=1, source_target_pairs={{0,4},{4,0},{8,12},{12,8},{1,5},{5,1},{9,13},{13,9},{2,6},{6,2},{1... | collective-permute-start | bytes 2820104 | tf_op jit(solution)/shard_map/ppermute | solution.py:31
  220.6 27.9 %collective-permute-start.23 = (bf16[3,136,1152]{2,1,0:T(8,128)(2,1)}, bf16[3,136,1152]{2,1,0:T(8,128)(2,1)S(1)}, u32[]{:S(2)}, u32[]{:S(2)}) collective-permute-start(bf16[3,136,1152]{2,1,0:T(8,128)(2,1)} %collective-permute-done.18.side_ref), channel_id=1, source_target_pairs={{0,8},{4,12},{8,0},{12,4},{1,9},{5,13},{9,1},{13,5},{2,10},{6,14},... | collective-permute-start | bytes 2820104 | tf_op jit(solution)/shard_map/ppermute | solution.py:31
  228.2 32.5 %collective-permute-start.25 = (bf16[3,72,1728]{2,1,0:T(8,128)(2,1)S(1)}, bf16[3,72,1728]{2,1,0:T(8,128)(2,1)}, u32[]{:S(2)}, u32[]{:S(2)}) collective-permute-start(bf16[3,72,1728]{2,1,0:T(8,128)(2,1)S(1)} %fusion.4.near_ref), channel_id=1, source_target_pairs={{0,8},{4,12},{8,0},{12,4},{1,9},{5,13},{9,1},{13,5},{2,10},{6,14},... | collective-permute-start | bytes 2239496 | tf_op jit(solution)/shard_map/ppermute | solution.py:31
  229.8 31.0 %collective-permute-start.24 = (bf16[3,72,1728]{2,1,0:T(8,128)(2,1)S(1)}, bf16[3,72,1728]{2,1,0:T(8,128)(2,1)}, u32[]{:S(2)}, u32[]{:S(2)}) collective-permute-start(bf16[3,72,1728]{2,1,0:T(8,128)(2,1)S(1)} %fusion.4.near_ref), channel_id=1, source_target_pairs={{0,4},{4,0},{8,12},{12,8},{1,5},{5,1},{9,13},{13,9},{2,6},{6,2},{1... | collective-permute-start | bytes 2239496 | tf_op jit(solution)/shard_map/ppermute | solution.py:31
  231.3 367.2 %reduce-scatter.16.cloned.1.call-start = ((), (), s32[]{:S(2)}) async-start(), calls=%async_computation.9 | async-start | bytes 1658880 | tf_op jit(solution)/shard_map/reduce_scatter | solution.py:903
  260.7 39.5 %collective-permute-start.28 = (bf16[3,72,2176]{2,1,0:T(8,128)(2,1)S(1)}, bf16[3,72,2176]{2,1,0:T(8,128)(2,1)S(1)}, u32[]{:S(2)}, u32[]{:S(2)}) collective-permute-start(bf16[3,72,2176]{2,1,0:T(8,128)(2,1)S(1)} %fusion.1.near_ref), channel_id=1, source_target_pairs={{0,8},{4,12},{8,0},{12,4},{1,9},{5,13},{9,1},{13,5},{2,10},{6,14},... | collective-permute-start | bytes 2820104 | tf_op jit(solution)/shard_map/ppermute | solution.py:31
  261.3 38.9 %collective-permute-start.27 = (bf16[3,72,2176]{2,1,0:T(8,128)(2,1)S(1)}, bf16[3,72,2176]{2,1,0:T(8,128)(2,1)S(1)}, u32[]{:S(2)}, u32[]{:S(2)}) collective-permute-start(bf16[3,72,2176]{2,1,0:T(8,128)(2,1)S(1)} %fusion.1.near_ref), channel_id=1, source_target_pairs={{0,4},{4,0},{8,12},{12,8},{1,5},{5,1},{9,13},{13,9},{2,6},{6,2},{1... | collective-permute-start | bytes 2820104 | tf_op jit(solution)/shard_map/ppermute | solution.py:31
  262.8 37.4 %collective-permute-start.26 = (bf16[3,72,1728]{2,1,0:T(8,128)(2,1)}, bf16[3,72,1728]{2,1,0:T(8,128)(2,1)}, u32[]{:S(2)}, u32[]{:S(2)}) collective-permute-start(bf16[3,72,1728]{2,1,0:T(8,128)(2,1)} %collective-permute-done.25.front_ref), channel_id=1, source_target_pairs={{0,4},{4,0},{8,12},{12,8},{1,5},{5,1},{9,13},{13,9},{2,6},{6,2},{1... | collective-permute-start | bytes 2239496 | tf_op jit(solution)/shard_map/ppermute | solution.py:31
  302.4 42.2 %collective-permute-start.32 = (bf16[3,72,2176]{2,1,0:T(8,128)(2,1)S(1)}, bf16[3,72,2176]{2,1,0:T(8,128)(2,1)}, u32[]{:S(2)}, u32[]{:S(2)}) collective-permute-start(bf16[3,72,2176]{2,1,0:T(8,128)(2,1)S(1)} %collective-permute-done.27.side_ref), channel_id=1, source_target_pairs={{0,8},{4,12},{8,0},{12,4},{1,9},{5,13},{9,1},{13,5},{2,10},{6,14},... | collective-permute-start | bytes 2820104 | tf_op jit(solution)/shard_map/ppermute | solution.py:31
  309.2 37.0 %collective-permute-start.34 = (bf16[3,136,1152]{2,1,0:T(8,128)(2,1)S(1)}, bf16[3,136,1152]{2,1,0:T(8,128)(2,1)S(1)}, u32[]{:S(2)}, u32[]{:S(2)}) collective-permute-start(bf16[3,136,1152]{2,1,0:T(8,128)(2,1)S(1)} %fusion.near_ref), channel_id=1, source_target_pairs={{0,8},{4,12},{8,0},{12,4},{1,9},{5,13},{9,1},{13,5},{2,10},{6,14},... | collective-permute-start | bytes 2820104 | tf_op jit(solution)/shard_map/ppermute | solution.py:31
  309.9 36.3 %collective-permute-start.33 = (bf16[3,136,1152]{2,1,0:T(8,128)(2,1)S(1)}, bf16[3,136,1152]{2,1,0:T(8,128)(2,1)}, u32[]{:S(2)}, u32[]{:S(2)}) collective-permute-start(bf16[3,136,1152]{2,1,0:T(8,128)(2,1)S(1)} %fusion.near_ref), channel_id=1, source_target_pairs={{0,4},{4,0},{8,12},{12,8},{1,5},{5,1},{9,13},{13,9},{2,6},{6,2},{1... | collective-permute-start | bytes 2820104 | tf_op jit(solution)/shard_map/ppermute | solution.py:31
  380.8 61.7 %collective-permute-start.45 = (bf16[4,2,136,1152]{3,2,1,0:T(8,128)(2,1)}, bf16[4,2,136,1152]{3,2,1,0:T(8,128)(2,1)S(1)}, u32[]{:S(2)}, u32[]{:S(2)}) collective-permute-start(bf16[4,2,136,1152]{3,2,1,0:T(8,128)(2,1)} %get-tuple-element.541), channel_id=1, source_target_pairs={{0,4},{4,0},{8,12},{12,8},{1,5},{5,1},{9,13},{13,9},{2,6},{6,2},{1... | collective-permute-start | bytes 7520264 | tf_op jit(solution)/shard_map/ppermute | solution.py:31
  396.2 29.5 %collective-permute-start.44 = (bf16[736,384]{1,0:T(8,128)(2,1)}, bf16[736,384]{1,0:T(8,128)(2,1)S(1)}, u32[]{:S(2)}, u32[]{:S(2)}) collective-permute-start(bf16[736,384]{1,0:T(8,128)(2,1)} %get-tuple-element.523), channel_id=1, source_target_pairs={{0,16},{16,0},{1,17},{17,1},{2,18},{18,2},{3,19},{19,3},{4,20},{20... | collective-permute-start | bytes 1695752 | tf_op jit(solution)/shard_map/ppermute | solution.py:26
  425.7 60.4 %collective-permute-start.46 = (bf16[4,2,72,2176]{3,2,1,0:T(8,128)(2,1)}, bf16[4,2,72,2176]{3,2,1,0:T(8,128)(2,1)}, u32[]{:S(2)}, u32[]{:S(2)}) collective-permute-start(bf16[4,2,72,2176]{3,2,1,0:T(8,128)(2,1)} %get-tuple-element.554), channel_id=1, source_target_pairs={{0,8},{4,12},{8,0},{12,4},{1,9},{5,13},{9,1},{13,5},{2,10},{6,14},... | collective-permute-start | bytes 7520264 | tf_op jit(solution)/shard_map/ppermute | solution.py:31
  442.4 170.4 %reduce-scatter.22.cloned.1.call-start = ((), (), s32[]{:S(2)}) async-start(), calls=%async_computation.17 | async-start | bytes 1566720
  449.0 60.5 %collective-permute-start.47 = (bf16[4,136,1152]{2,1,0:T(8,128)(2,1)}, bf16[4,136,1152]{2,1,0:T(8,128)(2,1)}, u32[]{:S(2)}, u32[]{:S(2)}) collective-permute-start(bf16[4,136,1152]{2,1,0:T(8,128)(2,1)} %get-tuple-element.567), channel_id=1, source_target_pairs={{0,8},{4,12},{8,0},{12,4},{1,9},{5,13},{9,1},{13,5},{2,10},{6,14},... | collective-permute-start | bytes 3760136 | tf_op jit(solution)/shard_map/ppermute | solution.py:31
  531.8 145.2 %reduce-scatter.24.cloned.1.call-start = ((), (), s32[]{:S(2)}) async-start(), calls=%async_computation.18 | async-start | bytes 1566720
  531.9 30.7 %collective-permute-start.51 = (bf16[4,72,2176]{2,1,0:T(8,128)(2,1)}, bf16[4,72,2176]{2,1,0:T(8,128)(2,1)S(1)}, u32[]{:S(2)}, u32[]{:S(2)}) collective-permute-start(bf16[4,72,2176]{2,1,0:T(8,128)(2,1)} %get-tuple-element.598), channel_id=1, source_target_pairs={{0,4},{4,0},{8,12},{12,8},{1,5},{5,1},{9,13},{13,9},{2,6},{6,2},{1... | collective-permute-start | bytes 3760136 | tf_op jit(solution)/shard_map/ppermute | solution.py:31
  533.4 47.1 %collective-permute-start.52 = (bf16[4,2,72,1728]{3,2,1,0:T(8,128)(2,1)}, bf16[4,2,72,1728]{3,2,1,0:T(8,128)(2,1)}, u32[]{:S(2)}, u32[]{:S(2)}) collective-permute-start(bf16[4,2,72,1728]{3,2,1,0:T(8,128)(2,1)} %get-tuple-element.611), channel_id=1, source_target_pairs={{0,8},{4,12},{8,0},{12,4},{1,9},{5,13},{9,1},{13,5},{2,10},{6,14},... | collective-permute-start | bytes 5971976 | tf_op jit(solution)/shard_map/ppermute | solution.py:31
  545.2 92.4 %collective-permute-start.58 = (bf16[4,2,136,1152]{3,2,1,0:T(8,128)(2,1)}, bf16[4,2,136,1152]{3,2,1,0:T(8,128)(2,1)S(1)}, u32[]{:S(2)}, u32[]{:S(2)}) collective-permute-start(bf16[4,2,136,1152]{3,2,1,0:T(8,128)(2,1)} %get-tuple-element.648), channel_id=1, source_target_pairs={{0,4},{4,0},{8,12},{12,8},{1,5},{5,1},{9,13},{13,9},{2,6},{6,2},{1... | collective-permute-start | bytes 7520264 | tf_op jit(solution)/shard_map/ppermute | solution.py:31
  564.0 185.2 %reduce-scatter.20.cloned.1.call-start = ((), (), s32[]{:S(2)}) async-start(), calls=%async_computation.11 | async-start | bytes 1290240 | tf_op jit(solution)/shard_map/reduce_scatter | solution.py:336
  584.8 65.4 %collective-permute-start.57 = (bf16[4,72,1728]{2,1,0:T(8,128)(2,1)}, bf16[4,72,1728]{2,1,0:T(8,128)(2,1)S(1)}, u32[]{:S(2)}, u32[]{:S(2)}) collective-permute-start(bf16[4,72,1728]{2,1,0:T(8,128)(2,1)} %get-tuple-element.646), channel_id=1, source_target_pairs={{0,4},{4,0},{8,12},{12,8},{1,5},{5,1},{9,13},{13,9},{2,6},{6,2},{1... | collective-permute-start | bytes 2985992 | tf_op jit(solution)/shard_map/ppermute | solution.py:31
  596.3 66.5 %collective-permute-start.56 = (bf16[4,2,72,2176]{3,2,1,0:T(8,128)(2,1)}, bf16[4,2,72,2176]{3,2,1,0:T(8,128)(2,1)}, u32[]{:S(2)}, u32[]{:S(2)}) collective-permute-start(bf16[4,2,72,2176]{3,2,1,0:T(8,128)(2,1)} %get-tuple-element.643), channel_id=1, source_target_pairs={{0,8},{4,12},{8,0},{12,4},{1,9},{5,13},{9,1},{13,5},{2,10},{6,14},... | collective-permute-start | bytes 7520264 | tf_op jit(solution)/shard_map/ppermute | solution.py:31
  653.7 102.0 %reduce-scatter.18.cloned.1.call-start = ((), (), s32[]{:S(2)}) async-start(), calls=%async_computation.10 | async-start | bytes 1658880 | tf_op jit(solution)/shard_map/reduce_scatter | solution.py:946
  654.4 29.7 %collective-permute-start.62 = (bf16[4,136,1152]{2,1,0:T(8,128)(2,1)}, bf16[4,136,1152]{2,1,0:T(8,128)(2,1)}, u32[]{:S(2)}, u32[]{:S(2)}) collective-permute-start(bf16[4,136,1152]{2,1,0:T(8,128)(2,1)} %get-tuple-element.677), channel_id=1, source_target_pairs={{0,8},{4,12},{8,0},{12,4},{1,9},{5,13},{9,1},{13,5},{2,10},{6,14},... | collective-permute-start | bytes 3760136 | tf_op jit(solution)/shard_map/ppermute | solution.py:31
  675.9 104.6 %reduce-scatter.26.cloned.1.call-start = ((), (), s32[]{:S(2)}) async-start(), calls=%async_computation.19 | async-start | bytes 1566720
  697.6 35.4 %collective-permute-start.66 = (bf16[4,2,72,896]{3,2,1,0:T(8,128)(2,1)}, bf16[4,2,72,896]{3,2,1,0:T(8,128)(2,1)}, u32[]{:S(2)}, u32[]{:S(2)}) collective-permute-start(bf16[4,2,72,896]{3,2,1,0:T(8,128)(2,1)} %get-tuple-element.700), channel_id=1, source_target_pairs={{0,4},{4,0},{8,12},{12,8},{1,5},{5,1},{9,13},{13,9},{2,6},{6,2},{1... | collective-permute-start | bytes 3096584 | tf_op jit(solution)/shard_map/ppermute | solution.py:31
  699.3 25.4 %collective-permute-start.93 = (f32[4,3392]{1,0:T(4,128)S(1)}, f32[4,3392]{1,0:T(4,128)S(1)}, u32[]{:S(2)}, u32[]{:S(2)}) collective-permute-start(f32[4,3392]{1,0:T(4,128)S(1)} %select_add_fusion), channel_id=1, source_target_pairs={{0,4},{4,0},{8,12},{12,8},{1,5},{5,1},{9,13},{13,9},{2,6},{6,2},{1... | collective-permute-start | bytes 162824 | tf_op jit(solution)/shard_map/ppermute | solution.py:31
  701.1 37.4 %collective-permute-start.67 = (bf16[4,2,72,832]{3,2,1,0:T(8,128)(2,1)}, bf16[4,2,72,832]{3,2,1,0:T(8,128)(2,1)}, u32[]{:S(2)}, u32[]{:S(2)}) collective-permute-start(bf16[4,2,72,832]{3,2,1,0:T(8,128)(2,1)} %get-tuple-element.705), channel_id=1, source_target_pairs={{0,8},{4,12},{8,0},{12,4},{1,9},{5,13},{9,1},{13,5},{2,10},{6,14},... | collective-permute-start | bytes 2875400 | tf_op jit(solution)/shard_map/ppermute | solution.py:31
  702.4 49.3 %collective-permute-start.69 = (bf16[4,72,2176]{2,1,0:T(8,128)(2,1)}, bf16[4,72,2176]{2,1,0:T(8,128)(2,1)}, u32[]{:S(2)}, u32[]{:S(2)}) collective-permute-start(bf16[4,72,2176]{2,1,0:T(8,128)(2,1)} %get-tuple-element.711), channel_id=1, source_target_pairs={{0,4},{4,0},{8,12},{12,8},{1,5},{5,1},{9,13},{13,9},{2,6},{6,2},{1... | collective-permute-start | bytes 3760136 | tf_op jit(solution)/shard_map/ppermute | solution.py:31
  727.8 112.7 %reduce-scatter.28.cloned.1.call-start = ((), (), s32[]{:S(2)}) async-start(), calls=%async_computation.20 | async-start | bytes 1566720
  745.7 34.8 %collective-permute-start.74 = (bf16[4,72,832]{2,1,0:T(8,128)(2,1)}, bf16[4,72,832]{2,1,0:T(8,128)(2,1)}, u32[]{:S(2)}, u32[]{:S(2)}) collective-permute-start(bf16[4,72,832]{2,1,0:T(8,128)(2,1)} %get-tuple-element.728), channel_id=1, source_target_pairs={{0,4},{4,0},{8,12},{12,8},{1,5},{5,1},{9,13},{13,9},{2,6},{6,2},{1... | collective-permute-start | bytes 1437704 | tf_op jit(solution)/shard_map/ppermute | solution.py:31
  786.8 26.3 %collective-permute-start.79 = (bf16[72,832]{1,0:T(8,128)(2,1)S(1)}, bf16[72,832]{1,0:T(8,128)(2,1)S(1)}, u32[]{:S(2)}, u32[]{:S(2)}) collective-permute-start(bf16[72,832]{1,0:T(8,128)(2,1)S(1)} %get-tuple-element.868), channel_id=1, source_target_pairs={{0,2},{1,3},{2,0},{3,1},{4,6},{5,7},{6,4},{7,5},{8,10},{9,11},{10,... | collective-permute-start | bytes 359432 | tf_op jit(solution)/shard_map/ppermute | solution.py:343
  787.4 34.0 %collective-permute-start.77 = (bf16[2,136,1152]{2,1,0:T(8,128)(2,1)S(1)}, bf16[2,136,1152]{2,1,0:T(8,128)(2,1)S(1)}, u32[]{:S(2)}, u32[]{:S(2)}) collective-permute-start(bf16[2,136,1152]{2,1,0:T(8,128)(2,1)S(1)} %pad_maximum_fusion.7), channel_id=1, source_target_pairs={{0,8},{4,12},{8,0},{12,4},{1,9},{5,13},{9,1},{13,5},{2,10},{6,14},... | collective-permute-start | bytes 1880072 | tf_op jit(solution)/shard_map/ppermute | solution.py:31
  788.7 32.8 %collective-permute-start.76 = (bf16[2,136,1152]{2,1,0:T(8,128)(2,1)S(1)}, bf16[2,136,1152]{2,1,0:T(8,128)(2,1)S(1)}, u32[]{:S(2)}, u32[]{:S(2)}) collective-permute-start(bf16[2,136,1152]{2,1,0:T(8,128)(2,1)S(1)} %pad_maximum_fusion.7), channel_id=1, source_target_pairs={{0,4},{4,0},{8,12},{12,8},{1,5},{5,1},{9,13},{13,9},{2,6},{6,2},{1... | collective-permute-start | bytes 1880072 | tf_op jit(solution)/shard_map/ppermute | solution.py:31
  856.2 34.2 %collective-permute-start.91 = (bf16[2,144,1152]{2,1,0:T(8,128)(2,1)S(1)}, bf16[2,144,1152]{2,1,0:T(8,128)(2,1)S(1)}, u32[]{:S(2)}, u32[]{:S(2)}) collective-permute-start(bf16[2,144,1152]{2,1,0:T(8,128)(2,1)S(1)} %add_convert_fusion.7), channel_id=1, source_target_pairs={{0,4},{4,0},{8,12},{12,8},{1,5},{5,1},{9,13},{13,9},{2,6},{6,2},{1... | collective-permute-start | bytes 1990664 | tf_op jit(solution)/shard_map/ppermute | solution.py:31
  (128 other events, 1423.2 us)
Sparse Core Ops, SparseCore 0:
  33.8 36.3 all-gather.12
  72.4 34.9 all-gather.16
  116.8 29.6 all-gather.14
  150.2 29.4 all-gather.18
  181.1 31.1 all-gather.20
  213.8 34.5 all-gather.22
  249.9 30.5 all-gather.24
  442.5 30.5 reduce-scatter.15
  532.0 29.8 reduce-scatter.21
  564.1 29.8 reduce-scatter.23
  653.8 26.3 reduce-scatter.19
  683.0 30.2 reduce-scatter.17
  728.0 29.3 reduce-scatter.25
  770.4 40.9 reduce-scatter.27

commit v2 on v1

--- a/solution.py
+++ b/solution.py
@@ -7,7 +7,7 @@
 
 HEAD_DIM = 72
 SCALE = HEAD_DIM**-0.5
-VMEM_LIMIT = 56 * 1024 * 1024
+VMEM_LIMIT = 32 * 1024 * 1024
 F32 = jnp.float32
 BF16 = jnp.bfloat16
 LIGHT = pl.CostEstimate(flops=1, bytes_accessed=1, transcendentals=0)
@@ -26,9 +26,24 @@
     return jax.tree.map(lambda array: lax.ppermute(array, "section", swap), value)
 
 
-def swap_seq(value, bit):
+def swap_seq(value, bits):
+    bits = bits if isinstance(bits, tuple) else (bits, bits)
     count = lax.axis_size("seq")
-    return lax.ppermute(value, "seq", [(index, index ^ bit) for index in range(count)])
+    pairs = [
+        (core * count + index, core * count + (index ^ bits[core]))
+        for core in range(2)
+        for index in range(count)
+        if bits[core]
+    ]
+    return lax.ppermute(value, ("section", "seq"), pairs)
+
+
+FIRST, SECOND = (1, 2), (2, 1)
+
+
+def relative_bits():
+    core = lax.axis_index("section")
+    return (0, 1 + core, 2 - core, 3)
 
 
 def dot(left, right, left_axis, right_axis):
@@ -111,7 +126,7 @@
             num_scalar_prefetch=1,
             grid=(count,),
             in_specs=[block, block],
-            out_specs=pl.BlockSpec((1, rows, total), lambda j, place: (j ^ place[1], 0, 0)),
+            out_specs=pl.BlockSpec((1, rows, total), lambda j, place: (place[1 + j], 0, 0)),
         ),
         compiler_params=params_of(),
         cost_estimate=LIGHT,
@@ -128,18 +143,18 @@
 
         @pl.when(half == place_ref[0])
         def _():
-            out_ref[...] = mine_ref[0].astype(F32)
+            out_ref[:, 0, :] = mine_ref[0].astype(F32)
 
         @pl.when(half != place_ref[0])
         def _():
-            out_ref[...] = other_ref[0].astype(F32)
+            out_ref[:, 0, :] = other_ref[0].astype(F32)
 
     def quarter(step):
         return lax.rem(step, count)
 
     return pl.pallas_call(
         kernel,
-        out_shape=jax.ShapeDtypeStruct((total, width), F32),
+        out_shape=jax.ShapeDtypeStruct((total, 1, width), F32),
         grid_spec=pltpu.PrefetchScalarGridSpec(
             num_scalar_prefetch=1,
             grid=(2 * count,),
@@ -148,8 +163,8 @@
                 pl.BlockSpec((1, rows, width), lambda t, place: (quarter(t), 0, 0)),
             ],
             out_specs=pl.BlockSpec(
-                (rows, width),
-                lambda t, place: (lax.div(t, count) * count + (quarter(t) ^ place[1]), 0),
+                (rows, 1, width),
+                lambda t, place: (lax.div(t, count) * count + place[1 + quarter(t)], 0, 0),
             ),
         ),
         compiler_params=params_of(),
@@ -158,20 +173,22 @@
     )(place, mine, other)
 
 
-def assemble(own, near, side, front, across):
+def assemble(own, near, first, second, across):
     parts, rows, columns = near.shape
     count = parts + 1
-    place = jnp.stack([lax.axis_index("dp"), lax.axis_index("seq")]).astype(jnp.int32)
-
-    def kernel(place_ref, own_ref, near_ref, side_ref, front_ref, across_ref, out_ref, sem):
-        along, here = place_ref[0], place_ref[1]
+    here = lax.axis_index("seq")
+    place = [lax.axis_index("dp")] + [here ^ bits for bits in relative_bits()]
+    place = jnp.stack(place).astype(jnp.int32)
+
+    def kernel(place_ref, own_ref, near_ref, first_ref, second_ref, across_ref, out_ref, sem):
+        along = place_ref[0]
         copies = [pltpu.make_async_copy(own_ref, out_ref.at[along], sem.at[0])]
         for step in range(parts):
             there = lax.rem(along + step + 1, count)
-            for bits, ref in enumerate((near_ref, side_ref, front_ref, across_ref)):
+            for index, ref in enumerate((near_ref, first_ref, second_ref, across_ref)):
                 copies.append(
                     pltpu.make_async_copy(
-                        ref.at[step], out_ref.at[there, here ^ bits], sem.at[len(copies)]
+                        ref.at[step], out_ref.at[there, place_ref[1 + index]], sem.at[len(copies)]
                     )
                 )
         for copy in copies:
@@ -189,17 +206,15 @@
         compiler_params=params_of(),
         cost_estimate=LIGHT,
         name="assemble",
-    )(place, own, near, side, front, across)
+    )(place, own, near, first, second, across)
 
 
 def line_shifts(value):
     count = lax.axis_size("dp")
-    return jnp.stack(
-        [
-            lax.ppermute(value, "dp", [((to + step) % count, to) for to in range(count)])
-            for step in range(1, count)
-        ]
-    )
+    return [
+        lax.ppermute(value, "dp", [((to + step) % count, to) for to in range(count)])
+        for step in range(1, count)
+    ]
 
 
 def line_gather(value):
@@ -215,56 +230,52 @@
 
 
 def spread(near):
-    return swap_seq(near, 1), swap_seq(near, 2)
-
-
-def spread_on(neighbours, by_side):
-    side, front = neighbours
-    return swap_seq(front, 1) if by_side else swap_seq(side, 2)
+    return swap_seq(near, FIRST), swap_seq(near, SECOND)
+
+
+def spread_on(neighbours):
+    return swap_seq(neighbours[1], FIRST)
 
 
 def bits_of_place():
-    here = lax.axis_index("seq")
-    return lax.rem(here, 2), lax.div(here, 2)
-
-
-def grad_halves(left, right, count, by_side, start, end):
+    core, here = lax.axis_index("section"), lax.axis_index("seq")
+    x, y = lax.rem(here, 2), lax.div(here, 2)
+    first, second = jnp.where(core == 0, x, y), jnp.where(core == 0, y, x)
+    return jnp.stack([core, first, second]).astype(jnp.int32)
+
+
+def grad_halves(left, right, count):
     length, depth = left.shape
-    columns = end - start
+    columns = right.shape[1]
     rows = depth // count
     quarter = round_up(rows, 32) // 4
-    x, y = bits_of_place()
-    bit = (x if by_side else y).astype(jnp.int32).reshape(1)
-
-    def kernel(bit_ref, left_ref, right_ref, keep_ref, send_ref, turned):
+
+    def kernel(bits_ref, left_ref, right_ref, keep_ref, send_ref, turned):
         block = pl.program_id(0)
 
         @pl.when(block == 0)
         def _():
             turned[...] = left_ref[...].astype(F32).T.astype(BF16).reshape(turned.shape)
 
-        grad = dot(turned[block], right_ref[:, start:end], 1, 0)
+        grad = dot(turned[block], right_ref[...], 1, 0)
         if 4 * quarter > rows:
             empty = jnp.zeros((4 * quarter - rows, columns), F32)
             grad = jnp.concatenate([grad, empty], axis=0)
-        parts = [grad[at * quarter : (at + 1) * quarter].astype(BF16) for at in range(4)]
-        zeros, ones = ((0, 2), (1, 3)) if by_side else ((0, 1), (2, 3))
-
-        def write(ref, which):
-            for index, at in enumerate(which):
-                ref[0, index] = parts[at]
-
-        @pl.when(bit_ref[0] == 0)
-        def _():
-            write(keep_ref, zeros)
-            write(send_ref, ones)
-
-        @pl.when(bit_ref[0] == 1)
-        def _():
-            write(keep_ref, ones)
-            write(send_ref, zeros)
-
-    out = pl.BlockSpec((1, 2, quarter, columns), lambda z, bit: (z, 0, 0, 0))
+        for at in range(4):
+            part = grad[at * quarter : (at + 1) * quarter].astype(BF16)
+            x, y = at % 2, at // 2
+            first = jnp.where(bits_ref[0] == 0, x, y)
+            second = jnp.where(bits_ref[0] == 0, y, x)
+
+            @pl.when(first == bits_ref[1])
+            def _():
+                keep_ref[0, second] = part
+
+            @pl.when(first != bits_ref[1])
+            def _():
+                send_ref[0, second] = part
+
+    out = pl.BlockSpec((1, 2, quarter, columns), lambda z, bits: (z, 0, 0, 0))
     shape = jax.ShapeDtypeStruct((count, 2, quarter, columns), BF16)
     return pl.pallas_call(
         kernel,
@@ -273,8 +284,8 @@
             num_scalar_prefetch=1,
             grid=(count,),
             in_specs=[
-                pl.BlockSpec((length, depth), lambda z, bit: (0, 0)),
-                pl.BlockSpec(right.shape, lambda z, bit: (0, 0)),
+                pl.BlockSpec((length, depth), lambda z, bits: (0, 0)),
+                pl.BlockSpec((length, columns), lambda z, bits: (0, 0)),
             ],
             out_specs=(out, out),
             scratch_shapes=[pltpu.VMEM((count, rows, length), BF16)],
@@ -282,23 +293,21 @@
         compiler_params=params_of(),
         cost_estimate=LIGHT,
         name="grad_halves",
-    )(bit, left, right)
-
-
-def add_half(held, moved, by_side):
+    )(bits_of_place(), left, right)
+
+
+def add_half(held, moved):
     count, _, rows, columns = held.shape
-    x, y = bits_of_place()
-    bit = (y if by_side else x).astype(jnp.int32).reshape(1)
-
-    def kernel(bit_ref, held_ref, moved_ref, keep_ref, send_ref):
+
+    def kernel(bits_ref, held_ref, moved_ref, keep_ref, send_ref):
         def total(index):
             return (held_ref[0, index].astype(F32) + moved_ref[0, index].astype(F32)).astype(BF16)
 
-        keep_ref[0] = total(bit_ref[0])
-        send_ref[0] = total(1 - bit_ref[0])
-
-    both = pl.BlockSpec((1, 2, rows, columns), lambda z, bit: (z, 0, 0, 0))
-    out = pl.BlockSpec((1, rows, columns), lambda z, bit: (z, 0, 0))
+        keep_ref[0] = total(bits_ref[2])
+        send_ref[0] = total(1 - bits_ref[2])
+
+    both = pl.BlockSpec((1, 2, rows, columns), lambda z, bits: (z, 0, 0, 0))
+    out = pl.BlockSpec((1, rows, columns), lambda z, bits: (z, 0, 0))
     shape = jax.ShapeDtypeStruct((count, rows, columns), BF16)
     return pl.pallas_call(
         kernel,
@@ -309,7 +318,7 @@
         compiler_params=params_of(),
         cost_estimate=LIGHT,
         name="add_half",
-    )(bit, held, moved)
+    )(bits_of_place(), held, moved)
 
 
 def add_low(left, right):
@@ -317,36 +326,34 @@
 
 
 class Sum:
-    def __init__(self, left, right, count, by_side, columns=None):
-        self.by_side = by_side
-        start, end = columns or (0, right.shape[1])
-        self.keep, self.send = grad_halves(left, right, count, by_side, start, end)
+    def __init__(self, left, right, count):
+        self.keep, self.send = grad_halves(left, right, count)
 
     def first(self):
-        self.moved = swap_seq(self.send, 1 if self.by_side else 2)
+        self.moved = swap_seq(self.send, FIRST)
 
     def add(self):
-        self.keep, self.send = add_half(self.keep, self.moved, self.by_side)
+        self.keep, self.send = add_half(self.keep, self.moved)
 
     def second(self):
-        self.moved = swap_seq(self.send, 2 if self.by_side else 1)
+        self.moved = swap_seq(self.send, SECOND)
 
     def over_line(self, gate):
         part = gate(add_low(self.keep, self.moved))
         self.line = lax.psum_scatter(part, "dp", scatter_dimension=0, tiled=True)[0]
 
-    def over_line_shifts(self):
-        line, count = lax.axis_index("dp"), lax.axis_size("dp")
-        part = self.keep.astype(F32) + self.moved.astype(F32)
-        total = pick(part, line)
-        for step in range(1, count):
-            moved = lax.ppermute(
-                pick(part, lax.rem(line + step, count)).astype(BF16),
-                "dp",
-                [(source, (source + step) % count) for source in range(count)],
-            )
-            total = total + moved.astype(F32)
-        self.line = total.astype(BF16)
+
+def line_sum(part):
+    line, count = lax.axis_index("dp"), lax.axis_size("dp")
+    total = pick(part, line).astype(F32)
+    for step in range(1, count):
+        moved = lax.ppermute(
+            pick(part, lax.rem(line + step, count)),
+            "dp",
+            [(source, (source + step) % count) for source in range(count)],
+        )
+        total = total + moved.astype(F32)
+    return total.astype(BF16)
 
 
 def plain_grad(left, right):
@@ -443,7 +450,9 @@
     length, width = d_out.shape
     heads = width // HEAD_DIM
 
-    def kernel(qkv_ref, do_ref, lse_ref, hidden_ref, out_ref, q_s, k_s, v_s, do_s, dq_s, dk_s, dv_s):
+    def kernel(
+        qkv_ref, do_ref, lse_ref, hidden_ref, out_ref, sums_ref, q_s, k_s, v_s, do_s, dq_s, dk_s, dv_s
+    ):
         head = pl.program_id(0)
 
         @pl.when(head == 0)
@@ -473,19 +482,26 @@
                 out_ref[:, at : at + HEAD_DIM] = dq_s[index]
                 out_ref[:, width + at : width + at + HEAD_DIM] = dk_s[index]
                 out_ref[:, 2 * width + at : 2 * width + at + HEAD_DIM] = dv_s[index]
+            sums_ref[...] = jnp.sum(out_ref[...].astype(F32), axis=0, keepdims=True)
 
     slab = pltpu.VMEM((heads, length, HEAD_DIM), BF16)
     return pl.pallas_call(
         kernel,
         grid=(heads,),
-        out_shape=jax.ShapeDtypeStruct((length, 3 * width), BF16),
+        out_shape=(
+            jax.ShapeDtypeStruct((length, 3 * width), BF16),
+            jax.ShapeDtypeStruct((1, 3 * width), F32),
+        ),
         in_specs=[
             pl.BlockSpec((length, 3 * width), lambda h: (0, 0)),
             pl.BlockSpec((length, width), lambda h: (0, 0)),
             pl.BlockSpec((1, 1, length), lambda h: (h, 0, 0)),
             pl.BlockSpec((length, 1), lambda h: (0, 0)),
         ],
-        out_specs=pl.BlockSpec((length, 3 * width), lambda h: (0, 0)),
+        out_specs=(
+            pl.BlockSpec((length, 3 * width), lambda h: (0, 0)),
+            pl.BlockSpec((1, 3 * width), lambda h: (0, 0)),
+        ),
         scratch_shapes=[slab] * 7,
         compiler_params=params_of(),
         cost_estimate=LIGHT,
@@ -518,7 +534,12 @@
     )(*arrays)
 
 
-PIECES = 3
+PIECES = 2
+
+
+def piece_bounds(columns):
+    step = round_up(columns // PIECES, 128)
+    return [(at * step, min((at + 1) * step, columns)) for at in range(PIECES)]
 
 
 def join_pieces(refs):
@@ -526,25 +547,24 @@
 
 
 def partial_product(left, weight, turned, name):
-    length = left.shape[0]
+    length, depth = left.shape
     columns = weight.shape[0 if turned else 1]
-    piece = columns // PIECES
+    bounds = piece_bounds(columns)
 
     def kernel(left_ref, weight_ref, *out_refs):
         for start, end in tiles(columns):
             if turned:
-                product = dot(left_ref[...], weight_ref[start:end, :], 1, 1)
+                product = dot(left_ref[...], weight_ref[start:end, :depth], 1, 1)
             else:
                 product = dot(left_ref[...], weight_ref[:, start:end], 1, 0)
             product = product.astype(BF16)
-            for index, ref in enumerate(out_refs):
-                low, high = max(start, index * piece), min(end, (index + 1) * piece)
+            for ref, (first, last) in zip(out_refs, bounds):
+                low, high = max(start, first), min(end, last)
                 if low < high:
-                    ref[:, low - index * piece : high - index * piece] = product[
-                        :, low - start : high - start
-                    ]
-
-    return whole_call(kernel, name, [((length, piece), BF16)] * PIECES, left, weight)
+                    ref[:, low - first : high - first] = product[:, low - start : high - start]
+
+    shapes = [((length, last - first), BF16) for first, last in bounds]
+    return whole_call(kernel, name, shapes, left, weight)
 
 
 def project_in(base, partials, vectors, weight, shift):
@@ -591,7 +611,7 @@
 
 def expand_hidden(stream, own, other, vectors, weight, shift):
     length, width = stream.shape
-    columns = weight.shape[1]
+    columns = shift.shape[1]
     root = 0.7978845608028654
 
     def kernel(stream_ref, *refs):
@@ -699,7 +719,6 @@
     count = lax.axis_size("dp")
     first = core == 0
     core_ref = core.astype(jnp.int32).reshape(1)
-    place_ref = jnp.stack([core, here]).astype(jnp.int32)
 
     width = attention_out.shape[2]
     own_rows = attention_out.shape[1]
@@ -733,61 +752,69 @@
         whole = whole.reshape(count, -1, whole.shape[3])[:, :rows]
         return whole.reshape(count * rows, whole.shape[2])
 
+    micro, images, block, _ = section_inputs.shape[1:]
+    tokens = section_inputs[0].reshape(micro * images, block, width)
+    token_blocks = [pick(tokens, here ^ bits) for bits in range(4)]
+    hidden_shift = jnp.pad(expand_bias[0], (0, 2 * half_hidden - own_hidden))
+    packed = jnp.concatenate([norm_gains[0].reshape(-1), biases[0].reshape(-1), hidden_shift])
+    small_size = packed.size
+    packed = jnp.concatenate(both_layers(packed, packed))
     in_own, in_mine = prepared(
         both_layers(*split_columns(attention_in[0], in_runs, in_width, core_ref))
     )
-    in_mine, attention_out, expand_weight, contract_weight, norm_gains, biases, expand_bias = gate(
-        in_mine, attention_out, expand_weight, contract_weight, norm_gains, biases, expand_bias
-    )
-
-    near_in_0 = line_shifts(in_mine[0])
-    hidden_shift = jnp.pad(expand_bias[0], (0, 2 * half_hidden - own_hidden))
-    packed = jnp.concatenate([norm_gains[0].reshape(-1), biases[0].reshape(-1), hidden_shift])
-    packed = both_layers(packed, packed)
-    packed_rows = round_up(packed[0].size, width) // width
+    packed_rows = round_up(round_up(packed.size, in_width) // in_width, 8)
+    packed = jnp.pad(packed, (0, packed_rows * in_width - packed.size)).reshape(-1, in_width)
+    first_rows = in_mine[0].shape[0]
+    in_first = jnp.concatenate([in_mine[0], packed], axis=0)
+    token_blocks, in_first, expand_weight, attention_out, contract_weight = gate(
+        token_blocks, in_first, expand_weight, attention_out, contract_weight
+    )
+    near_in_0 = line_shifts(in_first)
+    inputs = [swap_seq(token_blocks[bits], (bits, 0)) for bits in range(1, 4)]
     out_parts = attention_out[0].reshape(2, half_heads, width)
     out_halves = both_layers(pick(out_parts, core), pick(out_parts, 1 - core))
-    out_whole = []
-    for half, vector in zip(out_halves, packed):
-        vector = jnp.pad(vector, (0, packed_rows * width - vector.size)).reshape(-1, width)
-        out_whole.append(pad_rows(jnp.concatenate([half, vector], axis=0)))
-    out_0 = lax.all_gather(out_whole[0], "dp", axis=0)
+    expand_halves = both_layers(
+        *split_columns(expand_weight[0], hidden_runs, hidden_width, core_ref)
+    )
     expand_own, expand_mine = prepared(
-        both_layers(*split_columns(expand_weight[0], hidden_runs, hidden_width, core_ref))
-    )
+        [
+            jnp.concatenate([high, low.reshape(own_rows, -1)], axis=1)
+            for high, low in zip(expand_halves, out_halves)
+        ]
+    )
+    expand_mine = gate(expand_mine)
     near_expand_0 = line_gather(expand_mine[0])
-    near_in_0, expand_mine, out_whole, contract_weight, section_inputs = gate(
-        near_in_0, expand_mine, out_whole, contract_weight, section_inputs
-    )
-
-    beside_in_0 = spread(near_in_0)
+
+    def heads_of(merged):
+        return merged[:, hidden_width:].reshape(count * half_heads, width)
+
     contract_parts = jnp.pad(
         contract_weight[0], ((0, 2 * half_hidden - own_hidden), (0, 0))
     ).reshape(2, half_hidden, width)
     contract_own, contract_mine = prepared(
         both_layers(pick(contract_parts, core), pick(contract_parts, 1 - core))
     )
+    contract_mine = gate(contract_mine)
     near_contract_0 = line_gather(contract_mine[0])
-    beside_in_0, out_0, near_expand_0, contract_mine, in_mine, section_inputs = gate(
-        beside_in_0, out_0, near_expand_0, contract_mine, in_mine, section_inputs
-    )
-
-    across_in_0 = spread_on(beside_in_0, False)
-    micro, images, block, _ = section_inputs.shape[1:]
-    tokens = section_inputs[0].reshape(micro * images, block, width)
-    pieces = [pick(tokens, here)]
-    pieces += [swap_seq(pick(tokens, here ^ bits), bits) for bits in range(1, 4)]
-    in_padded = jnp.pad(in_mine[1], ((0, 8), (0, 0)))
-    near_in_1 = line_gather(in_padded)[:, : in_mine[1].shape[0]]
+    near_in_0, inputs = gate(near_in_0, inputs)
+    packed = [packed] + [part[first_rows:] for part in near_in_0]
+    near_in_0 = jnp.stack([part[:first_rows] for part in near_in_0])
+    beside_in_0, near_expand_0 = gate(spread(near_in_0), near_expand_0)
+    across_in_0 = spread_on(beside_in_0)
+    image = jnp.concatenate([token_blocks[0], *inputs], axis=0)
+    start = jnp.where(first, image, swap_cores(image))
     mask = pick(key_mask.reshape(micro * images, 4, block), here)
     mask = jnp.concatenate([pick(mask, here ^ bits) for bits in range(4)])
     hidden_keys = jnp.where(mask > 0, 0.0, 1.0).astype(F32)[:, None]
 
-    def small_of(gathered):
-        packed = gathered[:, half_heads : half_heads + packed_rows].reshape(count, -1)
-        packed = packed.astype(F32)
+    packed = jnp.stack([part.reshape(-1) for part in packed])
+    packed = lax.dynamic_slice_in_dim(
+        jnp.concatenate([packed, packed], 0), lax.rem(count - line, count), count, 0
+    ).astype(F32)
+
+    def small_of(packed):
         vectors = packed[:, : 8 * own_rows].reshape(count, 8, own_rows)
-        hidden = packed[:, 8 * own_rows :][:, : 2 * half_hidden].reshape(count, 2, half_hidden)
+        hidden = packed[:, 8 * own_rows :].reshape(count, 2, half_hidden)
         heads_part = pick(vectors.reshape(count, 8, 2, half_heads), core, 2)
         vectors = vectors.transpose(1, 0, 2).reshape(8, width)
         query, value = heads_part[:, 4].reshape(-1), heads_part[:, 5].reshape(-1)
@@ -795,302 +822,267 @@
         hidden_shift = pick(hidden, core, 1).reshape(1, -1)
         return vectors, qkv_shift.reshape(1, -1), hidden_shift
 
-    def heads_of(gathered):
-        return gathered[:, :half_heads].reshape(count * half_heads, width)
-
-    vectors_0, qkv_shift_0, hidden_shift_0 = small_of(out_0)
-    attn_out_0 = heads_of(out_0)
-    pieces, across_in_0, near_expand_0, out_whole, qkv_shift_0 = gate(
-        pieces, across_in_0, near_expand_0, out_whole, qkv_shift_0
-    )
+    vectors_0, qkv_shift_0, hidden_shift_0 = small_of(packed[:, :small_size])
+    vectors_1, qkv_shift_1, hidden_shift_1 = small_of(packed[:, small_size : 2 * small_size])
+    across_in_0, start, hidden_keys, qkv_shift_0, in_mine, expand_mine = gate(
+        across_in_0, start, hidden_keys, qkv_shift_0, in_mine, expand_mine
+    )
+
     beside_expand_0 = spread(near_expand_0)
-    image = jnp.concatenate(pieces, axis=0)
-    other = swap_cores(image)
-    start = jnp.where(first, image, other)
-    cotangent = jnp.where(first, other, image)
+    near_in_1 = line_shifts(in_mine[1])
     attn_in_0 = built(in_own[0], near_in_0, (*beside_in_0, across_in_0), own_rows)
-    out_1 = lax.all_gather(out_whole[1], "dp", axis=0)
-    beside_expand_0, near_contract_0, start, attn_in_0, hidden_keys, expand_mine = gate(
-        beside_expand_0, near_contract_0, start, attn_in_0, hidden_keys, expand_mine
-    )
-
-    across_expand_0 = spread_on(beside_expand_0, True)
+    stream_0, normed_0, qkv_0 = project_in(start, None, vectors_0, attn_in_0, qkv_shift_0)
+    beside_expand_0, near_in_1, qkv_0, expand_mine = gate(
+        beside_expand_0, near_in_1, qkv_0, expand_mine
+    )
+    across_expand_0 = spread_on(beside_expand_0)
+    near_in_1 = jnp.stack(near_in_1)
+    beside_in_1 = spread(near_in_1)
+    near_expand_1 = line_gather(expand_mine[1])
+    mixed_0, lse_0 = attention_forward(qkv_0, hidden_keys)
+    mixed_0, across_expand_0 = gate(mixed_0, across_expand_0)
+    expand_0 = built(expand_own[0], near_expand_0, (*beside_expand_0, across_expand_0), own_rows)
+    attn_out_0 = heads_of(expand_0)
+    own = partial_product(mixed_0, attn_out_0, False, "project_heads")
+    own, beside_in_1, near_contract_0, contract_mine = gate(
+        own, beside_in_1, near_contract_0, contract_mine
+    )
+    across_in_1 = spread_on(beside_in_1)
     beside_contract_0 = spread(near_contract_0)
-    near_expand_1 = line_gather(expand_mine[1])
-    stream_0, normed_0, qkv_0 = project_in(start, None, vectors_0, attn_in_0, qkv_shift_0)
-    mixed_0, lse_0 = attention_forward(qkv_0, hidden_keys)
-    own = partial_product(mixed_0, attn_out_0, False, "project_heads")
-    across_expand_0, beside_contract_0, contract_mine, own = gate(
-        across_expand_0, beside_contract_0, contract_mine, own
-    )
-    expand_0 = built(expand_own[0], near_expand_0, (*beside_expand_0, across_expand_0), own_rows)
-    own, other, expand_0, near_in_1 = gate(own, swap_cores(own), expand_0, near_in_1)
-
-    across_contract_0 = spread_on(beside_contract_0, False)
-    beside_in_1 = spread(near_in_1)
     near_contract_1 = line_gather(contract_mine[1])
+    own, other = gate(own, swap_cores(own))
     middle_0, normed_mid_0, hidden_0, slope_0 = expand_hidden(
         stream_0, own, other, vectors_0, expand_0, hidden_shift_0
     )
-    across_contract_0, beside_in_1, near_expand_1, hidden_0 = gate(
-        across_contract_0, beside_in_1, near_expand_1, hidden_0
-    )
-
-    across_in_1 = spread_on(beside_in_1, True)
+    hidden_0, across_in_1, beside_contract_0, near_expand_1 = gate(
+        hidden_0, across_in_1, beside_contract_0, near_expand_1
+    )
+    across_contract_0 = spread_on(beside_contract_0)
     beside_expand_1 = spread(near_expand_1)
+    attn_in_1 = built(in_own[1], near_in_1, (*beside_in_1, across_in_1), own_rows)
+    attn_in_1, across_contract_0 = gate(attn_in_1, across_contract_0)
     contract_0 = built(
         contract_own[0], near_contract_0, (*beside_contract_0, across_contract_0), half_hidden
     )
-    own = partial_product(hidden_0, contract_0, False, "contract_hidden")
-    vectors_1, qkv_shift_1, hidden_shift_1 = small_of(out_1)
-    attn_out_1 = heads_of(out_1)
-    own, across_in_1, beside_expand_1, qkv_shift_1, attn_out_1 = gate(
-        own, across_in_1, beside_expand_1, qkv_shift_1, attn_out_1
-    )
-    attn_in_1 = built(in_own[1], near_in_1, (*beside_in_1, across_in_1), own_rows)
-    own, other, attn_in_1, near_contract_1 = gate(own, swap_cores(own), attn_in_1, near_contract_1)
-
-    across_expand_1 = spread_on(beside_expand_1, False)
-    beside_contract_1 = spread(near_contract_1)
+    own = gate(partial_product(hidden_0, contract_0, False, "contract_hidden"))
+    own, other, token_blocks = gate(own, swap_cores(own), token_blocks)
+
+    cotangents = [swap_seq(token_blocks[bits], (0, bits)) for bits in range(1, 3)]
     partials = (own, other, vectors_0[7:8])
     stream_1, normed_1, qkv_1 = project_in(middle_0, partials, vectors_1, attn_in_1, qkv_shift_1)
+    beside_expand_1, near_contract_1, qkv_1, cotangents, token_blocks = gate(
+        beside_expand_1, near_contract_1, qkv_1, cotangents, token_blocks
+    )
+    across_expand_1 = spread_on(beside_expand_1)
+    beside_contract_1 = spread(near_contract_1)
+    cotangents.append(swap_seq(token_blocks[3], (0, 3)))
     mixed_1, lse_1 = attention_forward(qkv_1, hidden_keys)
+    mixed_1, across_expand_1 = gate(mixed_1, across_expand_1)
+    expand_1 = built(expand_own[1], near_expand_1, (*beside_expand_1, across_expand_1), own_rows)
+    attn_out_1 = heads_of(expand_1)
     own = partial_product(mixed_1, attn_out_1, False, "project_heads")
-    across_expand_1, beside_contract_1, own = gate(across_expand_1, beside_contract_1, own)
-    expand_1 = built(expand_own[1], near_expand_1, (*beside_expand_1, across_expand_1), own_rows)
-    own, other, expand_1 = gate(own, swap_cores(own), expand_1)
-
-    across_contract_1 = spread_on(beside_contract_1, True)
+    own, beside_contract_1, cotangents = gate(own, beside_contract_1, cotangents)
+    across_contract_1 = spread_on(beside_contract_1)
+    image = jnp.concatenate([token_blocks[0], *cotangents], axis=0)
+    own, other = gate(own, swap_cores(own))
+    cotangent = jnp.where(first, swap_cores(image), image)
     middle_1, normed_mid_1, hidden_1, slope_1 = expand_hidden(
         stream_1, own, other, vectors_1, expand_1, hidden_shift_1
     )
     hidden_1, across_contract_1, cotangent = gate(hidden_1, across_contract_1, cotangent)
+
+    small_rows = round_up(7 + round_up(hidden_width, width) // width, 16)
+
+    def out_sum(grad, in_sums, mid_sums, hidden_sums, qkv_sums):
+        heads = [qkv_sums[:, : width // 2], qkv_sums[:, width:]]
+        rows = [in_sums[:1], mid_sums[:1], in_sums[1:2], mid_sums[1:], jnp.concatenate(heads, axis=1)]
+        spare = (small_rows - 7) * width - hidden_width
+        rows.append(jnp.pad(hidden_sums, ((0, 0), (0, spare))).reshape(-1, width))
+        small = jnp.concatenate(rows, axis=0).astype(BF16)
+        small = jnp.broadcast_to(small, (count, small_rows, width))
+        parts = [grad.reshape(count, half_heads, width), small]
+        part = gate(jnp.concatenate(parts, axis=1))
+        return lax.psum_scatter(part, "dp", scatter_dimension=0, tiled=True)[0]
+
+    def own_layer(low, high):
+        return jnp.stack([jnp.where(first, low, high), swap_cores(jnp.where(first, high, low))])
+
+    def last_place():
+        return jnp.stack([gate.token, *(here ^ bits for bits in relative_bits())]).astype(jnp.int32)
+
+    def rows_of(pieces, total):
+        mine, other = jnp.stack(pieces, axis=1)
+        return join_rows(mine, other, total, last_place())
+
+    def columns_of(pieces, runs, total):
+        mine, other = jnp.stack(pieces, axis=1)
+        return join_columns(mine, other, runs, total, last_place())
+
+    contract_sum_1 = Sum(hidden_1, cotangent, count)
+    gate.sent(contract_sum_1)
+    contract_sum_1.first()
     contract_1 = built(
         contract_own[1], near_contract_1, (*beside_contract_1, across_contract_1), half_hidden
     )
-
-    def rows_of(pieces, rows, total):
-        mine, other = jnp.stack(pieces, axis=1)
-        if 4 * mine.shape[1] == rows:
-            return join_rows(mine, other, total, place_ref)
-        halves = [jnp.where(first, mine, other), jnp.where(first, other, mine)]
-        halves = [in_order(half).reshape(-1, width)[:rows] for half in halves]
-        return jnp.concatenate(halves, axis=0).astype(F32)[:total]
-
-    def columns_of(pieces, runs, total, place):
-        mine, other = jnp.stack(pieces, axis=1)
-        return join_columns(mine, other, runs, total, place)[:own_rows]
-
-    contract_sum_1 = Sum(hidden_1, cotangent, count, True)
-    gate.sent(contract_sum_1)
-    contract_sum_1.first()
-    own_out = partial_product(hidden_1, contract_1, False, "contract_hidden")
     d_pre_1, hidden_sums_1 = back_hidden(cotangent, contract_1, slope_1)
     d_pre_1 = gate(d_pre_1)
-    expand_sum_1 = Sum(normed_mid_1, d_pre_1, count, False)
+    expand_sum_1 = Sum(normed_mid_1, d_pre_1, count)
     gate.sent(expand_sum_1)
     expand_sum_1.first()
-    own = partial_product(d_pre_1, expand_1, True, "back_expand")
+    own = gate(partial_product(gate(d_pre_1), expand_1, True, "back_expand"))
+    gate.arrived(contract_sum_1)
+    contract_sum_1.add()
+    own_out = partial_product(hidden_1, contract_1, False, "contract_hidden")
+    own, other, own_out = gate(own, swap_cores(own), own_out)
+    gate.sent(contract_sum_1)
+    contract_sum_1.second()
+    d_branch_1, mid_sums_1, d_middle_1, d_mixed_1 = back_norm(
+        cotangent, own, other, middle_1, vectors_1[1:2], attn_out_1
+    )
+    d_branch_1, d_mixed_1 = gate(d_branch_1, d_mixed_1)
+    out_grad_1 = plain_grad(mixed_1, d_branch_1)
+    gate.arrived(expand_sum_1)
+    expand_sum_1.add()
+    gate.sent(expand_sum_1)
+    expand_sum_1.second()
+    d_qkv_1, qkv_sums_1 = gate(attention_backward(qkv_1, gate(d_mixed_1), lse_1, hidden_keys))
+    gate.arrived(contract_sum_1)
+    contract_sum_1.over_line(gate)
+    in_sum_1 = Sum(normed_1, gate(d_qkv_1), count)
+    gate.sent(in_sum_1)
+    in_sum_1.first()
+    gate.arrived(expand_sum_1)
+    expand_sum_1.over_line(gate)
+    own = gate(partial_product(gate(d_qkv_1), attn_in_1, True, "back_in"))
     own, other, other_out = gate(own, swap_cores(own), swap_cores(own_out))
     own_out, other_out = jnp.concatenate(own_out, axis=1), jnp.concatenate(other_out, axis=1)
     output = middle_1 + own_out.astype(F32) + other_out.astype(F32) + vectors_1[7:8]
     output = output.astype(BF16)
-    d_branch_1, mid_sums_1, d_middle_1, d_mixed_1 = back_norm(
-        cotangent, own, other, middle_1, vectors_1[1:2], attn_out_1
-    )
-    d_branch_1, d_mixed_1 = gate(d_branch_1, d_mixed_1)
-    out_grad_1 = gate(plain_grad(mixed_1, d_branch_1))
-    out_line_1 = lax.psum_scatter(out_grad_1, "dp", scatter_dimension=0, tiled=True)
-    gate.arrived(contract_sum_1)
-    contract_sum_1.add()
-    gate.sent(contract_sum_1)
-    contract_sum_1.second()
-    d_qkv_1 = attention_backward(qkv_1, gate(d_mixed_1), lse_1, hidden_keys)
-    d_qkv_1 = gate(d_qkv_1)
-    in_sum_1 = Sum(normed_1, d_qkv_1, count, False)
-    gate.sent(in_sum_1)
-    in_sum_1.first()
-    gate.arrived(expand_sum_1)
-    expand_sum_1.add()
-    gate.sent(expand_sum_1)
-    expand_sum_1.second()
-    own = partial_product(gate(d_qkv_1), attn_in_1, True, "back_in")
-    gate.arrived(contract_sum_1)
-    own = gate(own)
-    own, other, output = gate(own, swap_cores(own), output)
     d_result_0, in_sums_1 = back_norm(d_middle_1, own, other, stream_1, vectors_1[0:1], None)
     d_result_0 = gate(d_result_0)
-    contract_sum_0 = Sum(hidden_0, d_result_0, count, True)
-    gate.sent(contract_sum_0)
-    contract_sum_0.first()
-    contract_sum_1.over_line(gate)
-    d_pre_0, hidden_sums_0 = back_hidden(gate(d_result_0), contract_0, slope_0)
-    d_pre_0 = gate(d_pre_0)
-    expand_sum_0 = Sum(normed_mid_0, d_pre_0, count, False)
-    gate.sent(expand_sum_0)
-    gate.arrived(expand_sum_1)
-    expand_sum_0.first()
-    expand_sum_1.over_line(gate)
-    own = partial_product(gate(d_pre_0), expand_0, True, "back_expand")
     gate.arrived(in_sum_1)
     in_sum_1.add()
     gate.sent(in_sum_1)
-    own = gate(own)
-    own, other, out_line_1 = gate(own, swap_cores(own), out_line_1)
     in_sum_1.second()
+
+    contract_sum_0 = Sum(hidden_0, gate(d_result_0), count)
+    gate.sent(contract_sum_0)
+    contract_sum_0.first()
+    d_pre_0, hidden_sums_0 = back_hidden(gate(d_result_0), contract_0, slope_0)
+    d_pre_0, output = gate(d_pre_0, output)
+    gate.arrived(in_sum_1)
+    in_sum_1.over_line(gate)
+    expand_sum_0 = Sum(normed_mid_0, gate(d_pre_0), count)
+    gate.sent(expand_sum_0)
+    expand_sum_0.first()
+    gate.summed(contract_sum_1)
+    own = gate(partial_product(gate(d_pre_0), expand_0, True, "back_expand"))
+    gate.arrived(contract_sum_0)
+    contract_sum_0.add()
+    own, other = gate(own, swap_cores(own))
+    gate.sent(contract_sum_0)
+    contract_sum_0.second()
     d_branch_0, mid_sums_0, d_middle_0, d_mixed_0 = back_norm(
-        d_result_0, own, other, middle_0, vectors_0[1:2], attn_out_0
+        d_result_0, gate(own), other, middle_0, vectors_0[1:2], attn_out_0
     )
     d_branch_0, d_mixed_0 = gate(d_branch_0, d_mixed_0)
     out_grad_0 = gate(plain_grad(mixed_0, d_branch_0))
-    out_line_0 = lax.psum_scatter(out_grad_0, "dp", scatter_dimension=0, tiled=True)
-    gate.summed(contract_sum_1)
-    d_qkv_0 = gate(attention_backward(qkv_0, gate(d_mixed_0), lse_0, hidden_keys))
-    gate.arrived(contract_sum_0)
-    contract_sum_0.add()
-    gate.sent(contract_sum_0)
-    contract_sum_0.second()
-    cut = round_up(in_width // 2, 128)
-    in_sums_a = Sum(normed_0, gate(d_qkv_0), count, True, (0, cut))
-    gate.sent(in_sums_a)
-    gate.arrived(in_sum_1)
-    in_sums_a.first()
-    in_sum_1.over_line(gate)
-    in_sums_b = Sum(normed_0, gate(d_qkv_0), count, False, (cut, in_width))
-    gate.sent(in_sums_b)
+    gate.summed(expand_sum_1)
+    out_line_1 = out_sum(out_grad_1, in_sums_1, mid_sums_1, hidden_sums_1, qkv_sums_1)
+    output = output.reshape(4, block, width)
+    outputs = [swap_seq(output[bits], (0, bits)) for bits in range(1, 4)]
+    d_qkv_0, qkv_sums_0 = gate(attention_backward(qkv_0, gate(d_mixed_0), lse_0, hidden_keys))
+    outputs = gate(outputs)
     gate.arrived(expand_sum_0)
-    in_sums_b.first()
     expand_sum_0.add()
     gate.sent(expand_sum_0)
-    own = partial_product(gate(d_qkv_0), attn_in_0, True, "back_in")
-    own = gate(own)
-    gate.summed(expand_sum_1)
+    expand_sum_0.second()
     gate.arrived(contract_sum_0)
+    contract_sum_0.over_line(gate)
+    in_sum_0 = Sum(normed_0, gate(d_qkv_0), count)
+    gate.sent(in_sum_0)
+    in_sum_0.first()
+    gate.summed(in_sum_1)
+    own = gate(partial_product(gate(d_qkv_0), attn_in_0, True, "back_in"))
     own, other = gate(own, swap_cores(own))
-    expand_sum_0.second()
-    contract_sum_0.over_line(gate)
-    d_input_0, in_sums_0 = back_norm(d_middle_0, gate(own), other, stream_0, vectors_0[0:1], None)
-    d_input_0 = gate(d_input_0)
-    gate.arrived(in_sums_a, in_sums_b)
-    in_sums_a.add()
-    in_sums_b.add()
-    gate.sent(in_sums_a, in_sums_b)
-    in_sums_a.second()
-    in_sums_b.second()
-    gate.summed(in_sum_1)
     gate.arrived(expand_sum_0)
     expand_sum_0.over_line(gate)
-
-    def own_layer(low, high):
-        return jnp.stack([jnp.where(first, low, high), swap_cores(jnp.where(first, high, low))])
-
-    out_line_0 = gate(out_line_0)
+    d_input_0, in_sums_0 = back_norm(d_middle_0, gate(own), other, stream_0, vectors_0[0:1], None)
+    d_input_0, out_line_1 = gate(d_input_0, out_line_1)
+
+    d_input_0 = d_input_0.reshape(4, block, width)
+    gate.arrived(in_sum_0)
+    in_sum_0.add()
+    gate.summed(contract_sum_0)
+    gate.sent(in_sum_0)
+    in_sum_0.second()
+    contract_near = own_layer(contract_sum_0.line, contract_sum_1.line)
+    gate.arrived(in_sum_0)
+    contract_near = gate(contract_near)
+    contract_beside = spread(contract_near)
+    in_sum_0.over_line(gate)
+    gate.summed(expand_sum_0)
+    contract_beside = gate(contract_beside)
+    contract_across = spread_on(contract_beside)
+    inputs_back = [swap_seq(d_input_0[bits], (bits, 0)) for bits in range(1, 3)]
+    expand_near = own_layer(expand_sum_0.line, expand_sum_1.line)
+    contract_across, inputs_back, expand_near = gate(contract_across, inputs_back, expand_near)
+    expand_beside = spread(expand_near)
+    inputs_back.append(swap_seq(d_input_0[3], (3, 0)))
+    grad_contract = rows_of([contract_near, *contract_beside, contract_across], own_hidden)
+    gate.summed(in_sum_0)
+    out_line_0 = out_sum(out_grad_0, in_sums_0, mid_sums_0, hidden_sums_0, qkv_sums_0)
+    expand_beside, grad_contract, inputs_back = gate(expand_beside, grad_contract, inputs_back)
+    in_near = gate(own_layer(in_sum_0.line, in_sum_1.line))
+    in_beside = spread(in_near)
+    expand_across = spread_on(expand_beside)
+    in_beside, expand_across = gate(in_beside, expand_across)
+    in_across = spread_on(in_beside)
+    grad_expand = columns_of(
+        [expand_near, *expand_beside, expand_across], hidden_runs, count * own_hidden
+    )
+    out_line_0, in_across, grad_expand = gate(out_line_0, in_across, grad_expand)
     out_near = gate(own_layer(out_line_0, out_line_1))
-    gate.arrived(in_sums_a, in_sums_b)
-    in_sums_a.over_line_shifts()
-    in_sums_b.over_line_shifts()
-    gate.summed(contract_sum_0)
-    contract_near = gate(own_layer(contract_sum_0.line, contract_sum_1.line))
-    contract_beside = gate(spread(contract_near))
-    contract_across = spread_on(contract_beside, True)
-    out_moved = swap_seq(out_near, 2)
-    gate.summed(in_sums_a, in_sums_b)
-    contract_across, out_moved = gate(contract_across, out_moved)
+    out_moved = swap_seq(out_near, FIRST)
+    grad_in = columns_of([in_near, *in_beside, in_across], in_runs, 3 * width)
+    out_moved, grad_in = gate(out_moved, grad_in)
     out_near = add_low(out_near, out_moved)
-    in_line_0 = jnp.concatenate([in_sums_a.line, in_sums_b.line], axis=1)
-    in_near = gate(own_layer(in_line_0, in_sum_1.line))
-    in_beside = spread(in_near)
-    grad_contract = rows_of(
-        [contract_near, *contract_beside, contract_across], half_hidden, own_hidden
-    )
-    gate.summed(expand_sum_0)
-    expand_near = gate(own_layer(expand_sum_0.line, expand_sum_1.line))
-    in_beside, grad_contract = gate(in_beside, grad_contract)
-    in_across = spread_on(in_beside, True)
-    expand_beside = spread(expand_near)
-    in_across, expand_beside = gate(in_across, expand_beside)
-    expand_across = spread_on(expand_beside, False)
-    out_moved = swap_seq(out_near, 1)
-    last_place = jnp.stack([gate.token, here]).astype(jnp.int32)
-    grad_in = columns_of([in_near, *in_beside, in_across], in_runs, 3 * width, last_place)
-    expand_across, out_moved, grad_in = gate(expand_across, out_moved, grad_in)
-    out_near = add_low(out_near, out_moved).astype(F32)
-    grad_out = jnp.concatenate(
-        [jnp.where(first, out_near[0], out_near[1]), jnp.where(first, out_near[1], out_near[0])]
-    )
-    last_place = jnp.stack([gate.token, here]).astype(jnp.int32)
-    grad_expand = columns_of(
-        [expand_near, *expand_beside, expand_across],
-        hidden_runs,
-        count * own_hidden,
-        last_place,
-    )
-
-    def small_sums(in_sums, mid_sums, hidden_sums, d_qkv):
-        heads = column_sums(d_qkv).reshape(3, -1)
-        shared = jnp.stack(
-            [in_sums[0], mid_sums[0], in_sums[1], mid_sums[1], mid_sums[2], mid_sums[3]]
-        )
-        return shared, heads[0], heads[2], hidden_sums[0]
-
-    small_0 = small_sums(in_sums_0, mid_sums_0, hidden_sums_0, d_qkv_0)
-    small_1 = small_sums(in_sums_1, mid_sums_1, hidden_sums_1, d_qkv_1)
-
-    def pack_small(small):
-        shared, query, value, hidden = small
-        shared = jnp.where(first, shared, 0.0)
-        none = jnp.zeros((count, half_heads), F32)
-
-        def spread(vector, size):
-            vector = vector.reshape(count, size)
-            nothing = jnp.zeros_like(vector)
-            return jnp.concatenate(
-                [jnp.where(first, vector, nothing), jnp.where(first, nothing, vector)], axis=1
-            )
-
-        shared = shared.reshape(6, count, own_rows)
-        return jnp.concatenate(
-            [
-                shared[0],
-                shared[1],
-                shared[2],
-                shared[3],
-                spread(query, half_heads),
-                spread(value, half_heads),
-                shared[4],
-                shared[5],
-                spread(hidden, half_hidden),
-            ],
-            axis=1,
-        )
-
-    low_sums, high_sums = pack_small(small_0), pack_small(small_1)
-    sums = jnp.where(first, low_sums, high_sums)
-    sums = sums + swap_cores(jnp.where(first, high_sums, low_sums))
-    sums = sums + swap_seq(sums, 1)
-    sums = sums + swap_seq(sums, 2)
-    total = pick(sums, line)
-    for step in range(1, count):
-        total = total + lax.ppermute(
-            pick(sums, lax.rem(line + step, count)),
-            "dp",
-            [(source, (source + step) % count) for source in range(count)],
-        )
-    sums = total
-
-    result = jnp.where(first, d_input_0, output).reshape(4, block, width)
-    returned = jnp.stack([result[0]] + [swap_seq(result[bits], bits) for bits in range(1, 4)])
-    results = in_order(returned).astype(F32).reshape(1, micro, images, block, width)
+    out_moved = swap_seq(out_near, SECOND)
+    returned = [
+        jnp.where(first, low, high)
+        for low, high in zip([d_input_0[0], *inputs_back], [output[0], *outputs])
+    ]
+    results = in_order(jnp.stack(returned)).astype(F32)
+    results = results.reshape(1, micro, images, block, width)
+    out_near = add_low(out_near, gate(out_moved)).astype(F32)
+    mine, other = out_near[0, :half_heads], out_near[1, :half_heads]
+    grad_out = jnp.concatenate([jnp.where(first, mine, other), jnp.where(first, other, mine)])
+
+    def own_part(rows, size):
+        return lax.dynamic_slice_in_dim(rows, line * size, size, rows.ndim - 1)
+
+    def halves_of(mine, other, size):
+        mine, other = own_part(mine, size), own_part(other, size)
+        low, high = jnp.where(first, mine, other), jnp.where(first, other, mine)
+        return jnp.concatenate([low, high], axis=-1)
+
+    mine, other = out_near[0, half_heads:], out_near[1, half_heads:]
+    shared = own_part(mine[:6], own_rows)
+    query = halves_of(mine[6, : width // 2], other[6, : width // 2], half_heads)
+    value = halves_of(mine[6, width // 2 :], other[6, width // 2 :], half_heads)
+    hidden = [rows[7:].reshape(-1)[:hidden_width] for rows in (mine, other)]
+    hidden = halves_of(*hidden, half_hidden)[:own_hidden]
+    grad_shifts = jnp.concatenate([shared[2:4], query[None], value[None], shared[4:6]])
 
     return (
         results,
         grad_in[None],
         grad_out[None],
         grad_expand[None],
-        grad_contract[None],
-        sums[: 2 * own_rows].reshape(1, 2, own_rows),
-        sums[2 * own_rows : 8 * own_rows].reshape(1, 6, own_rows),
-        sums[8 * own_rows : 8 * own_rows + own_hidden][None],
+        grad_contract.transpose(1, 0, 2),
+        shared[None, :2],
+        grad_shifts[None],
+        hidden[None],
     )
 
 
@@ -1444,7 +1436,10 @@
     def by_size(section_inputs, *others):
         _, micro, images, _, _ = section_inputs.shape
         one_image_each = micro * images == lax.axis_size("seq") == 4
-        plan = on_device if one_image_each else on_device_any
+        rows, hidden = others[2].shape[1], others[4].shape[1]
+        even = rows % (2 * HEAD_DIM) == 0 and rows % 32 == 0
+        even = even and round_up(round_up(hidden, 2) // 2, 16) % 32 == 0
+        plan = on_device if one_image_each and even else on_device_any
         return plan(section_inputs, *others)
 
     return jax.shard_map(

time: 916 us -> 826 us (0.902)
  Pallas kernels: 404 us -> 268 us
  local copies, waits for them, and re-layouts: 67.8 us -> 173 us
  waiting for transfers between devices: 274 us -> 178 us
  other arithmetic: 58.3 us -> 80.3 us
  starting transfers between devices: 87 us -> 96.2 us
    unnamed x136 -> x354, local copies, waits for them, and re-layouts: 25.2 us -> 130 us
    pallas_call x20, Pallas kernels: 172 us -> 99.4 us  [whole_call(): pl.pallas_call(kernel, out_shape=shapes, in_specs=whole_vmem(len(arrays))...]
    ppermute x60 -> x53, waiting for transfers between devices: 214 us -> 144 us  [swap_seq(): return lax.ppermute(value, ('section', 'seq'), pairs)]
    all_gather x2 -> x0, waiting for transfers between devices: 32.3 us -> none  [the longest x1 32.3 us: on_device(): out_0 = lax.all_gather(out_whole[0], 'dp', axis=0)]
    pallas_call x7 -> x6, Pallas kernels: 61.7 us -> 44 us  [grad_halves(): pl.pallas_call(kernel, out_shape=(shape, shape), grid_spec=pltpu.Prefetch...]
    pallas_call x6, Pallas kernels: 31.8 us -> 20.1 us  [assemble(): pl.pallas_call(kernel, out_shape=jax.ShapeDtypeStruct((count, 4, rows, co...]
    pallas_call x3, Pallas kernels: 57.3 us -> 46.7 us  [the longest x2 42 us: attention_backward(): pl.pallas_call(kernel, grid=(heads,), out_shape=(jax.ShapeDtypeStruct((le...]
    pallas_call x7 -> x6, Pallas kernels: 30.6 us -> 22.9 us  [add_half(): pl.pallas_call(kernel, out_shape=(shape, shape), grid_spec=pltpu.Prefetch...]
  transfers between devices with their start and end apart: 112 -> 98, of which waited for: 38 -> 32; matrix products, arithmetic and copies ran while one was open for 12% -> 14% of each run, Pallas kernels for 42% -> 32%
where the time goes in v2:
time: 826 us; the launch traced here: 812 us
  Pallas kernels  268 us (32%)
  waiting for transfers between devices  178 us (22%)
  local copies, waits for them, and re-layouts  173 us (21%)
  starting transfers between devices  96.2 us (12%)
  other arithmetic  80.3 us (10%)
  between operations  16.5 us (2%)
    ppermute x53, waiting for transfers between devices, swap_seq(): return lax.ppermute(value, ('section', 'seq'), pairs)  144 us
    unnamed x354, local copies, waits for them, and re-layouts  130 us
    pallas_call x20, Pallas kernels, whole_call(): pl.pallas_call(kernel, out_shape=shapes, in_specs=whole_vmem(len(arrays))...  99.4 us
    ppermute x53, starting transfers between devices, swap_seq(): return lax.ppermute(value, ('section', 'seq'), pairs)  72.1 us
    pallas_call x6, Pallas kernels, grad_halves(): pl.pallas_call(kernel, out_shape=(shape, shape), grid_spec=pltpu.Prefetch...  44 us
    pallas_call x2, Pallas kernels, attention_backward(): pl.pallas_call(kernel, grid=(heads,), out_shape=(jax.ShapeDtypeStruct((le...  42 us
    pallas_call x2, Pallas kernels, attention_forward(): pl.pallas_call(kernel, grid=(heads,), out_shape=(jax.ShapeDtypeStruct((le...  26.5 us
    pallas_call x6, Pallas kernels, add_half(): pl.pallas_call(kernel, out_shape=(shape, shape), grid_spec=pltpu.Prefetch...  22.9 us
  transfers between devices with their start and end apart: 98, of which 32 were waited for; matrix products, arithmetic and copies ran while one was open for 14% of the time, Pallas kernels for 32%

profile of v2, /device:TPU:0, one launch (start us, length us, event | category | flops | bytes accessed | tf_op | source)
XLA Modules:
  0.0 811.7 jit_solution(16042411682975213171)
XLA Ops:
  53.3 10.4 %collective-permute-done.7 = bf16[184,1152]{1,0:T(8,128)(2,1)S(1)} collective-permute-done((bf16[184,1152]{1,0:T(8,128)(2,1)}, bf16[184,1152]{1,0:T(8,128)(2,1)S(1)}, u32[]{:S(2)}, u32[]{:S(2)}) %collective-permute-start.7) | collective-permute-done | bytes 423968 | tf_op jit(solution)/shard_map/ppermute | solution.py:38
  75.2 13.7 %all-gather.9.cloned.1.call-done = bf16[288,2752]{1,0:T(8,128)(2,1)} async-done(((bf16[72,2752]{1,0:T(8,128)(2,1)}), bf16[288,2752]{1,0:T(8,128)(2,1)}) %all-gather.9.cloned.1.call-update) | async-done | bytes 1585168 | tf_op jit(solution)/shard_map/all_gather | solution.py:222
  98.6 31.0 %collective-permute-done.13.across_ref = bf16[3,72,1728]{2,1,0:T(8,128)(2,1)} collective-permute-done((bf16[3,72,1728]{2,1,0:T(8,128)(2,1)}, bf16[3,72,1728]{2,1,0:T(8,128)(2,1)}, u32[]{:S(2)}, u32[]{:S(2)}) %collective-permute-start.13) | collective-permute-done | bytes 746528 | tf_op jit(solution)/shard_map/ppermute | solution.py:38
  136.7 4.2 assemble.6
  140.9 4.5 project_in.2
  164.1 13.2 %attention_forward.2 = (bf16[736,576]{1,0:T(8,128)(2,1)S(1)}, f32[8,1,736]{2,1,0:T(1,128)S(1)}) custom-call(bf16[736,1728]{1,0:T(8,128)(2,1)S(1)} %copy-done.34, f32[736,1]{1,0:T(8,128)S(1)} %broadcast_select_fusion.10.hidden_ref), custom_call_target="tpu_custom_call" | custom-call | flops 1 | bytes 1 | tf_op jit(solution)/shard_map/attention_forward/pallas_call | solution.py:427
  197.8 11.8 %expand_hidden.2 = (f32[736,1152]{1,0:T(8,128)S(1)}, bf16[736,1152]{1,0:T(8,128)(2,1)S(1)}, bf16[736,2176]{1,0:T(8,128)(2,1)S(1)}, bf16[736,2176]{1,0:T(8,128)(2,1)S(1)}) custom-call(bf16[736,1152]{1,0:T(8,128)(2,1)S(1)} %broadcast_select_fusion.1.refs_0_.stream_ref.refs_5_, bf16[736,640]{1,0:T(8,128)(2,1)} %get-tuple-element.448.refs_0_, ...), custom_call_target="tpu_custom_call" | custom-call | flops 1 | bytes 1 | tf_op jit(solution)/shard_map/expand_hidden/pallas_call | solution.py:526
  218.7 5.6 collective-permute-done.25.across_ref
  232.2 6.0 collective-permute-done.28.across_ref
  241.3 5.6 contract_hidden.2
  266.6 7.2 project_in.3
  282.9 13.2 %attention_forward.3 = (bf16[736,576]{1,0:T(8,128)(2,1)S(1)}, f32[8,1,736]{2,1,0:T(1,128)S(1)}) custom-call(bf16[736,1728]{1,0:T(8,128)(2,1)S(1)} %get-tuple-element.485.qkv_ref, f32[736,1]{1,0:T(8,128)S(1)} %broadcast_select_fusion.10.hidden_ref), custom_call_target="tpu_custom_call" | custom-call | flops 1 | bytes 1 | tf_op jit(solution)/shard_map/attention_forward/pallas_call | solution.py:427
  298.0 6.6 collective-permute-done.35.across_ref
  327.6 4.4 collective-permute-done.40.refs_3_
  333.4 11.2 %expand_hidden.3 = (f32[736,1152]{1,0:T(8,128)S(1)}, bf16[736,1152]{1,0:T(8,128)(2,1)S(1)}, bf16[736,2176]{1,0:T(8,128)(2,1)S(1)}, bf16[736,2176]{1,0:T(8,128)(2,1)S(1)}) custom-call(bf16[736,1152]{1,0:T(8,128)(2,1)S(1)} %copy-done.41, bf16[736,640]{1,0:T(8,128)(2,1)} %get-tuple-element.502.refs_0_, bf16[736,512]{1,0:T(8,128)(2,1)} %get-tuple-element.503.refs_1_, ...), custom_call_target="tpu_custom_call" | custom-call | flops 1 | bytes 1 | tf_op jit(solution)/shard_map/expand_hidden/pallas_call | solution.py:526
  347.6 8.1 grad_halves.6
  359.9 4.6 back_hidden.2
  364.6 7.6 grad_halves.7
  373.2 4.6 back_expand.2
  379.1 4.5 contract_hidden.3
  386.4 4.5 add_half.6
  405.1 4.6 back_norm.4
  412.8 13.9 %collective-permute-done.46.moved_ref = bf16[4,2,72,2176]{3,2,1,0:T(8,128)(2,1)} collective-permute-done((bf16[4,2,72,2176]{3,2,1,0:T(8,128)(2,1)}, bf16[4,2,72,2176]{3,2,1,0:T(8,128)(2,1)}, u32[]{:S(2)}, u32[]{:S(2)}) %collective-permute-start.46) | collective-permute-done | bytes 2506784 | tf_op jit(solution)/shard_map/ppermute | solution.py:38
  431.3 20.9 %attention_backward.2 = (bf16[736,1728]{1,0:T(8,128)(2,1)S(1)}, f32[1,1728]{1,0:T(1,128)S(1)}) custom-call(bf16[736,1728]{1,0:T(8,128)(2,1)S(1)} %copy-done.37, bf16[736,576]{1,0:T(8,128)(2,1)S(1)} %get-tuple-element.559.do_ref, f32[8,1,736]{2,1,0:T(1,128)S(1)} %get-tuple-element.560.lse_ref, f32[736,1]{1,0:T(8,128)S(1)} %copy-done.39), custom_call_target="tpu_custom_call" | custom-call | flops 1 | bytes 1 | tf_op jit(solution)/shard_map/attention_backward/pallas_call | solution.py:488
  462.0 6.8 grad_halves.8
  470.7 6.2 collective-permute-done.47
  482.5 4.6 back_in.2
  495.6 5.3 back_norm.5
  501.0 4.4 add_half.8
  508.7 4.9 add_convert_fusion
  515.5 8.2 %grad_halves.9 = (bf16[4,2,136,1152]{3,2,1,0:T(8,128)(2,1)S(1)}, bf16[4,2,136,1152]{3,2,1,0:T(8,128)(2,1)}) custom-call(s32[3]{0:T(128)S(1)} %pad_add_fusion.bits_ref, bf16[736,2176]{1,0:T(8,128)(2,1)S(1)} %copy-done.19, bf16[736,1152]{1,0:T(8,128)(2,1)S(1)} %copy-done.10), custom_call_target="tpu_custom_call" | custom-call | flops 1 | bytes 1 | tf_op jit(solution)/shard_map/grad_halves/pallas_call | solution.py:280
  525.4 4.6 back_hidden.3
  537.9 6.8 grad_halves.10
  552.4 4.6 back_expand.3
  574.7 6.4 back_norm.6
  592.8 21.1 %attention_backward.3 = (bf16[736,1728]{1,0:T(8,128)(2,1)S(1)}, f32[1,1728]{1,0:T(1,128)S(1)}) custom-call(bf16[736,1728]{1,0:T(8,128)(2,1)S(1)} %copy-done.35, bf16[736,576]{1,0:T(8,128)(2,1)S(1)} %copy-done.108, f32[8,1,736]{2,1,0:T(1,128)S(1)} %get-tuple-element.665.lse_ref, f32[736,1]{1,0:T(8,128)S(1)} %copy-done.39), custom_call_target="tpu_custom_call" | custom-call | flops 1 | bytes 1 | tf_op jit(solution)/shard_map/attention_backward/pallas_call | solution.py:488
  626.5 6.4 grad_halves.11
  641.8 4.7 collective-permute-start.63
  665.4 9.0 %collective-permute-done.66.moved_ref = bf16[4,2,72,1728]{3,2,1,0:T(8,128)(2,1)} collective-permute-done((bf16[4,2,72,1728]{3,2,1,0:T(8,128)(2,1)}, bf16[4,2,72,1728]{3,2,1,0:T(8,128)(2,1)}, u32[]{:S(2)}, u32[]{:S(2)}) %collective-permute-start.66) | collective-permute-done | bytes 1990688 | tf_op jit(solution)/shard_map/ppermute | solution.py:38
  686.1 8.9 %collective-permute-done.68 = bf16[4,72,1728]{2,1,0:T(8,128)(2,1)} collective-permute-done((bf16[4,72,1728]{2,1,0:T(8,128)(2,1)}, bf16[4,72,1728]{2,1,0:T(8,128)(2,1)}, u32[]{:S(2)}, u32[]{:S(2)}) %collective-permute-start.68) | collective-permute-done | bytes 995360 | tf_op jit(solution)/shard_map/ppermute | solution.py:38
  713.1 4.5 collective-permute-start.77
  719.5 4.5 collective-permute-done.71
  734.2 4.7 join_rows.1
  738.9 4.2 collective-permute-done.76
  749.1 9.4 %collective-permute-done.81 = bf16[2,72,2176]{2,1,0:T(8,128)(2,1)S(1)} collective-permute-done((bf16[2,72,2176]{2,1,0:T(8,128)(2,1)}, bf16[2,72,2176]{2,1,0:T(8,128)(2,1)S(1)}, u32[]{:S(2)}, u32[]{:S(2)}) %collective-permute-start.81) | collective-permute-done | bytes 626720 | tf_op jit(solution)/shard_map/ppermute | solution.py:38
  759.5 4.5 collective-permute-done.79
  782.5 5.3 collective-permute-done.84
  793.2 7.5 collective-permute-done.85
  (744 shorter events, 415.6 us)
Async XLA Ops:
  7.2 81.7 %all-gather.9.cloned.1.call-start = ((), (), s32[]{:S(2)}) async-start(), calls=%async_computation.12 | async-start | bytes 2027520 | tf_op jit(solution)/shard_map/all_gather | solution.py:222
  19.2 30.1 %collective-permute-start.4 = (bf16[80,1728]{1,0:T(8,128)(2,1)}, bf16[80,1728]{1,0:T(8,128)(2,1)}, u32[]{:S(2)}, u32[]{:S(2)}) collective-permute-start(bf16[80,1728]{1,0:T(8,128)(2,1)} %pad_maximum_fusion.15), channel_id=1, source_target_pairs={{3,0},{0,1},{1,2},{2,3},{7,4},{4,5},{5,6},{6,7},{11,8},{8,9},{9,10... | collective-permute-start | bytes 829448 | tf_op jit(solution)/shard_map/ppermute | solution.py:215
  22.2 31.1 %collective-permute-start.3 = (bf16[80,1728]{1,0:T(8,128)(2,1)}, bf16[80,1728]{1,0:T(8,128)(2,1)}, u32[]{:S(2)}, u32[]{:S(2)}) collective-permute-start(bf16[80,1728]{1,0:T(8,128)(2,1)} %pad_maximum_fusion.15), channel_id=1, source_target_pairs={{2,0},{3,1},{0,2},{1,3},{6,4},{7,5},{4,6},{5,7},{10,8},{11,9},{8,1... | collective-permute-start | bytes 829448 | tf_op jit(solution)/shard_map/ppermute | solution.py:215
  24.8 28.5 %collective-permute-start.2 = (bf16[80,1728]{1,0:T(8,128)(2,1)}, bf16[80,1728]{1,0:T(8,128)(2,1)}, u32[]{:S(2)}, u32[]{:S(2)}) collective-permute-start(bf16[80,1728]{1,0:T(8,128)(2,1)} %pad_maximum_fusion.15), channel_id=1, source_target_pairs={{1,0},{2,1},{3,2},{0,3},{5,4},{6,5},{7,6},{4,7},{9,8},{10,9},{11,1... | collective-permute-start | bytes 829448 | tf_op jit(solution)/shard_map/ppermute | solution.py:215
  52.5 107.3 %all-gather.11.cloned.1.call-start = ((), (), s32[]{:S(2)}) async-start(), calls=%async_computation.13 | async-start | bytes 1566720 | tf_op jit(solution)/shard_map/all_gather | solution.py:222
  69.0 22.6 %collective-permute-start.12 = (bf16[3,72,1728]{2,1,0:T(8,128)(2,1)S(1)}, bf16[3,72,1728]{2,1,0:T(8,128)(2,1)}, u32[]{:S(2)}, u32[]{:S(2)}) collective-permute-start(bf16[3,72,1728]{2,1,0:T(8,128)(2,1)S(1)} %pad_maximum_fusion.9.near_ref), channel_id=1, source_target_pairs={{0,8},{4,12},{8,0},{12,4},{16,20},{20,16},{24,28},{28,24},{1,9},{5... | collective-permute-start | bytes 2239496 | tf_op jit(solution)/shard_map/ppermute | solution.py:38
  74.3 22.4 %collective-permute-start.14 = (bf16[736,1152]{1,0:T(8,128)(2,1)}, bf16[736,1152]{1,0:T(8,128)(2,1)}, u32[]{:S(2)}, u32[]{:S(2)}) collective-permute-start(bf16[736,1152]{1,0:T(8,128)(2,1)} %constant_dynamic-update-slice_fusion), channel_id=1, source_target_pairs={{0,16},{16,0},{1,17},{17,1},{2,18},{18,2},{3,19},{19,3},{4,20},{20... | collective-permute-start | bytes 5087240 | tf_op jit(solution)/shard_map/ppermute | solution.py:26
  74.3 141.6 %all-gather.13.cloned.1.call-start = ((), (), s32[]{:S(2)}) async-start(), calls=%async_computation.14 | async-start | bytes 2027520 | tf_op jit(solution)/shard_map/all_gather | solution.py:222
  92.5 58.7 %collective-permute-start.16 = (bf16[3,72,2752]{2,1,0:T(8,128)(2,1)}, bf16[3,72,2752]{2,1,0:T(8,128)(2,1)}, u32[]{:S(2)}, u32[]{:S(2)}) collective-permute-start(bf16[3,72,2752]{2,1,0:T(8,128)(2,1)} %fusion.1.near_ref), channel_id=1, source_target_pairs={{0,8},{4,12},{8,0},{12,4},{16,20},{20,16},{24,28},{28,24},{1,9},{5... | collective-permute-start | bytes 3566600 | tf_op jit(solution)/shard_map/ppermute | solution.py:38
  94.0 57.2 %collective-permute-start.15 = (bf16[3,72,2752]{2,1,0:T(8,128)(2,1)}, bf16[3,72,2752]{2,1,0:T(8,128)(2,1)}, u32[]{:S(2)}, u32[]{:S(2)}) collective-permute-start(bf16[3,72,2752]{2,1,0:T(8,128)(2,1)} %fusion.1.near_ref), channel_id=1, source_target_pairs={{0,4},{4,0},{8,12},{12,8},{16,24},{20,28},{24,16},{28,20},{1,5},{5... | collective-permute-start | bytes 3566600 | tf_op jit(solution)/shard_map/ppermute | solution.py:38
  95.8 33.8 %collective-permute-start.13 = (bf16[3,72,1728]{2,1,0:T(8,128)(2,1)}, bf16[3,72,1728]{2,1,0:T(8,128)(2,1)}, u32[]{:S(2)}, u32[]{:S(2)}) collective-permute-start(bf16[3,72,1728]{2,1,0:T(8,128)(2,1)} %collective-permute-done.12.second_ref), channel_id=1, source_target_pairs={{0,4},{4,0},{8,12},{12,8},{16,24},{20,28},{24,16},{28,20},{1,5},{5... | collective-permute-start | bytes 2239496 | tf_op jit(solution)/shard_map/ppermute | solution.py:38
  151.3 108.7 %all-gather.15.cloned.1.call-start = ((), (), s32[]{:S(2)}) async-start(), calls=%async_computation.15 | async-start | bytes 1566720 | tf_op jit(solution)/shard_map/all_gather | solution.py:222
  151.3 27.0 %collective-permute-start.20 = (bf16[3,72,2752]{2,1,0:T(8,128)(2,1)}, bf16[3,72,2752]{2,1,0:T(8,128)(2,1)S(1)}, u32[]{:S(2)}, u32[]{:S(2)}) collective-permute-start(bf16[3,72,2752]{2,1,0:T(8,128)(2,1)} %collective-permute-done.16.second_ref), channel_id=1, source_target_pairs={{0,4},{4,0},{8,12},{12,8},{16,24},{20,28},{24,16},{28,20},{1,5},{5... | collective-permute-start | bytes 3566600 | tf_op jit(solution)/shard_map/ppermute | solution.py:38
  154.9 37.4 %collective-permute-start.22 = (bf16[3,72,1728]{2,1,0:T(8,128)(2,1)}, bf16[3,72,1728]{2,1,0:T(8,128)(2,1)}, u32[]{:S(2)}, u32[]{:S(2)}) collective-permute-start(bf16[3,72,1728]{2,1,0:T(8,128)(2,1)} %pad_maximum_fusion.10.near_ref), channel_id=1, source_target_pairs={{0,8},{4,12},{8,0},{12,4},{16,20},{20,16},{24,28},{28,24},{1,9},{5... | collective-permute-start | bytes 2239496 | tf_op jit(solution)/shard_map/ppermute | solution.py:38
  156.4 35.9 %collective-permute-start.21 = (bf16[3,72,1728]{2,1,0:T(8,128)(2,1)}, bf16[3,72,1728]{2,1,0:T(8,128)(2,1)}, u32[]{:S(2)}, u32[]{:S(2)}) collective-permute-start(bf16[3,72,1728]{2,1,0:T(8,128)(2,1)} %pad_maximum_fusion.10.near_ref), channel_id=1, source_target_pairs={{0,4},{4,0},{8,12},{12,8},{16,24},{20,28},{24,16},{28,20},{1,5},{5... | collective-permute-start | bytes 2239496 | tf_op jit(solution)/shard_map/ppermute | solution.py:38
  192.8 31.4 %collective-permute-start.27 = (bf16[3,136,1152]{2,1,0:T(8,128)(2,1)}, bf16[3,136,1152]{2,1,0:T(8,128)(2,1)}, u32[]{:S(2)}, u32[]{:S(2)}) collective-permute-start(bf16[3,136,1152]{2,1,0:T(8,128)(2,1)} %fusion.3.near_ref), channel_id=1, source_target_pairs={{0,8},{4,12},{8,0},{12,4},{16,20},{20,16},{24,28},{28,24},{1,9},{5... | collective-permute-start | bytes 2820104 | tf_op jit(solution)/shard_map/ppermute | solution.py:38
  193.4 30.8 %collective-permute-start.26 = (bf16[3,136,1152]{2,1,0:T(8,128)(2,1)}, bf16[3,136,1152]{2,1,0:T(8,128)(2,1)}, u32[]{:S(2)}, u32[]{:S(2)}) collective-permute-start(bf16[3,136,1152]{2,1,0:T(8,128)(2,1)} %fusion.3.near_ref), channel_id=1, source_target_pairs={{0,4},{4,0},{8,12},{12,8},{16,24},{20,28},{24,16},{28,20},{1,5},{5... | collective-permute-start | bytes 2820104 | tf_op jit(solution)/shard_map/ppermute | solution.py:38
  194.8 29.5 %collective-permute-start.25 = (bf16[3,72,1728]{2,1,0:T(8,128)(2,1)}, bf16[3,72,1728]{2,1,0:T(8,128)(2,1)}, u32[]{:S(2)}, u32[]{:S(2)}) collective-permute-start(bf16[3,72,1728]{2,1,0:T(8,128)(2,1)} %collective-permute-done.22.second_ref), channel_id=1, source_target_pairs={{0,4},{4,0},{8,12},{12,8},{16,24},{20,28},{24,16},{28,20},{1,5},{5... | collective-permute-start | bytes 2239496 | tf_op jit(solution)/shard_map/ppermute | solution.py:38
  225.6 322.0 %reduce-scatter.25.cloned.1.call-start = ((), (), s32[]{:S(2)}) async-start(), calls=%async_computation.16 | async-start | bytes 1566720
  247.5 29.6 %collective-permute-start.32 = (bf16[3,72,2752]{2,1,0:T(8,128)(2,1)S(1)}, bf16[3,72,2752]{2,1,0:T(8,128)(2,1)}, u32[]{:S(2)}, u32[]{:S(2)}) collective-permute-start(bf16[3,72,2752]{2,1,0:T(8,128)(2,1)S(1)} %copy-done.55), channel_id=1, source_target_pairs={{0,8},{4,12},{8,0},{12,4},{16,20},{20,16},{24,28},{28,24},{1,9},{5... | collective-permute-start | bytes 3566600 | tf_op jit(solution)/shard_map/ppermute | solution.py:38
  248.0 29.8 %collective-permute-start.31 = (bf16[3,72,2752]{2,1,0:T(8,128)(2,1)S(1)}, bf16[3,72,2752]{2,1,0:T(8,128)(2,1)}, u32[]{:S(2)}, u32[]{:S(2)}) collective-permute-start(bf16[3,72,2752]{2,1,0:T(8,128)(2,1)S(1)} %copy-done.55), channel_id=1, source_target_pairs={{0,4},{4,0},{8,12},{12,8},{16,24},{20,28},{24,16},{28,20},{1,5},{5... | collective-permute-start | bytes 3566600 | tf_op jit(solution)/shard_map/ppermute | solution.py:38
  250.9 27.0 %collective-permute-start.33 = (bf16[184,1152]{1,0:T(8,128)(2,1)}, bf16[184,1152]{1,0:T(8,128)(2,1)}, u32[]{:S(2)}, u32[]{:S(2)}) collective-permute-start(bf16[184,1152]{1,0:T(8,128)(2,1)} %get-tuple-element.480), channel_id=1, source_target_pairs={{16,20},{20,16},{24,28},{28,24},{17,21},{21,17},{25,29},{29,25},{1... | collective-permute-start | bytes 1271816 | tf_op jit(solution)/shard_map/ppermute | solution.py:38
  252.3 25.6 %collective-permute-start.34 = (bf16[184,1152]{1,0:T(8,128)(2,1)}, bf16[184,1152]{1,0:T(8,128)(2,1)}, u32[]{:S(2)}, u32[]{:S(2)}) collective-permute-start(bf16[184,1152]{1,0:T(8,128)(2,1)} %get-tuple-element.481), channel_id=1, source_target_pairs={{16,24},{20,28},{24,16},{28,20},{17,25},{21,29},{25,17},{29,21},{1... | collective-permute-start | bytes 1271816 | tf_op jit(solution)/shard_map/ppermute | solution.py:38
  277.9 26.7 %collective-permute-start.35 = (bf16[3,72,2752]{2,1,0:T(8,128)(2,1)}, bf16[3,72,2752]{2,1,0:T(8,128)(2,1)S(1)}, u32[]{:S(2)}, u32[]{:S(2)}) collective-permute-start(bf16[3,72,2752]{2,1,0:T(8,128)(2,1)} %collective-permute-done.32.second_ref), channel_id=1, source_target_pairs={{0,4},{4,0},{8,12},{12,8},{16,24},{20,28},{24,16},{28,20},{1,5},{5... | collective-permute-start | bytes 3566600 | tf_op jit(solution)/shard_map/ppermute | solution.py:38
  279.3 39.4 %collective-permute-start.37 = (bf16[3,136,1152]{2,1,0:T(8,128)(2,1)}, bf16[3,136,1152]{2,1,0:T(8,128)(2,1)}, u32[]{:S(2)}, u32[]{:S(2)}) collective-permute-start(bf16[3,136,1152]{2,1,0:T(8,128)(2,1)} %fusion.2.near_ref), channel_id=1, source_target_pairs={{0,8},{4,12},{8,0},{12,4},{16,20},{20,16},{24,28},{28,24},{1,9},{5... | collective-permute-start | bytes 2820104 | tf_op jit(solution)/shard_map/ppermute | solution.py:38
  280.7 38.8 %collective-permute-start.36 = (bf16[3,136,1152]{2,1,0:T(8,128)(2,1)}, bf16[3,136,1152]{2,1,0:T(8,128)(2,1)}, u32[]{:S(2)}, u32[]{:S(2)}) collective-permute-start(bf16[3,136,1152]{2,1,0:T(8,128)(2,1)} %fusion.2.near_ref), channel_id=1, source_target_pairs={{0,4},{4,0},{8,12},{12,8},{16,24},{20,28},{24,16},{28,20},{1,5},{5... | collective-permute-start | bytes 2820104 | tf_op jit(solution)/shard_map/ppermute | solution.py:38
  281.3 37.3 %collective-permute-start.38 = (bf16[184,1152]{1,0:T(8,128)(2,1)}, bf16[184,1152]{1,0:T(8,128)(2,1)}, u32[]{:S(2)}, u32[]{:S(2)}) collective-permute-start(bf16[184,1152]{1,0:T(8,128)(2,1)} %get-tuple-element.497), channel_id=1, source_target_pairs={{16,28},{20,24},{24,20},{28,16},{17,29},{21,25},{25,21},{29,17},{1... | collective-permute-start | bytes 1271816 | tf_op jit(solution)/shard_map/ppermute | solution.py:38
  355.7 30.7 %collective-permute-start.45 = (bf16[4,2,136,1152]{3,2,1,0:T(8,128)(2,1)}, bf16[4,2,136,1152]{3,2,1,0:T(8,128)(2,1)}, u32[]{:S(2)}, u32[]{:S(2)}) collective-permute-start(bf16[4,2,136,1152]{3,2,1,0:T(8,128)(2,1)} %get-tuple-element.535), channel_id=1, source_target_pairs={{0,4},{4,0},{8,12},{12,8},{16,24},{20,28},{24,16},{28,20},{1,5},{5... | collective-permute-start | bytes 7520264 | tf_op jit(solution)/shard_map/ppermute | solution.py:38
  372.1 54.6 %collective-permute-start.46 = (bf16[4,2,72,2176]{3,2,1,0:T(8,128)(2,1)}, bf16[4,2,72,2176]{3,2,1,0:T(8,128)(2,1)}, u32[]{:S(2)}, u32[]{:S(2)}) collective-permute-start(bf16[4,2,72,2176]{3,2,1,0:T(8,128)(2,1)} %get-tuple-element.553), channel_id=1, source_target_pairs={{0,4},{4,0},{8,12},{12,8},{16,24},{20,28},{24,16},{28,20},{1,5},{5... | collective-permute-start | bytes 7520264 | tf_op jit(solution)/shard_map/ppermute | solution.py:38
  393.9 59.8 %collective-permute-start.48 = (bf16[4,136,1152]{2,1,0:T(8,128)(2,1)}, bf16[4,136,1152]{2,1,0:T(8,128)(2,1)}, u32[]{:S(2)}, u32[]{:S(2)}) collective-permute-start(bf16[4,136,1152]{2,1,0:T(8,128)(2,1)} %get-tuple-element.569), channel_id=1, source_target_pairs={{0,8},{4,12},{8,0},{12,4},{16,20},{20,16},{24,28},{28,24},{1,9},{5... | collective-permute-start | bytes 3760136 | tf_op jit(solution)/shard_map/ppermute | solution.py:38
  456.4 129.8 %reduce-scatter.27.cloned.1.call-start = ((), (), s32[]{:S(2)}) async-start(), calls=%async_computation.17 | async-start | bytes 1566720
  470.1 30.8 %collective-permute-start.53 = (bf16[4,2,72,1728]{3,2,1,0:T(8,128)(2,1)}, bf16[4,2,72,1728]{3,2,1,0:T(8,128)(2,1)}, u32[]{:S(2)}, u32[]{:S(2)}) collective-permute-start(bf16[4,2,72,1728]{3,2,1,0:T(8,128)(2,1)} %get-tuple-element.598), channel_id=1, source_target_pairs={{0,4},{4,0},{8,12},{12,8},{16,24},{20,28},{24,16},{28,20},{1,5},{5... | collective-permute-start | bytes 5971976 | tf_op jit(solution)/shard_map/ppermute | solution.py:38
  478.3 156.0 %reduce-scatter.17.cloned.1.call-start = ((), (), s32[]{:S(2)}) async-start(), calls=%async_computation.8 | async-start | bytes 1290240 | tf_op jit(solution)/shard_map/reduce_scatter | solution.py:343
  506.3 25.3 %collective-permute-start.54 = (bf16[4,72,1728]{2,1,0:T(8,128)(2,1)}, bf16[4,72,1728]{2,1,0:T(8,128)(2,1)}, u32[]{:S(2)}, u32[]{:S(2)}) collective-permute-start(bf16[4,72,1728]{2,1,0:T(8,128)(2,1)} %get-tuple-element.618), channel_id=1, source_target_pairs={{0,8},{4,12},{8,0},{12,4},{16,20},{20,16},{24,28},{28,24},{1,9},{5... | collective-permute-start | bytes 2985992 | tf_op jit(solution)/shard_map/ppermute | solution.py:38
  531.7 33.4 %collective-permute-start.57 = (bf16[4,2,136,1152]{3,2,1,0:T(8,128)(2,1)}, bf16[4,2,136,1152]{3,2,1,0:T(8,128)(2,1)}, u32[]{:S(2)}, u32[]{:S(2)}) collective-permute-start(bf16[4,2,136,1152]{3,2,1,0:T(8,128)(2,1)} %get-tuple-element.634), channel_id=1, source_target_pairs={{0,4},{4,0},{8,12},{12,8},{16,24},{20,28},{24,16},{28,20},{1,5},{5... | collective-permute-start | bytes 7520264 | tf_op jit(solution)/shard_map/ppermute | solution.py:38
  534.2 131.2 %reduce-scatter.19.cloned.1.call-start = ((), (), s32[]{:S(2)}) async-start(), calls=%async_computation.9 | async-start | bytes 1843200 | tf_op jit(solution)/shard_map/reduce_scatter | solution.py:905
  560.4 55.0 %collective-permute-start.59 = (bf16[4,2,72,2176]{3,2,1,0:T(8,128)(2,1)}, bf16[4,2,72,2176]{3,2,1,0:T(8,128)(2,1)}, u32[]{:S(2)}, u32[]{:S(2)}) collective-permute-start(bf16[4,2,72,2176]{3,2,1,0:T(8,128)(2,1)} %copy-done.125), channel_id=1, source_target_pairs={{0,4},{4,0},{8,12},{12,8},{16,24},{20,28},{24,16},{28,20},{1,5},{5... | collective-permute-start | bytes 7520264 | tf_op jit(solution)/shard_map/ppermute | solution.py:38
  586.3 93.7 %reduce-scatter.29.cloned.1.call-start = ((), (), s32[]{:S(2)}) async-start(), calls=%async_computation.18 | async-start | bytes 1566720
  586.3 34.9 %collective-permute-start.58 = (bf16[4,136,1152]{2,1,0:T(8,128)(2,1)}, bf16[4,136,1152]{2,1,0:T(8,128)(2,1)S(1)}, u32[]{:S(2)}, u32[]{:S(2)}) collective-permute-start(bf16[4,136,1152]{2,1,0:T(8,128)(2,1)} %copy-done.126), channel_id=1, source_target_pairs={{0,8},{4,12},{8,0},{12,4},{16,20},{20,16},{24,28},{28,24},{1,9},{5... | collective-permute-start | bytes 3760136 | tf_op jit(solution)/shard_map/ppermute | solution.py:38
  587.7 27.7 %collective-permute-start.62 = (bf16[184,1152]{1,0:T(8,128)(2,1)S(1)}, bf16[184,1152]{1,0:T(8,128)(2,1)S(1)}, u32[]{:S(2)}, u32[]{:S(2)}) collective-permute-start(bf16[184,1152]{1,0:T(8,128)(2,1)S(1)} %get-tuple-element.810), channel_id=1, source_target_pairs={{16,28},{20,24},{24,20},{28,16},{17,29},{21,25},{25,21},{29,17},{1... | collective-permute-start | bytes 1271816 | tf_op jit(solution)/shard_map/ppermute | solution.py:38
  588.4 27.0 %collective-permute-start.61 = (bf16[184,1152]{1,0:T(8,128)(2,1)S(1)}, bf16[184,1152]{1,0:T(8,128)(2,1)S(1)}, u32[]{:S(2)}, u32[]{:S(2)}) collective-permute-start(bf16[184,1152]{1,0:T(8,128)(2,1)S(1)} %get-tuple-element.811), channel_id=1, source_target_pairs={{16,24},{20,28},{24,16},{28,20},{17,25},{21,29},{25,17},{29,21},{1... | collective-permute-start | bytes 1271816 | tf_op jit(solution)/shard_map/ppermute | solution.py:38
  589.1 26.3 %collective-permute-start.60 = (bf16[184,1152]{1,0:T(8,128)(2,1)S(1)}, bf16[184,1152]{1,0:T(8,128)(2,1)S(1)}, u32[]{:S(2)}, u32[]{:S(2)}) collective-permute-start(bf16[184,1152]{1,0:T(8,128)(2,1)S(1)} %get-tuple-element.812), channel_id=1, source_target_pairs={{16,20},{20,16},{24,28},{28,24},{17,21},{21,17},{25,29},{29,25},{1... | collective-permute-start | bytes 1271816 | tf_op jit(solution)/shard_map/ppermute | solution.py:38
  622.6 77.7 %reduce-scatter.31.cloned.1.call-start = ((), (), s32[]{:S(2)}) async-start(), calls=%async_computation.19 | async-start | bytes 1566720
  622.7 28.9 %collective-permute-start.65 = (bf16[4,72,2176]{2,1,0:T(8,128)(2,1)}, bf16[4,72,2176]{2,1,0:T(8,128)(2,1)}, u32[]{:S(2)}, u32[]{:S(2)}) collective-permute-start(bf16[4,72,2176]{2,1,0:T(8,128)(2,1)} %copy-done.127), channel_id=1, source_target_pairs={{0,8},{4,12},{8,0},{12,4},{16,20},{20,16},{24,28},{28,24},{1,9},{5... | collective-permute-start | bytes 3760136 | tf_op jit(solution)/shard_map/ppermute | solution.py:38
  648.4 26.0 %collective-permute-start.66 = (bf16[4,2,72,1728]{3,2,1,0:T(8,128)(2,1)}, bf16[4,2,72,1728]{3,2,1,0:T(8,128)(2,1)}, u32[]{:S(2)}, u32[]{:S(2)}) collective-permute-start(bf16[4,2,72,1728]{3,2,1,0:T(8,128)(2,1)} %get-tuple-element.715), channel_id=1, source_target_pairs={{0,4},{4,0},{8,12},{12,8},{16,24},{20,28},{24,16},{28,20},{1,5},{5... | collective-permute-start | bytes 5971976 | tf_op jit(solution)/shard_map/ppermute | solution.py:38
  654.3 76.3 %reduce-scatter.21.cloned.1.call-start = ((), (), s32[]{:S(2)}) async-start(), calls=%async_computation.10 | async-start | bytes 1290240 | tf_op jit(solution)/shard_map/reduce_scatter | solution.py:343
  700.4 72.9 %reduce-scatter.23.cloned.1.call-start = ((), (), s32[]{:S(2)}) async-start(), calls=%async_computation.11 | async-start | bytes 1843200 | tf_op jit(solution)/shard_map/reduce_scatter | solution.py:905
  713.1 25.9 %collective-permute-start.77 = (bf16[184,1152]{1,0:T(8,128)(2,1)S(1)}, bf16[184,1152]{1,0:T(8,128)(2,1)}, u32[]{:S(2)}, u32[]{:S(2)}) collective-permute-start(bf16[184,1152]{1,0:T(8,128)(2,1)S(1)} %copy-done.150), channel_id=1, source_target_pairs={{0,12},{4,8},{8,4},{12,0},{1,13},{5,9},{9,5},{13,1},{2,14},{6,10},... | collective-permute-start | bytes 1271816 | tf_op jit(solution)/shard_map/ppermute | solution.py:38
  (223 other events, 1787.9 us)
Sparse Core Ops, SparseCore 0:
  52.6 36.2 all-gather.8
  90.4 30.5 all-gather.10
  151.4 41.1 all-gather.12
  225.7 34.1 all-gather.14
  456.5 34.4 reduce-scatter.24
  493.2 29.1 reduce-scatter.26
  534.3 30.6 reduce-scatter.16
  586.4 36.8 reduce-scatter.18
  625.6 37.2 reduce-scatter.28
  665.7 29.1 reduce-scatter.30
  700.5 29.9 reduce-scatter.20
  733.4 33.0 reduce-scatter.22

commit v3 on v2

--- a/solution.py
+++ b/solution.py
@@ -101,76 +101,78 @@
     )(core, weight)
 
 
-def join_columns(mine, other, runs, total, place):
-    count, rows, width = mine.shape
-
-    def kernel(place_ref, mine_ref, other_ref, out_ref):
-        def write(first, second):
-            for ref, pieces in ((first, runs[0]), (second, runs[1])):
-                for start, size, at in pieces:
-                    out_ref[0, :, start : start + size] = ref[0, :, at : at + size].astype(F32)
-
-        @pl.when(place_ref[0] == 0)
-        def _():
-            write(mine_ref, other_ref)
-
-        @pl.when(place_ref[0] == 1)
-        def _():
-            write(other_ref, mine_ref)
-
-    block = pl.BlockSpec((1, rows, width), lambda j, place: (j, 0, 0))
+def join_columns(pieces, runs, total, place):
+    count = len(pieces)
+    _, rows, width = pieces[0].shape
+
+    def kernel(place_ref, *refs):
+        out_ref = refs[count]
+
+        def write(piece_ref, halves):
+            for half, parts in zip(halves, runs):
+                for start, size, at in parts:
+                    value = piece_ref[half, :, at : at + size]
+                    out_ref[0, :, start : start + size] = value.astype(F32)
+
+        for index in range(count):
+            for core, halves in enumerate(((0, 1), (1, 0))):
+
+                @pl.when(jnp.logical_and(pl.program_id(0) == index, place_ref[0] == core))
+                def _(index=index, halves=halves):
+                    write(refs[index], halves)
+
+    whole = pl.BlockSpec((2, rows, width), lambda j, place: (0, 0, 0))
     out = pl.pallas_call(
         kernel,
         out_shape=jax.ShapeDtypeStruct((count, rows, total), F32),
         grid_spec=pltpu.PrefetchScalarGridSpec(
             num_scalar_prefetch=1,
             grid=(count,),
-            in_specs=[block, block],
+            in_specs=[whole] * count,
             out_specs=pl.BlockSpec((1, rows, total), lambda j, place: (place[1 + j], 0, 0)),
         ),
         compiler_params=params_of(),
         cost_estimate=LIGHT,
         name="join_columns",
-    )(place, mine, other)
+    )(place, *pieces)
     return out.reshape(count * rows, total)
 
 
-def join_rows(mine, other, total, place):
-    count, rows, width = mine.shape
-
-    def kernel(place_ref, mine_ref, other_ref, out_ref):
-        half = pl.program_id(0) // count
-
-        @pl.when(half == place_ref[0])
-        def _():
-            out_ref[:, 0, :] = mine_ref[0].astype(F32)
-
-        @pl.when(half != place_ref[0])
-        def _():
-            out_ref[:, 0, :] = other_ref[0].astype(F32)
-
-    def quarter(step):
-        return lax.rem(step, count)
-
+def join_rows(pieces, total, place):
+    count = len(pieces)
+    _, rows, width = pieces[0].shape
+
+    def kernel(place_ref, *refs):
+        out_ref = refs[count]
+        half, step = pl.program_id(0) // count, lax.rem(pl.program_id(0), count)
+        which = jnp.where(half == place_ref[0], 0, 1)
+        for index in range(count):
+
+            @pl.when(step == index)
+            def _(index=index):
+                out_ref[:, 0, :] = refs[index][which].astype(F32)
+
+    whole = pl.BlockSpec((2, rows, width), lambda t, place: (0, 0, 0))
     return pl.pallas_call(
         kernel,
         out_shape=jax.ShapeDtypeStruct((total, 1, width), F32),
         grid_spec=pltpu.PrefetchScalarGridSpec(
             num_scalar_prefetch=1,
             grid=(2 * count,),
-            in_specs=[
-                pl.BlockSpec((1, rows, width), lambda t, place: (quarter(t), 0, 0)),
-                pl.BlockSpec((1, rows, width), lambda t, place: (quarter(t), 0, 0)),
-            ],
+            in_specs=[whole] * count,
             out_specs=pl.BlockSpec(
                 (rows, 1, width),
-                lambda t, place: (lax.div(t, count) * count + place[1 + quarter(t)], 0, 0),
+                lambda t, place: (
+                    lax.div(t, count) * count + place[1 + lax.rem(t, count)],
+                    0,
+                    0,
+                ),
             ),
         ),
         compiler_params=params_of(),
         cost_estimate=LIGHT,
         name="join_rows",
-    )(place, mine, other)
+    )(place, *pieces)
 
 
 def assemble(own, near, first, second, across):
@@ -911,12 +913,10 @@
         return jnp.stack([gate.token, *(here ^ bits for bits in relative_bits())]).astype(jnp.int32)
 
     def rows_of(pieces, total):
-        mine, other = jnp.stack(pieces, axis=1)
-        return join_rows(mine, other, total, last_place())
+        return join_rows(pieces, total, last_place())
 
     def columns_of(pieces, runs, total):
-        mine, other = jnp.stack(pieces, axis=1)
-        return join_columns(mine, other, runs, total, last_place())
+        return join_columns(pieces, runs, total, last_place())
 
     contract_sum_1 = Sum(hidden_1, cotangent, count)
     gate.sent(contract_sum_1)
@@ -940,41 +940,41 @@
         cotangent, own, other, middle_1, vectors_1[1:2], attn_out_1
     )
     d_branch_1, d_mixed_1 = gate(d_branch_1, d_mixed_1)
-    out_grad_1 = plain_grad(mixed_1, d_branch_1)
+    out_grad_1 = gate(plain_grad(mixed_1, d_branch_1))
+    d_qkv_1, qkv_sums_1 = gate(attention_backward(qkv_1, gate(d_mixed_1), lse_1, hidden_keys))
+    gate.arrived(contract_sum_1)
+    contract_sum_1.over_line(gate)
     gate.arrived(expand_sum_1)
     expand_sum_1.add()
     gate.sent(expand_sum_1)
     expand_sum_1.second()
-    d_qkv_1, qkv_sums_1 = gate(attention_backward(qkv_1, gate(d_mixed_1), lse_1, hidden_keys))
-    gate.arrived(contract_sum_1)
-    contract_sum_1.over_line(gate)
     in_sum_1 = Sum(normed_1, gate(d_qkv_1), count)
     gate.sent(in_sum_1)
     in_sum_1.first()
+    own = gate(partial_product(gate(d_qkv_1), attn_in_1, True, "back_in"))
+    own, other, other_out = gate(own, swap_cores(own), swap_cores(own_out))
     gate.arrived(expand_sum_1)
     expand_sum_1.over_line(gate)
-    own = gate(partial_product(gate(d_qkv_1), attn_in_1, True, "back_in"))
-    own, other, other_out = gate(own, swap_cores(own), swap_cores(own_out))
     own_out, other_out = jnp.concatenate(own_out, axis=1), jnp.concatenate(other_out, axis=1)
     output = middle_1 + own_out.astype(F32) + other_out.astype(F32) + vectors_1[7:8]
     output = output.astype(BF16)
     d_result_0, in_sums_1 = back_norm(d_middle_1, own, other, stream_1, vectors_1[0:1], None)
     d_result_0 = gate(d_result_0)
+
+    contract_sum_0 = Sum(hidden_0, gate(d_result_0), count)
+    gate.sent(contract_sum_0)
+    contract_sum_0.first()
     gate.arrived(in_sum_1)
     in_sum_1.add()
     gate.sent(in_sum_1)
     in_sum_1.second()
-
-    contract_sum_0 = Sum(hidden_0, gate(d_result_0), count)
-    gate.sent(contract_sum_0)
-    contract_sum_0.first()
     d_pre_0, hidden_sums_0 = back_hidden(gate(d_result_0), contract_0, slope_0)
     d_pre_0, output = gate(d_pre_0, output)
-    gate.arrived(in_sum_1)
-    in_sum_1.over_line(gate)
     expand_sum_0 = Sum(normed_mid_0, gate(d_pre_0), count)
     gate.sent(expand_sum_0)
     expand_sum_0.first()
+    gate.arrived(in_sum_1)
+    in_sum_1.over_line(gate)
     gate.summed(contract_sum_1)
     own = gate(partial_product(gate(d_pre_0), expand_0, True, "back_expand"))
     gate.arrived(contract_sum_0)

time: 826 us -> 802 us (0.971)
  other arithmetic: 80.3 us -> 70.2 us
    unnamed x354 -> x346, local copies, waits for them, and re-layouts: 130 us -> 130 us
  transfers between devices with their start and end apart: 98 -> 98, of which waited for: 32 -> 31; matrix products, arithmetic and copies ran while one was open for 14% -> 13% of each run, Pallas kernels for 32% -> 33%
where the time goes in v3:
time: 802 us; the launch traced here: 791 us
  Pallas kernels  267 us (33%)
  local copies, waits for them, and re-layouts  173 us (22%)
  waiting for transfers between devices  171 us (21%)
  starting transfers between devices  92.8 us (12%)
  other arithmetic  70.2 us (9%)
  between operations  16.5 us (2%)
    ppermute x53, waiting for transfers between devices, swap_seq(): return lax.ppermute(value, ('section', 'seq'), pairs)  139 us
    unnamed x346, local copies, waits for them, and re-layouts  130 us
    pallas_call x20, Pallas kernels, whole_call(): pl.pallas_call(kernel, out_shape=shapes, in_specs=whole_vmem(len(arrays))...  96.2 us
    ppermute x53, starting transfers between devices, swap_seq(): return lax.ppermute(value, ('section', 'seq'), pairs)  65.4 us
    pallas_call x6, Pallas kernels, grad_halves(): pl.pallas_call(kernel, out_shape=(shape, shape), grid_spec=pltpu.Prefetch...  43.7 us
    pallas_call x2, Pallas kernels, attention_backward(): pl.pallas_call(kernel, grid=(heads,), out_shape=(jax.ShapeDtypeStruct((le...  41.7 us
    pallas_call x2, Pallas kernels, attention_forward(): pl.pallas_call(kernel, grid=(heads,), out_shape=(jax.ShapeDtypeStruct((le...  26.5 us
    pallas_call x6, Pallas kernels, add_half(): pl.pallas_call(kernel, out_shape=(shape, shape), grid_spec=pltpu.Prefetch...  22.9 us
  transfers between devices with their start and end apart: 98, of which 31 were waited for; matrix products, arithmetic and copies ran while one was open for 13% of the time, Pallas kernels for 33%

profile of v3, /device:TPU:0, one launch (start us, length us, event | category | flops | bytes accessed | tf_op | source)
XLA Modules:
  0.0 790.8 jit_solution(11045245715795059267)
XLA Ops:
  53.2 10.4 %collective-permute-done.7 = bf16[184,1152]{1,0:T(8,128)(2,1)S(1)} collective-permute-done((bf16[184,1152]{1,0:T(8,128)(2,1)}, bf16[184,1152]{1,0:T(8,128)(2,1)S(1)}, u32[]{:S(2)}, u32[]{:S(2)}) %collective-permute-start.7) | collective-permute-done | bytes 423968 | tf_op jit(solution)/shard_map/ppermute | solution.py:38
  75.0 13.7 %all-gather.9.cloned.1.call-done = bf16[288,2752]{1,0:T(8,128)(2,1)} async-done(((bf16[72,2752]{1,0:T(8,128)(2,1)}), bf16[288,2752]{1,0:T(8,128)(2,1)}) %all-gather.9.cloned.1.call-update) | async-done | bytes 1585168 | tf_op jit(solution)/shard_map/all_gather | solution.py:224
  98.5 31.0 %collective-permute-done.13.across_ref = bf16[3,72,1728]{2,1,0:T(8,128)(2,1)} collective-permute-done((bf16[3,72,1728]{2,1,0:T(8,128)(2,1)}, bf16[3,72,1728]{2,1,0:T(8,128)(2,1)}, u32[]{:S(2)}, u32[]{:S(2)}) %collective-permute-start.13) | collective-permute-done | bytes 746528 | tf_op jit(solution)/shard_map/ppermute | solution.py:38
  136.7 4.2 assemble.6
  140.9 4.5 project_in.2
  164.0 13.2 %attention_forward.2 = (bf16[736,576]{1,0:T(8,128)(2,1)S(1)}, f32[8,1,736]{2,1,0:T(1,128)S(1)}) custom-call(bf16[736,1728]{1,0:T(8,128)(2,1)S(1)} %copy-done.34, f32[736,1]{1,0:T(8,128)S(1)} %broadcast_select_fusion.10.hidden_ref), custom_call_target="tpu_custom_call" | custom-call | flops 1 | bytes 1 | tf_op jit(solution)/shard_map/attention_forward/pallas_call | solution.py:429
  196.6 11.7 %expand_hidden.2 = (f32[736,1152]{1,0:T(8,128)S(1)}, bf16[736,1152]{1,0:T(8,128)(2,1)S(1)}, bf16[736,2176]{1,0:T(8,128)(2,1)S(1)}, bf16[736,2176]{1,0:T(8,128)(2,1)S(1)}) custom-call(bf16[736,1152]{1,0:T(8,128)(2,1)S(1)} %broadcast_select_fusion.1.refs_0_.stream_ref.refs_5_, bf16[736,640]{1,0:T(8,128)(2,1)} %get-tuple-element.449.refs_0_, ...), custom_call_target="tpu_custom_call" | custom-call | flops 1 | bytes 1 | tf_op jit(solution)/shard_map/expand_hidden/pallas_call | solution.py:528
  217.4 6.3 collective-permute-done.25.across_ref
  231.7 6.0 collective-permute-done.28.across_ref
  240.8 5.6 contract_hidden.2
  255.3 4.1 all-gather.15.cloned.1.call-done
  266.1 7.3 project_in.3
  282.3 13.2 %attention_forward.3 = (bf16[736,576]{1,0:T(8,128)(2,1)S(1)}, f32[8,1,736]{2,1,0:T(1,128)S(1)}) custom-call(bf16[736,1728]{1,0:T(8,128)(2,1)S(1)} %get-tuple-element.486.qkv_ref, f32[736,1]{1,0:T(8,128)S(1)} %copy-done.39), custom_call_target="tpu_custom_call" | custom-call | flops 1 | bytes 1 | tf_op jit(solution)/shard_map/attention_forward/pallas_call | solution.py:429
  296.5 7.5 collective-permute-done.35.across_ref
  337.1 11.3 %expand_hidden.3 = (f32[736,1152]{1,0:T(8,128)S(1)}, bf16[736,1152]{1,0:T(8,128)(2,1)S(1)}, bf16[736,2176]{1,0:T(8,128)(2,1)S(1)}, bf16[736,2176]{1,0:T(8,128)(2,1)S(1)}) custom-call(bf16[736,1152]{1,0:T(8,128)(2,1)S(1)} %copy-done.42, bf16[736,640]{1,0:T(8,128)(2,1)} %get-tuple-element.503.refs_0_, bf16[736,512]{1,0:T(8,128)(2,1)} %get-tuple-element.504.refs_1_, ...), custom_call_target="tpu_custom_call" | custom-call | flops 1 | bytes 1 | tf_op jit(solution)/shard_map/expand_hidden/pallas_call | solution.py:528
  353.6 8.1 %grad_halves.6 = (bf16[4,2,136,1152]{3,2,1,0:T(8,128)(2,1)S(1)}, bf16[4,2,136,1152]{3,2,1,0:T(8,128)(2,1)}) custom-call(s32[3]{0:T(128)S(1)} %pad_add_fusion.bits_ref, bf16[736,2176]{1,0:T(8,128)(2,1)S(1)} %get-tuple-element.519.left_ref, bf16[736,1152]{1,0:T(8,128)(2,1)S(1)} %broadcast_select_fusion.d_ref.right_ref.refs_0_), custom_call_target="tpu_custom_call" | custom-call | flops 1 | bytes 1 | tf_op jit(solution)/shard_map/grad_halves/pallas_call | solution.py:282
  367.3 4.6 back_hidden.2
  375.5 7.6 grad_halves.7
  383.1 4.6 back_expand.2
  390.3 4.5 contract_hidden.3
  395.7 4.5 add_half.6
  413.6 4.5 back_norm.4
  421.6 20.7 %attention_backward.2 = (bf16[736,1728]{1,0:T(8,128)(2,1)S(1)}, f32[1,1728]{1,0:T(1,128)S(1)}) custom-call(bf16[736,1728]{1,0:T(8,128)(2,1)S(1)} %copy-done.37, bf16[736,576]{1,0:T(8,128)(2,1)S(1)} %get-tuple-element.556.do_ref, f32[8,1,736]{2,1,0:T(1,128)S(1)} %get-tuple-element.557.lse_ref, f32[736,1]{1,0:T(8,128)S(1)} %copy-done.40), custom_call_target="tpu_custom_call" | custom-call | flops 1 | bytes 1 | tf_op jit(solution)/shard_map/attention_backward/pallas_call | solution.py:490
  448.3 4.0 add_half.7
  453.2 6.5 grad_halves.8
  482.1 8.3 %grad_halves.9 = (bf16[4,2,136,1152]{3,2,1,0:T(8,128)(2,1)S(1)}, bf16[4,2,136,1152]{3,2,1,0:T(8,128)(2,1)}) custom-call(s32[3]{0:T(128)S(1)} %pad_add_fusion.bits_ref, bf16[736,2176]{1,0:T(8,128)(2,1)S(1)} %copy-done.19, bf16[736,1152]{1,0:T(8,128)(2,1)S(1)} %get-tuple-element.610.right_ref.d_ref.refs_0_), custom_call_target="tpu_custom_call" | custom-call | flops 1 | bytes 1 | tf_op jit(solution)/shard_map/grad_halves/pallas_call | solution.py:282
  492.0 4.2 add_half.8
  498.9 4.9 add_convert_fusion
  506.3 4.7 back_hidden.3
  511.0 6.7 grad_halves.10
  528.2 4.5 back_expand.3
  547.4 6.4 back_norm.6
  566.2 21.0 %attention_backward.3 = (bf16[736,1728]{1,0:T(8,128)(2,1)S(1)}, f32[1,1728]{1,0:T(1,128)S(1)}) custom-call(bf16[736,1728]{1,0:T(8,128)(2,1)S(1)} %copy-done.35, bf16[736,576]{1,0:T(8,128)(2,1)S(1)} %copy-done.107, f32[8,1,736]{2,1,0:T(1,128)S(1)} %get-tuple-element.667.lse_ref, f32[736,1]{1,0:T(8,128)S(1)} %copy-done.40), custom_call_target="tpu_custom_call" | custom-call | flops 1 | bytes 1 | tf_op jit(solution)/shard_map/attention_backward/pallas_call | solution.py:490
  599.0 6.5 grad_halves.11
  614.3 6.9 collective-permute-start.63
  638.7 8.7 %collective-permute-done.66.moved_ref = bf16[4,2,72,1728]{3,2,1,0:T(8,128)(2,1)} collective-permute-done((bf16[4,2,72,1728]{3,2,1,0:T(8,128)(2,1)}, bf16[4,2,72,1728]{3,2,1,0:T(8,128)(2,1)}, u32[]{:S(2)}, u32[]{:S(2)}) %collective-permute-start.66) | collective-permute-done | bytes 1990688 | tf_op jit(solution)/shard_map/ppermute | solution.py:38
  656.5 10.3 %collective-permute-done.68 = bf16[4,72,1728]{2,1,0:T(8,128)(2,1)S(1)} collective-permute-done((bf16[4,72,1728]{2,1,0:T(8,128)(2,1)S(1)}, bf16[4,72,1728]{2,1,0:T(8,128)(2,1)S(1)}, u32[]{:S(2)}, u32[]{:S(2)}) %collective-permute-start.68) | collective-permute-done | bytes 995360 | tf_op jit(solution)/shard_map/ppermute | solution.py:38
  687.2 4.4 collective-permute-done.73
  694.6 4.2 reduce-scatter.21.cloned.1.call-done
  698.9 4.5 collective-permute-start.77
  706.4 5.8 join_rows.1
  714.3 7.0 collective-permute-done.76.refs_2_
  725.9 10.1 %collective-permute-done.81.refs_3_ = bf16[2,72,2176]{2,1,0:T(8,128)(2,1)S(1)} collective-permute-done((bf16[2,72,2176]{2,1,0:T(8,128)(2,1)}, bf16[2,72,2176]{2,1,0:T(8,128)(2,1)S(1)}, u32[]{:S(2)}, u32[]{:S(2)}) %collective-permute-start.81) | collective-permute-done | bytes 626720 | tf_op jit(solution)/shard_map/ppermute | solution.py:38
  737.7 3.8 collective-permute-done.79.refs_1_
  741.9 4.9 join_columns.2
  746.8 3.8 collective-permute-done.82.refs_3_
  762.4 4.5 collective-permute-done.84
  771.3 8.5 %collective-permute-done.85 = bf16[2,160,1152]{2,1,0:T(8,128)(2,1)S(1)} collective-permute-done((bf16[2,160,1152]{2,1,0:T(8,128)(2,1)S(1)}, bf16[2,160,1152]{2,1,0:T(8,128)(2,1)S(1)}, u32[]{:S(2)}, u32[]{:S(2)}) %collective-permute-start.85) | collective-permute-done | bytes 737312 | tf_op jit(solution)/shard_map/ppermute | solution.py:38
  (730 shorter events, 400.1 us)
Async XLA Ops:
  7.2 81.6 %all-gather.9.cloned.1.call-start = ((), (), s32[]{:S(2)}) async-start(), calls=%async_computation.12 | async-start | bytes 2027520 | tf_op jit(solution)/shard_map/all_gather | solution.py:224
  19.1 30.1 %collective-permute-start.4 = (bf16[80,1728]{1,0:T(8,128)(2,1)}, bf16[80,1728]{1,0:T(8,128)(2,1)}, u32[]{:S(2)}, u32[]{:S(2)}) collective-permute-start(bf16[80,1728]{1,0:T(8,128)(2,1)} %pad_maximum_fusion.12), channel_id=1, source_target_pairs={{3,0},{0,1},{1,2},{2,3},{7,4},{4,5},{5,6},{6,7},{11,8},{8,9},{9,10... | collective-permute-start | bytes 829448 | tf_op jit(solution)/shard_map/ppermute | solution.py:217
  22.1 31.1 %collective-permute-start.3 = (bf16[80,1728]{1,0:T(8,128)(2,1)}, bf16[80,1728]{1,0:T(8,128)(2,1)}, u32[]{:S(2)}, u32[]{:S(2)}) collective-permute-start(bf16[80,1728]{1,0:T(8,128)(2,1)} %pad_maximum_fusion.12), channel_id=1, source_target_pairs={{2,0},{3,1},{0,2},{1,3},{6,4},{7,5},{4,6},{5,7},{10,8},{11,9},{8,1... | collective-permute-start | bytes 829448 | tf_op jit(solution)/shard_map/ppermute | solution.py:217
  24.7 28.5 %collective-permute-start.2 = (bf16[80,1728]{1,0:T(8,128)(2,1)}, bf16[80,1728]{1,0:T(8,128)(2,1)}, u32[]{:S(2)}, u32[]{:S(2)}) collective-permute-start(bf16[80,1728]{1,0:T(8,128)(2,1)} %pad_maximum_fusion.12), channel_id=1, source_target_pairs={{1,0},{2,1},{3,2},{0,3},{5,4},{6,5},{7,6},{4,7},{9,8},{10,9},{11,1... | collective-permute-start | bytes 829448 | tf_op jit(solution)/shard_map/ppermute | solution.py:217
  52.4 107.2 %all-gather.11.cloned.1.call-start = ((), (), s32[]{:S(2)}) async-start(), calls=%async_computation.13 | async-start | bytes 1566720 | tf_op jit(solution)/shard_map/all_gather | solution.py:224
  68.9 22.7 %collective-permute-start.12 = (bf16[3,72,1728]{2,1,0:T(8,128)(2,1)S(1)}, bf16[3,72,1728]{2,1,0:T(8,128)(2,1)}, u32[]{:S(2)}, u32[]{:S(2)}) collective-permute-start(bf16[3,72,1728]{2,1,0:T(8,128)(2,1)S(1)} %pad_maximum_fusion.6.near_ref), channel_id=1, source_target_pairs={{0,8},{4,12},{8,0},{12,4},{16,20},{20,16},{24,28},{28,24},{1,9},{5... | collective-permute-start | bytes 2239496 | tf_op jit(solution)/shard_map/ppermute | solution.py:38
  74.2 140.5 %all-gather.13.cloned.1.call-start = ((), (), s32[]{:S(2)}) async-start(), calls=%async_computation.14 | async-start | bytes 2027520 | tf_op jit(solution)/shard_map/all_gather | solution.py:224
  92.4 58.7 %collective-permute-start.16 = (bf16[3,72,2752]{2,1,0:T(8,128)(2,1)}, bf16[3,72,2752]{2,1,0:T(8,128)(2,1)}, u32[]{:S(2)}, u32[]{:S(2)}) collective-permute-start(bf16[3,72,2752]{2,1,0:T(8,128)(2,1)} %fusion.1.near_ref), channel_id=1, source_target_pairs={{0,8},{4,12},{8,0},{12,4},{16,20},{20,16},{24,28},{28,24},{1,9},{5... | collective-permute-start | bytes 3566600 | tf_op jit(solution)/shard_map/ppermute | solution.py:38
  93.9 57.2 %collective-permute-start.15 = (bf16[3,72,2752]{2,1,0:T(8,128)(2,1)}, bf16[3,72,2752]{2,1,0:T(8,128)(2,1)}, u32[]{:S(2)}, u32[]{:S(2)}) collective-permute-start(bf16[3,72,2752]{2,1,0:T(8,128)(2,1)} %fusion.1.near_ref), channel_id=1, source_target_pairs={{0,4},{4,0},{8,12},{12,8},{16,24},{20,28},{24,16},{28,20},{1,5},{5... | collective-permute-start | bytes 3566600 | tf_op jit(solution)/shard_map/ppermute | solution.py:38
  95.7 33.8 %collective-permute-start.13 = (bf16[3,72,1728]{2,1,0:T(8,128)(2,1)}, bf16[3,72,1728]{2,1,0:T(8,128)(2,1)}, u32[]{:S(2)}, u32[]{:S(2)}) collective-permute-start(bf16[3,72,1728]{2,1,0:T(8,128)(2,1)} %collective-permute-done.12.second_ref), channel_id=1, source_target_pairs={{0,4},{4,0},{8,12},{12,8},{16,24},{20,28},{24,16},{28,20},{1,5},{5... | collective-permute-start | bytes 2239496 | tf_op jit(solution)/shard_map/ppermute | solution.py:38
  151.1 108.3 %all-gather.15.cloned.1.call-start = ((), (), s32[]{:S(2)}) async-start(), calls=%async_computation.15 | async-start | bytes 1566720 | tf_op jit(solution)/shard_map/all_gather | solution.py:224
  151.2 27.0 %collective-permute-start.20 = (bf16[3,72,2752]{2,1,0:T(8,128)(2,1)}, bf16[3,72,2752]{2,1,0:T(8,128)(2,1)S(1)}, u32[]{:S(2)}, u32[]{:S(2)}) collective-permute-start(bf16[3,72,2752]{2,1,0:T(8,128)(2,1)} %collective-permute-done.16.second_ref), channel_id=1, source_target_pairs={{0,4},{4,0},{8,12},{12,8},{16,24},{20,28},{24,16},{28,20},{1,5},{5... | collective-permute-start | bytes 3566600 | tf_op jit(solution)/shard_map/ppermute | solution.py:38
  154.8 37.0 %collective-permute-start.22 = (bf16[3,72,1728]{2,1,0:T(8,128)(2,1)}, bf16[3,72,1728]{2,1,0:T(8,128)(2,1)}, u32[]{:S(2)}, u32[]{:S(2)}) collective-permute-start(bf16[3,72,1728]{2,1,0:T(8,128)(2,1)} %pad_maximum_fusion.7.near_ref), channel_id=1, source_target_pairs={{0,8},{4,12},{8,0},{12,4},{16,20},{20,16},{24,28},{28,24},{1,9},{5... | collective-permute-start | bytes 2239496 | tf_op jit(solution)/shard_map/ppermute | solution.py:38
  156.3 35.5 %collective-permute-start.21 = (bf16[3,72,1728]{2,1,0:T(8,128)(2,1)}, bf16[3,72,1728]{2,1,0:T(8,128)(2,1)}, u32[]{:S(2)}, u32[]{:S(2)}) collective-permute-start(bf16[3,72,1728]{2,1,0:T(8,128)(2,1)} %pad_maximum_fusion.7.near_ref), channel_id=1, source_target_pairs={{0,4},{4,0},{8,12},{12,8},{16,24},{20,28},{24,16},{28,20},{1,5},{5... | collective-permute-start | bytes 2239496 | tf_op jit(solution)/shard_map/ppermute | solution.py:38
  192.3 31.4 %collective-permute-start.27 = (bf16[3,136,1152]{2,1,0:T(8,128)(2,1)}, bf16[3,136,1152]{2,1,0:T(8,128)(2,1)}, u32[]{:S(2)}, u32[]{:S(2)}) collective-permute-start(bf16[3,136,1152]{2,1,0:T(8,128)(2,1)} %fusion.3.near_ref), channel_id=1, source_target_pairs={{0,8},{4,12},{8,0},{12,4},{16,20},{20,16},{24,28},{28,24},{1,9},{5... | collective-permute-start | bytes 2820104 | tf_op jit(solution)/shard_map/ppermute | solution.py:38
  192.9 30.8 %collective-permute-start.26 = (bf16[3,136,1152]{2,1,0:T(8,128)(2,1)}, bf16[3,136,1152]{2,1,0:T(8,128)(2,1)}, u32[]{:S(2)}, u32[]{:S(2)}) collective-permute-start(bf16[3,136,1152]{2,1,0:T(8,128)(2,1)} %fusion.3.near_ref), channel_id=1, source_target_pairs={{0,4},{4,0},{8,12},{12,8},{16,24},{20,28},{24,16},{28,20},{1,5},{5... | collective-permute-start | bytes 2820104 | tf_op jit(solution)/shard_map/ppermute | solution.py:38
  194.2 29.4 %collective-permute-start.25 = (bf16[3,72,1728]{2,1,0:T(8,128)(2,1)}, bf16[3,72,1728]{2,1,0:T(8,128)(2,1)}, u32[]{:S(2)}, u32[]{:S(2)}) collective-permute-start(bf16[3,72,1728]{2,1,0:T(8,128)(2,1)} %collective-permute-done.22.second_ref), channel_id=1, source_target_pairs={{0,4},{4,0},{8,12},{12,8},{16,24},{20,28},{24,16},{28,20},{1,5},{5... | collective-permute-start | bytes 2239496 | tf_op jit(solution)/shard_map/ppermute | solution.py:38
  225.1 298.4 %reduce-scatter.25.cloned.1.call-start = ((), (), s32[]{:S(2)}) async-start(), calls=%async_computation.16 | async-start | bytes 1566720
  246.9 29.6 %collective-permute-start.32 = (bf16[3,72,2752]{2,1,0:T(8,128)(2,1)S(1)}, bf16[3,72,2752]{2,1,0:T(8,128)(2,1)}, u32[]{:S(2)}, u32[]{:S(2)}) collective-permute-start(bf16[3,72,2752]{2,1,0:T(8,128)(2,1)S(1)} %copy-done.56), channel_id=1, source_target_pairs={{0,8},{4,12},{8,0},{12,4},{16,20},{20,16},{24,28},{28,24},{1,9},{5... | collective-permute-start | bytes 3566600 | tf_op jit(solution)/shard_map/ppermute | solution.py:38
  247.5 29.8 %collective-permute-start.31 = (bf16[3,72,2752]{2,1,0:T(8,128)(2,1)S(1)}, bf16[3,72,2752]{2,1,0:T(8,128)(2,1)}, u32[]{:S(2)}, u32[]{:S(2)}) collective-permute-start(bf16[3,72,2752]{2,1,0:T(8,128)(2,1)S(1)} %copy-done.56), channel_id=1, source_target_pairs={{0,4},{4,0},{8,12},{12,8},{16,24},{20,28},{24,16},{28,20},{1,5},{5... | collective-permute-start | bytes 3566600 | tf_op jit(solution)/shard_map/ppermute | solution.py:38
  250.3 27.0 %collective-permute-start.33 = (bf16[184,1152]{1,0:T(8,128)(2,1)}, bf16[184,1152]{1,0:T(8,128)(2,1)}, u32[]{:S(2)}, u32[]{:S(2)}) collective-permute-start(bf16[184,1152]{1,0:T(8,128)(2,1)} %get-tuple-element.481), channel_id=1, source_target_pairs={{16,20},{20,16},{24,28},{28,24},{17,21},{21,17},{25,29},{29,25},{1... | collective-permute-start | bytes 1271816 | tf_op jit(solution)/shard_map/ppermute | solution.py:38
  251.7 25.5 %collective-permute-start.34 = (bf16[184,1152]{1,0:T(8,128)(2,1)}, bf16[184,1152]{1,0:T(8,128)(2,1)}, u32[]{:S(2)}, u32[]{:S(2)}) collective-permute-start(bf16[184,1152]{1,0:T(8,128)(2,1)} %get-tuple-element.482), channel_id=1, source_target_pairs={{16,24},{20,28},{24,16},{28,20},{17,25},{21,29},{25,17},{29,21},{1... | collective-permute-start | bytes 1271816 | tf_op jit(solution)/shard_map/ppermute | solution.py:38
  277.3 26.7 %collective-permute-start.35 = (bf16[3,72,2752]{2,1,0:T(8,128)(2,1)}, bf16[3,72,2752]{2,1,0:T(8,128)(2,1)S(1)}, u32[]{:S(2)}, u32[]{:S(2)}) collective-permute-start(bf16[3,72,2752]{2,1,0:T(8,128)(2,1)} %collective-permute-done.32.second_ref), channel_id=1, source_target_pairs={{0,4},{4,0},{8,12},{12,8},{16,24},{20,28},{24,16},{28,20},{1,5},{5... | collective-permute-start | bytes 3566600 | tf_op jit(solution)/shard_map/ppermute | solution.py:38
  278.7 39.5 %collective-permute-start.37 = (bf16[3,136,1152]{2,1,0:T(8,128)(2,1)}, bf16[3,136,1152]{2,1,0:T(8,128)(2,1)}, u32[]{:S(2)}, u32[]{:S(2)}) collective-permute-start(bf16[3,136,1152]{2,1,0:T(8,128)(2,1)} %fusion.2.near_ref), channel_id=1, source_target_pairs={{0,8},{4,12},{8,0},{12,4},{16,20},{20,16},{24,28},{28,24},{1,9},{5... | collective-permute-start | bytes 2820104 | tf_op jit(solution)/shard_map/ppermute | solution.py:38
  280.1 38.8 %collective-permute-start.36 = (bf16[3,136,1152]{2,1,0:T(8,128)(2,1)}, bf16[3,136,1152]{2,1,0:T(8,128)(2,1)}, u32[]{:S(2)}, u32[]{:S(2)}) collective-permute-start(bf16[3,136,1152]{2,1,0:T(8,128)(2,1)} %fusion.2.near_ref), channel_id=1, source_target_pairs={{0,4},{4,0},{8,12},{12,8},{16,24},{20,28},{24,16},{28,20},{1,5},{5... | collective-permute-start | bytes 2820104 | tf_op jit(solution)/shard_map/ppermute | solution.py:38
  280.8 37.4 %collective-permute-start.38 = (bf16[184,1152]{1,0:T(8,128)(2,1)}, bf16[184,1152]{1,0:T(8,128)(2,1)}, u32[]{:S(2)}, u32[]{:S(2)}) collective-permute-start(bf16[184,1152]{1,0:T(8,128)(2,1)} %get-tuple-element.498), channel_id=1, source_target_pairs={{16,28},{20,24},{24,20},{28,16},{17,29},{21,25},{25,21},{29,17},{1... | collective-permute-start | bytes 1271816 | tf_op jit(solution)/shard_map/ppermute | solution.py:38
  324.3 27.6 %collective-permute-start.42 = (bf16[736,1152]{1,0:T(8,128)(2,1)}, bf16[736,1152]{1,0:T(8,128)(2,1)}, u32[]{:S(2)}, u32[]{:S(2)}) collective-permute-start(bf16[736,1152]{1,0:T(8,128)(2,1)} %constant_dynamic-update-slice_fusion.4), channel_id=1, source_target_pairs={{0,16},{16,0},{1,17},{17,1},{2,18},{18,2},{3,19},{19,3},{4,20},{20... | collective-permute-start | bytes 5087240 | tf_op jit(solution)/shard_map/ppermute | solution.py:26
  326.2 27.4 %collective-permute-start.41 = (bf16[3,136,1152]{2,1,0:T(8,128)(2,1)}, bf16[3,136,1152]{2,1,0:T(8,128)(2,1)}, u32[]{:S(2)}, u32[]{:S(2)}) collective-permute-start(bf16[3,136,1152]{2,1,0:T(8,128)(2,1)} %collective-permute-done.37.second_ref), channel_id=1, source_target_pairs={{0,4},{4,0},{8,12},{12,8},{16,24},{20,28},{24,16},{28,20},{1,5},{5... | collective-permute-start | bytes 2820104 | tf_op jit(solution)/shard_map/ppermute | solution.py:38
  363.1 31.7 %collective-permute-start.45 = (bf16[4,2,136,1152]{3,2,1,0:T(8,128)(2,1)}, bf16[4,2,136,1152]{3,2,1,0:T(8,128)(2,1)}, u32[]{:S(2)}, u32[]{:S(2)}) collective-permute-start(bf16[4,2,136,1152]{3,2,1,0:T(8,128)(2,1)} %get-tuple-element.536), channel_id=1, source_target_pairs={{0,4},{4,0},{8,12},{12,8},{16,24},{20,28},{24,16},{28,20},{1,5},{5... | collective-permute-start | bytes 7520264 | tf_op jit(solution)/shard_map/ppermute | solution.py:38
  389.7 56.9 %collective-permute-start.46 = (bf16[4,2,72,2176]{3,2,1,0:T(8,128)(2,1)}, bf16[4,2,72,2176]{3,2,1,0:T(8,128)(2,1)}, u32[]{:S(2)}, u32[]{:S(2)}) collective-permute-start(bf16[4,2,72,2176]{3,2,1,0:T(8,128)(2,1)} %get-tuple-element.564), channel_id=1, source_target_pairs={{0,4},{4,0},{8,12},{12,8},{16,24},{20,28},{24,16},{28,20},{1,5},{5... | collective-permute-start | bytes 7520264 | tf_op jit(solution)/shard_map/ppermute | solution.py:38
  403.2 40.6 %collective-permute-start.47 = (bf16[4,136,1152]{2,1,0:T(8,128)(2,1)}, bf16[4,136,1152]{2,1,0:T(8,128)(2,1)}, u32[]{:S(2)}, u32[]{:S(2)}) collective-permute-start(bf16[4,136,1152]{2,1,0:T(8,128)(2,1)} %get-tuple-element.566), channel_id=1, source_target_pairs={{0,8},{4,12},{8,0},{12,4},{16,20},{20,16},{24,28},{28,24},{1,9},{5... | collective-permute-start | bytes 3760136 | tf_op jit(solution)/shard_map/ppermute | solution.py:38
  446.5 112.4 %reduce-scatter.27.cloned.1.call-start = ((), (), s32[]{:S(2)}) async-start(), calls=%async_computation.17 | async-start | bytes 1566720
  465.8 26.1 %collective-permute-start.53 = (bf16[4,2,72,1728]{3,2,1,0:T(8,128)(2,1)}, bf16[4,2,72,1728]{3,2,1,0:T(8,128)(2,1)}, u32[]{:S(2)}, u32[]{:S(2)}) collective-permute-start(bf16[4,2,72,1728]{3,2,1,0:T(8,128)(2,1)} %get-tuple-element.601), channel_id=1, source_target_pairs={{0,4},{4,0},{8,12},{12,8},{16,24},{20,28},{24,16},{28,20},{1,5},{5... | collective-permute-start | bytes 5971976 | tf_op jit(solution)/shard_map/ppermute | solution.py:38
  471.5 135.3 %reduce-scatter.17.cloned.1.call-start = ((), (), s32[]{:S(2)}) async-start(), calls=%async_computation.8 | async-start | bytes 1290240 | tf_op jit(solution)/shard_map/reduce_scatter | solution.py:345
  497.1 23.5 %collective-permute-start.54 = (bf16[4,72,1728]{2,1,0:T(8,128)(2,1)}, bf16[4,72,1728]{2,1,0:T(8,128)(2,1)}, u32[]{:S(2)}, u32[]{:S(2)}) collective-permute-start(bf16[4,72,1728]{2,1,0:T(8,128)(2,1)} %get-tuple-element.619), channel_id=1, source_target_pairs={{0,8},{4,12},{8,0},{12,4},{16,20},{20,16},{24,28},{28,24},{1,9},{5... | collective-permute-start | bytes 2985992 | tf_op jit(solution)/shard_map/ppermute | solution.py:38
  503.8 34.2 %collective-permute-start.57 = (bf16[4,2,136,1152]{3,2,1,0:T(8,128)(2,1)}, bf16[4,2,136,1152]{3,2,1,0:T(8,128)(2,1)}, u32[]{:S(2)}, u32[]{:S(2)}) collective-permute-start(bf16[4,2,136,1152]{3,2,1,0:T(8,128)(2,1)} %get-tuple-element.636), channel_id=1, source_target_pairs={{0,4},{4,0},{8,12},{12,8},{16,24},{20,28},{24,16},{28,20},{1,5},{5... | collective-permute-start | bytes 7520264 | tf_op jit(solution)/shard_map/ppermute | solution.py:38
  523.2 115.5 %reduce-scatter.19.cloned.1.call-start = ((), (), s32[]{:S(2)}) async-start(), calls=%async_computation.9 | async-start | bytes 1843200 | tf_op jit(solution)/shard_map/reduce_scatter | solution.py:907
  534.0 54.8 %collective-permute-start.59 = (bf16[4,2,72,2176]{3,2,1,0:T(8,128)(2,1)}, bf16[4,2,72,2176]{3,2,1,0:T(8,128)(2,1)}, u32[]{:S(2)}, u32[]{:S(2)}) collective-permute-start(bf16[4,2,72,2176]{3,2,1,0:T(8,128)(2,1)} %copy-done.134), channel_id=1, source_target_pairs={{0,4},{4,0},{8,12},{12,8},{16,24},{20,28},{24,16},{28,20},{1,5},{5... | collective-permute-start | bytes 7520264 | tf_op jit(solution)/shard_map/ppermute | solution.py:38
  558.9 93.1 %reduce-scatter.29.cloned.1.call-start = ((), (), s32[]{:S(2)}) async-start(), calls=%async_computation.18 | async-start | bytes 1566720
  559.0 35.5 %collective-permute-start.58 = (bf16[4,136,1152]{2,1,0:T(8,128)(2,1)}, bf16[4,136,1152]{2,1,0:T(8,128)(2,1)S(1)}, u32[]{:S(2)}, u32[]{:S(2)}) collective-permute-start(bf16[4,136,1152]{2,1,0:T(8,128)(2,1)} %copy-done.135), channel_id=1, source_target_pairs={{0,8},{4,12},{8,0},{12,4},{16,20},{20,16},{24,28},{28,24},{1,9},{5... | collective-permute-start | bytes 3760136 | tf_op jit(solution)/shard_map/ppermute | solution.py:38
  561.2 27.5 %collective-permute-start.62 = (bf16[184,1152]{1,0:T(8,128)(2,1)S(1)}, bf16[184,1152]{1,0:T(8,128)(2,1)S(1)}, u32[]{:S(2)}, u32[]{:S(2)}) collective-permute-start(bf16[184,1152]{1,0:T(8,128)(2,1)S(1)} %get-tuple-element.806), channel_id=1, source_target_pairs={{16,28},{20,24},{24,20},{28,16},{17,29},{21,25},{25,21},{29,17},{1... | collective-permute-start | bytes 1271816 | tf_op jit(solution)/shard_map/ppermute | solution.py:38
  561.9 26.8 %collective-permute-start.61 = (bf16[184,1152]{1,0:T(8,128)(2,1)S(1)}, bf16[184,1152]{1,0:T(8,128)(2,1)S(1)}, u32[]{:S(2)}, u32[]{:S(2)}) collective-permute-start(bf16[184,1152]{1,0:T(8,128)(2,1)S(1)} %get-tuple-element.807), channel_id=1, source_target_pairs={{16,24},{20,28},{24,16},{28,20},{17,25},{21,29},{25,17},{29,21},{1... | collective-permute-start | bytes 1271816 | tf_op jit(solution)/shard_map/ppermute | solution.py:38
  562.6 26.2 %collective-permute-start.60 = (bf16[184,1152]{1,0:T(8,128)(2,1)S(1)}, bf16[184,1152]{1,0:T(8,128)(2,1)S(1)}, u32[]{:S(2)}, u32[]{:S(2)}) collective-permute-start(bf16[184,1152]{1,0:T(8,128)(2,1)S(1)} %get-tuple-element.808), channel_id=1, source_target_pairs={{16,20},{20,16},{24,28},{28,24},{17,21},{21,17},{25,29},{29,25},{1... | collective-permute-start | bytes 1271816 | tf_op jit(solution)/shard_map/ppermute | solution.py:38
  595.9 74.7 %reduce-scatter.31.cloned.1.call-start = ((), (), s32[]{:S(2)}) async-start(), calls=%async_computation.19 | async-start | bytes 1566720
  595.9 30.4 %collective-permute-start.65 = (bf16[4,72,2176]{2,1,0:T(8,128)(2,1)}, bf16[4,72,2176]{2,1,0:T(8,128)(2,1)}, u32[]{:S(2)}, u32[]{:S(2)}) collective-permute-start(bf16[4,72,2176]{2,1,0:T(8,128)(2,1)} %copy-done.136), channel_id=1, source_target_pairs={{0,8},{4,12},{8,0},{12,4},{16,20},{20,16},{24,28},{28,24},{1,9},{5... | collective-permute-start | bytes 3760136 | tf_op jit(solution)/shard_map/ppermute | solution.py:38
  621.3 26.0 %collective-permute-start.66 = (bf16[4,2,72,1728]{3,2,1,0:T(8,128)(2,1)}, bf16[4,2,72,1728]{3,2,1,0:T(8,128)(2,1)}, u32[]{:S(2)}, u32[]{:S(2)}) collective-permute-start(bf16[4,2,72,1728]{3,2,1,0:T(8,128)(2,1)} %get-tuple-element.717), channel_id=1, source_target_pairs={{0,4},{4,0},{8,12},{12,8},{16,24},{20,28},{24,16},{28,20},{1,5},{5... | collective-permute-start | bytes 5971976 | tf_op jit(solution)/shard_map/ppermute | solution.py:38
  629.0 69.8 %reduce-scatter.21.cloned.1.call-start = ((), (), s32[]{:S(2)}) async-start(), calls=%async_computation.10 | async-start | bytes 1290240 | tf_op jit(solution)/shard_map/reduce_scatter | solution.py:345
  668.0 82.7 %reduce-scatter.23.cloned.1.call-start = ((), (), s32[]{:S(2)}) async-start(), calls=%async_computation.11 | async-start | bytes 1843200 | tf_op jit(solution)/shard_map/reduce_scatter | solution.py:907
  (219 other events, 1587.5 us)
Sparse Core Ops, SparseCore 0:
  52.5 36.2 all-gather.8
  90.3 30.5 all-gather.10
  151.3 41.1 all-gather.12
  225.2 34.1 all-gather.14
  446.6 32.7 reduce-scatter.24
  481.7 29.1 reduce-scatter.26
  523.3 30.1 reduce-scatter.16
  559.1 38.1 reduce-scatter.18
  599.6 36.7 reduce-scatter.28
  639.2 29.1 reduce-scatter.30
  671.3 27.4 reduce-scatter.20
  701.7 32.4 reduce-scatter.22

commit v4 on v3

--- a/solution.py
+++ b/solution.py
@@ -798,7 +798,9 @@
     )
     contract_mine = gate(contract_mine)
     near_contract_0 = line_gather(contract_mine[0])
-    near_in_0, inputs = gate(near_in_0, inputs)
+    near_in_0, inputs, in_own, expand_own, contract_own = gate(
+        near_in_0, inputs, in_own, expand_own, contract_own
+    )
     packed = [packed] + [part[first_rows:] for part in near_in_0]
     near_in_0 = jnp.stack([part[:first_rows] for part in near_in_0])
     beside_in_0, near_expand_0 = gate(spread(near_in_0), near_expand_0)

time: 802 us -> 803 us (level)
    unnamed x346 -> x348, local copies, waits for them, and re-layouts: 130 us -> 132 us
  transfers between devices with their start and end apart: 98 -> 98, of which waited for: 31 -> 34; matrix products, arithmetic and copies ran while one was open for 13% -> 13% of each run, Pallas kernels for 33% -> 33%
where the time goes in v4:
time: 803 us; the launch traced here: 791 us
  Pallas kernels  267 us (33%)
  local copies, waits for them, and re-layouts  175 us (22%)
  waiting for transfers between devices  171 us (21%)
  starting transfers between devices  92.4 us (12%)
  other arithmetic  69.9 us (9%)
  between operations  16.5 us (2%)
    ppermute x53, waiting for transfers between devices, swap_seq(): return lax.ppermute(value, ('section', 'seq'), pairs)  136 us
    unnamed x348, local copies, waits for them, and re-layouts  132 us
    pallas_call x20, Pallas kernels, whole_call(): pl.pallas_call(kernel, out_shape=shapes, in_specs=whole_vmem(len(arrays))...  96.1 us
    ppermute x53, starting transfers between devices, swap_seq(): return lax.ppermute(value, ('section', 'seq'), pairs)  64.5 us
    pallas_call x6, Pallas kernels, grad_halves(): pl.pallas_call(kernel, out_shape=(shape, shape), grid_spec=pltpu.Prefetch...  43.8 us
    pallas_call x2, Pallas kernels, attention_backward(): pl.pallas_call(kernel, grid=(heads,), out_shape=(jax.ShapeDtypeStruct((le...  41.7 us
    pallas_call x2, Pallas kernels, attention_forward(): pl.pallas_call(kernel, grid=(heads,), out_shape=(jax.ShapeDtypeStruct((le...  26.4 us
    pallas_call x6, Pallas kernels, add_half(): pl.pallas_call(kernel, out_shape=(shape, shape), grid_spec=pltpu.Prefetch...  22.9 us
  transfers between devices with their start and end apart: 98, of which 34 were waited for; matrix products, arithmetic and copies ran while one was open for 13% of the time, Pallas kernels for 33%

profile of v4, /device:TPU:0, one launch (start us, length us, event | category | flops | bytes accessed | tf_op | source)
XLA Modules:
  0.0 791.3 jit_solution(2096340390463349023)
XLA Ops:
  55.9 8.0 %collective-permute-done.7 = bf16[184,1152]{1,0:T(8,128)(2,1)S(1)} collective-permute-done((bf16[184,1152]{1,0:T(8,128)(2,1)}, bf16[184,1152]{1,0:T(8,128)(2,1)S(1)}, u32[]{:S(2)}, u32[]{:S(2)}) %collective-permute-start.7) | collective-permute-done | bytes 423968 | tf_op jit(solution)/shard_map/ppermute | solution.py:38
  75.9 15.2 %all-gather.9.cloned.1.call-done = bf16[288,2752]{1,0:T(8,128)(2,1)} async-done(((bf16[72,2752]{1,0:T(8,128)(2,1)}), bf16[288,2752]{1,0:T(8,128)(2,1)}) %all-gather.9.cloned.1.call-update) | async-done | bytes 1585168 | tf_op jit(solution)/shard_map/all_gather | solution.py:224
  100.8 31.0 %collective-permute-done.13.across_ref = bf16[3,72,1728]{2,1,0:T(8,128)(2,1)} collective-permute-done((bf16[3,72,1728]{2,1,0:T(8,128)(2,1)}, bf16[3,72,1728]{2,1,0:T(8,128)(2,1)}, u32[]{:S(2)}, u32[]{:S(2)}) %collective-permute-start.13) | collective-permute-done | bytes 746528 | tf_op jit(solution)/shard_map/ppermute | solution.py:38
  139.0 4.2 assemble.6
  143.2 4.5 project_in.2
  163.5 13.2 %attention_forward.2 = (bf16[736,576]{1,0:T(8,128)(2,1)S(1)}, f32[8,1,736]{2,1,0:T(1,128)S(1)}) custom-call(bf16[736,1728]{1,0:T(8,128)(2,1)S(1)} %copy-done.34, f32[736,1]{1,0:T(8,128)S(1)} %broadcast_select_fusion.10.hidden_ref), custom_call_target="tpu_custom_call" | custom-call | flops 1 | bytes 1 | tf_op jit(solution)/shard_map/attention_forward/pallas_call | solution.py:429
  198.0 11.7 %expand_hidden.2 = (f32[736,1152]{1,0:T(8,128)S(1)}, bf16[736,1152]{1,0:T(8,128)(2,1)S(1)}, bf16[736,2176]{1,0:T(8,128)(2,1)S(1)}, bf16[736,2176]{1,0:T(8,128)(2,1)S(1)}) custom-call(bf16[736,1152]{1,0:T(8,128)(2,1)S(1)} %broadcast_select_fusion.1.refs_0_.stream_ref.refs_5_, bf16[736,640]{1,0:T(8,128)(2,1)} %get-tuple-element.457.refs_0_, ...), custom_call_target="tpu_custom_call" | custom-call | flops 1 | bytes 1 | tf_op jit(solution)/shard_map/expand_hidden/pallas_call | solution.py:528
  218.8 5.4 collective-permute-done.25.across_ref
  232.2 6.0 collective-permute-done.28.across_ref
  241.3 5.6 contract_hidden.2
  255.8 5.0 all-gather.15.cloned.1.call-done
  267.4 7.2 project_in.3
  282.8 13.2 %attention_forward.3 = (bf16[736,576]{1,0:T(8,128)(2,1)S(1)}, f32[8,1,736]{2,1,0:T(1,128)S(1)}) custom-call(bf16[736,1728]{1,0:T(8,128)(2,1)S(1)} %get-tuple-element.496.qkv_ref, f32[736,1]{1,0:T(8,128)S(1)} %copy-done.39), custom_call_target="tpu_custom_call" | custom-call | flops 1 | bytes 1 | tf_op jit(solution)/shard_map/attention_forward/pallas_call | solution.py:429
  296.9 8.6 %collective-permute-done.35.across_ref = bf16[3,72,2752]{2,1,0:T(8,128)(2,1)S(1)} collective-permute-done((bf16[3,72,2752]{2,1,0:T(8,128)(2,1)}, bf16[3,72,2752]{2,1,0:T(8,128)(2,1)S(1)}, u32[]{:S(2)}, u32[]{:S(2)}) %collective-permute-start.35) | collective-permute-done | bytes 1188896 | tf_op jit(solution)/shard_map/ppermute | solution.py:38
  339.5 11.3 %expand_hidden.3 = (f32[736,1152]{1,0:T(8,128)S(1)}, bf16[736,1152]{1,0:T(8,128)(2,1)S(1)}, bf16[736,2176]{1,0:T(8,128)(2,1)S(1)}, bf16[736,2176]{1,0:T(8,128)(2,1)S(1)}) custom-call(bf16[736,1152]{1,0:T(8,128)(2,1)S(1)} %copy-done.42, bf16[736,640]{1,0:T(8,128)(2,1)} %get-tuple-element.514.refs_0_, bf16[736,512]{1,0:T(8,128)(2,1)} %get-tuple-element.515.refs_1_, ...), custom_call_target="tpu_custom_call" | custom-call | flops 1 | bytes 1 | tf_op jit(solution)/shard_map/expand_hidden/pallas_call | solution.py:528
  356.0 8.1 %grad_halves.6 = (bf16[4,2,136,1152]{3,2,1,0:T(8,128)(2,1)S(1)}, bf16[4,2,136,1152]{3,2,1,0:T(8,128)(2,1)}) custom-call(s32[3]{0:T(128)S(1)} %pad_add_fusion.bits_ref, bf16[736,2176]{1,0:T(8,128)(2,1)S(1)} %get-tuple-element.531.left_ref, bf16[736,1152]{1,0:T(8,128)(2,1)S(1)} %broadcast_select_fusion.d_ref.right_ref.refs_0_), custom_call_target="tpu_custom_call" | custom-call | flops 1 | bytes 1 | tf_op jit(solution)/shard_map/grad_halves/pallas_call | solution.py:282
  366.0 3.7 assemble.11
  369.7 4.6 back_hidden.2
  377.9 7.6 grad_halves.7
  385.6 4.6 back_expand.2
  392.3 4.5 contract_hidden.3
  397.7 4.5 add_half.6
  414.0 4.5 back_norm.4
  422.0 20.7 %attention_backward.2 = (bf16[736,1728]{1,0:T(8,128)(2,1)S(1)}, f32[1,1728]{1,0:T(1,128)S(1)}) custom-call(bf16[736,1728]{1,0:T(8,128)(2,1)S(1)} %copy-done.37, bf16[736,576]{1,0:T(8,128)(2,1)S(1)} %get-tuple-element.568.do_ref, f32[8,1,736]{2,1,0:T(1,128)S(1)} %get-tuple-element.569.lse_ref, f32[736,1]{1,0:T(8,128)S(1)} %copy-done.40), custom_call_target="tpu_custom_call" | custom-call | flops 1 | bytes 1 | tf_op jit(solution)/shard_map/attention_backward/pallas_call | solution.py:490
  448.7 4.0 add_half.7
  455.2 6.5 grad_halves.8
  482.8 8.3 %grad_halves.9 = (bf16[4,2,136,1152]{3,2,1,0:T(8,128)(2,1)S(1)}, bf16[4,2,136,1152]{3,2,1,0:T(8,128)(2,1)}) custom-call(s32[3]{0:T(128)S(1)} %pad_add_fusion.bits_ref, bf16[736,2176]{1,0:T(8,128)(2,1)S(1)} %copy-done.19, bf16[736,1152]{1,0:T(8,128)(2,1)S(1)} %get-tuple-element.622.right_ref.d_ref.refs_0_), custom_call_target="tpu_custom_call" | custom-call | flops 1 | bytes 1 | tf_op jit(solution)/shard_map/grad_halves/pallas_call | solution.py:282
  493.8 4.2 add_half.8
  499.5 4.9 add_convert_fusion
  507.6 4.7 back_hidden.3
  512.3 6.7 grad_halves.10
  529.6 4.5 back_expand.3
  548.4 6.4 back_norm.6
  567.7 21.0 %attention_backward.3 = (bf16[736,1728]{1,0:T(8,128)(2,1)S(1)}, f32[1,1728]{1,0:T(1,128)S(1)}) custom-call(bf16[736,1728]{1,0:T(8,128)(2,1)S(1)} %copy-done.35, bf16[736,576]{1,0:T(8,128)(2,1)S(1)} %copy-done.108, f32[8,1,736]{2,1,0:T(1,128)S(1)} %get-tuple-element.679.lse_ref, f32[736,1]{1,0:T(8,128)S(1)} %copy-done.40), custom_call_target="tpu_custom_call" | custom-call | flops 1 | bytes 1 | tf_op jit(solution)/shard_map/attention_backward/pallas_call | solution.py:490
  600.0 6.5 grad_halves.11
  615.3 7.8 collective-permute-start.63
  640.6 8.6 %collective-permute-done.66.moved_ref = bf16[4,2,72,1728]{3,2,1,0:T(8,128)(2,1)} collective-permute-done((bf16[4,2,72,1728]{3,2,1,0:T(8,128)(2,1)}, bf16[4,2,72,1728]{3,2,1,0:T(8,128)(2,1)}, u32[]{:S(2)}, u32[]{:S(2)}) %collective-permute-start.66) | collective-permute-done | bytes 1990688 | tf_op jit(solution)/shard_map/ppermute | solution.py:38
  657.1 11.5 %collective-permute-done.68 = bf16[4,72,1728]{2,1,0:T(8,128)(2,1)S(1)} collective-permute-done((bf16[4,72,1728]{2,1,0:T(8,128)(2,1)S(1)}, bf16[4,72,1728]{2,1,0:T(8,128)(2,1)S(1)}, u32[]{:S(2)}, u32[]{:S(2)}) %collective-permute-start.68) | collective-permute-done | bytes 995360 | tf_op jit(solution)/shard_map/ppermute | solution.py:38
  689.0 4.6 collective-permute-done.73
  699.4 4.5 collective-permute-start.77
  707.0 5.8 join_rows.1
  714.9 7.0 collective-permute-done.76.refs_2_
  726.5 10.1 %collective-permute-done.81.refs_3_ = bf16[2,72,2176]{2,1,0:T(8,128)(2,1)S(1)} collective-permute-done((bf16[2,72,2176]{2,1,0:T(8,128)(2,1)}, bf16[2,72,2176]{2,1,0:T(8,128)(2,1)S(1)}, u32[]{:S(2)}, u32[]{:S(2)}) %collective-permute-start.81) | collective-permute-done | bytes 626720 | tf_op jit(solution)/shard_map/ppermute | solution.py:38
  738.3 3.8 collective-permute-done.79.refs_1_
  742.5 4.9 join_columns.2
  747.4 3.8 collective-permute-done.82.refs_3_
  763.0 4.5 collective-permute-done.84
  771.9 8.5 %collective-permute-done.85 = bf16[2,160,1152]{2,1,0:T(8,128)(2,1)S(1)} collective-permute-done((bf16[2,160,1152]{2,1,0:T(8,128)(2,1)S(1)}, bf16[2,160,1152]{2,1,0:T(8,128)(2,1)S(1)}, u32[]{:S(2)}, u32[]{:S(2)}) %collective-permute-start.85) | collective-permute-done | bytes 737312 | tf_op jit(solution)/shard_map/ppermute | solution.py:38
  (732 shorter events, 399.0 us)
Async XLA Ops:
  7.2 83.9 %all-gather.9.cloned.1.call-start = ((), (), s32[]{:S(2)}) async-start(), calls=%async_computation.12 | async-start | bytes 2027520 | tf_op jit(solution)/shard_map/all_gather | solution.py:224
  19.2 32.3 %collective-permute-start.4 = (bf16[80,1728]{1,0:T(8,128)(2,1)}, bf16[80,1728]{1,0:T(8,128)(2,1)}, u32[]{:S(2)}, u32[]{:S(2)}) collective-permute-start(bf16[80,1728]{1,0:T(8,128)(2,1)} %pad_maximum_fusion.12), channel_id=1, source_target_pairs={{3,0},{0,1},{1,2},{2,3},{7,4},{4,5},{5,6},{6,7},{11,8},{8,9},{9,10... | collective-permute-start | bytes 829448 | tf_op jit(solution)/shard_map/ppermute | solution.py:217
  22.2 33.3 %collective-permute-start.3 = (bf16[80,1728]{1,0:T(8,128)(2,1)}, bf16[80,1728]{1,0:T(8,128)(2,1)}, u32[]{:S(2)}, u32[]{:S(2)}) collective-permute-start(bf16[80,1728]{1,0:T(8,128)(2,1)} %pad_maximum_fusion.12), channel_id=1, source_target_pairs={{2,0},{3,1},{0,2},{1,3},{6,4},{7,5},{4,6},{5,7},{10,8},{11,9},{8,1... | collective-permute-start | bytes 829448 | tf_op jit(solution)/shard_map/ppermute | solution.py:217
  24.8 30.7 %collective-permute-start.2 = (bf16[80,1728]{1,0:T(8,128)(2,1)}, bf16[80,1728]{1,0:T(8,128)(2,1)}, u32[]{:S(2)}, u32[]{:S(2)}) collective-permute-start(bf16[80,1728]{1,0:T(8,128)(2,1)} %pad_maximum_fusion.12), channel_id=1, source_target_pairs={{1,0},{2,1},{3,2},{0,3},{5,4},{6,5},{7,6},{4,7},{9,8},{10,9},{11,1... | collective-permute-start | bytes 829448 | tf_op jit(solution)/shard_map/ppermute | solution.py:217
  30.6 24.9 %collective-permute-start.5 = (bf16[184,1152]{1,0:T(8,128)(2,1)}, bf16[184,1152]{1,0:T(8,128)(2,1)}, u32[]{:S(2)}, u32[]{:S(2)}) collective-permute-start(bf16[184,1152]{1,0:T(8,128)(2,1)} %get-tuple-element.491), channel_id=1, source_target_pairs={{0,4},{4,0},{8,12},{12,8},{1,5},{5,1},{9,13},{13,9},{2,6},{6,2},{1... | collective-permute-start | bytes 1271816 | tf_op jit(solution)/shard_map/ppermute | solution.py:38
  54.7 104.5 %all-gather.11.cloned.1.call-start = ((), (), s32[]{:S(2)}) async-start(), calls=%async_computation.13 | async-start | bytes 1566720 | tf_op jit(solution)/shard_map/all_gather | solution.py:224
  69.2 24.6 %collective-permute-start.12 = (bf16[3,72,1728]{2,1,0:T(8,128)(2,1)S(1)}, bf16[3,72,1728]{2,1,0:T(8,128)(2,1)}, u32[]{:S(2)}, u32[]{:S(2)}) collective-permute-start(bf16[3,72,1728]{2,1,0:T(8,128)(2,1)S(1)} %pad_maximum_fusion.6.near_ref), channel_id=1, source_target_pairs={{0,8},{4,12},{8,0},{12,4},{16,20},{20,16},{24,28},{28,24},{1,9},{5... | collective-permute-start | bytes 2239496 | tf_op jit(solution)/shard_map/ppermute | solution.py:38
  75.1 141.0 %all-gather.13.cloned.1.call-start = ((), (), s32[]{:S(2)}) async-start(), calls=%async_computation.14 | async-start | bytes 2027520 | tf_op jit(solution)/shard_map/all_gather | solution.py:224
  94.7 58.7 %collective-permute-start.16 = (bf16[3,72,2752]{2,1,0:T(8,128)(2,1)}, bf16[3,72,2752]{2,1,0:T(8,128)(2,1)}, u32[]{:S(2)}, u32[]{:S(2)}) collective-permute-start(bf16[3,72,2752]{2,1,0:T(8,128)(2,1)} %fusion.1.near_ref), channel_id=1, source_target_pairs={{0,8},{4,12},{8,0},{12,4},{16,20},{20,16},{24,28},{28,24},{1,9},{5... | collective-permute-start | bytes 3566600 | tf_op jit(solution)/shard_map/ppermute | solution.py:38
  96.2 57.2 %collective-permute-start.15 = (bf16[3,72,2752]{2,1,0:T(8,128)(2,1)}, bf16[3,72,2752]{2,1,0:T(8,128)(2,1)}, u32[]{:S(2)}, u32[]{:S(2)}) collective-permute-start(bf16[3,72,2752]{2,1,0:T(8,128)(2,1)} %fusion.1.near_ref), channel_id=1, source_target_pairs={{0,4},{4,0},{8,12},{12,8},{16,24},{20,28},{24,16},{28,20},{1,5},{5... | collective-permute-start | bytes 3566600 | tf_op jit(solution)/shard_map/ppermute | solution.py:38
  98.0 33.8 %collective-permute-start.13 = (bf16[3,72,1728]{2,1,0:T(8,128)(2,1)}, bf16[3,72,1728]{2,1,0:T(8,128)(2,1)}, u32[]{:S(2)}, u32[]{:S(2)}) collective-permute-start(bf16[3,72,1728]{2,1,0:T(8,128)(2,1)} %collective-permute-done.12.second_ref), channel_id=1, source_target_pairs={{0,4},{4,0},{8,12},{12,8},{16,24},{20,28},{24,16},{28,20},{1,5},{5... | collective-permute-start | bytes 2239496 | tf_op jit(solution)/shard_map/ppermute | solution.py:38
  153.4 107.4 %all-gather.15.cloned.1.call-start = ((), (), s32[]{:S(2)}) async-start(), calls=%async_computation.15 | async-start | bytes 1566720 | tf_op jit(solution)/shard_map/all_gather | solution.py:224
  153.5 25.2 %collective-permute-start.20 = (bf16[3,72,2752]{2,1,0:T(8,128)(2,1)}, bf16[3,72,2752]{2,1,0:T(8,128)(2,1)S(1)}, u32[]{:S(2)}, u32[]{:S(2)}) collective-permute-start(bf16[3,72,2752]{2,1,0:T(8,128)(2,1)} %collective-permute-done.16.second_ref), channel_id=1, source_target_pairs={{0,4},{4,0},{8,12},{12,8},{16,24},{20,28},{24,16},{28,20},{1,5},{5... | collective-permute-start | bytes 3566600 | tf_op jit(solution)/shard_map/ppermute | solution.py:38
  157.1 35.2 %collective-permute-start.22 = (bf16[3,72,1728]{2,1,0:T(8,128)(2,1)}, bf16[3,72,1728]{2,1,0:T(8,128)(2,1)}, u32[]{:S(2)}, u32[]{:S(2)}) collective-permute-start(bf16[3,72,1728]{2,1,0:T(8,128)(2,1)} %pad_maximum_fusion.7.near_ref), channel_id=1, source_target_pairs={{0,8},{4,12},{8,0},{12,4},{16,20},{20,16},{24,28},{28,24},{1,9},{5... | collective-permute-start | bytes 2239496 | tf_op jit(solution)/shard_map/ppermute | solution.py:38
  158.6 33.7 %collective-permute-start.21 = (bf16[3,72,1728]{2,1,0:T(8,128)(2,1)}, bf16[3,72,1728]{2,1,0:T(8,128)(2,1)}, u32[]{:S(2)}, u32[]{:S(2)}) collective-permute-start(bf16[3,72,1728]{2,1,0:T(8,128)(2,1)} %pad_maximum_fusion.7.near_ref), channel_id=1, source_target_pairs={{0,4},{4,0},{8,12},{12,8},{16,24},{20,28},{24,16},{28,20},{1,5},{5... | collective-permute-start | bytes 2239496 | tf_op jit(solution)/shard_map/ppermute | solution.py:38
  192.8 31.4 %collective-permute-start.27 = (bf16[3,136,1152]{2,1,0:T(8,128)(2,1)}, bf16[3,136,1152]{2,1,0:T(8,128)(2,1)}, u32[]{:S(2)}, u32[]{:S(2)}) collective-permute-start(bf16[3,136,1152]{2,1,0:T(8,128)(2,1)} %fusion.3.near_ref), channel_id=1, source_target_pairs={{0,8},{4,12},{8,0},{12,4},{16,20},{20,16},{24,28},{28,24},{1,9},{5... | collective-permute-start | bytes 2820104 | tf_op jit(solution)/shard_map/ppermute | solution.py:38
  194.3 30.0 %collective-permute-start.26 = (bf16[3,136,1152]{2,1,0:T(8,128)(2,1)}, bf16[3,136,1152]{2,1,0:T(8,128)(2,1)}, u32[]{:S(2)}, u32[]{:S(2)}) collective-permute-start(bf16[3,136,1152]{2,1,0:T(8,128)(2,1)} %fusion.3.near_ref), channel_id=1, source_target_pairs={{0,4},{4,0},{8,12},{12,8},{16,24},{20,28},{24,16},{28,20},{1,5},{5... | collective-permute-start | bytes 2820104 | tf_op jit(solution)/shard_map/ppermute | solution.py:38
  195.6 28.6 %collective-permute-start.25 = (bf16[3,72,1728]{2,1,0:T(8,128)(2,1)}, bf16[3,72,1728]{2,1,0:T(8,128)(2,1)}, u32[]{:S(2)}, u32[]{:S(2)}) collective-permute-start(bf16[3,72,1728]{2,1,0:T(8,128)(2,1)} %collective-permute-done.22.second_ref), channel_id=1, source_target_pairs={{0,4},{4,0},{8,12},{12,8},{16,24},{20,28},{24,16},{28,20},{1,5},{5... | collective-permute-start | bytes 2239496 | tf_op jit(solution)/shard_map/ppermute | solution.py:38
  225.6 299.2 %reduce-scatter.25.cloned.1.call-start = ((), (), s32[]{:S(2)}) async-start(), calls=%async_computation.16 | async-start | bytes 1566720
  247.4 29.6 %collective-permute-start.32 = (bf16[3,72,2752]{2,1,0:T(8,128)(2,1)S(1)}, bf16[3,72,2752]{2,1,0:T(8,128)(2,1)}, u32[]{:S(2)}, u32[]{:S(2)}) collective-permute-start(bf16[3,72,2752]{2,1,0:T(8,128)(2,1)S(1)} %copy-done.57), channel_id=1, source_target_pairs={{0,8},{4,12},{8,0},{12,4},{16,20},{20,16},{24,28},{28,24},{1,9},{5... | collective-permute-start | bytes 3566600 | tf_op jit(solution)/shard_map/ppermute | solution.py:38
  248.9 29.8 %collective-permute-start.31 = (bf16[3,72,2752]{2,1,0:T(8,128)(2,1)S(1)}, bf16[3,72,2752]{2,1,0:T(8,128)(2,1)}, u32[]{:S(2)}, u32[]{:S(2)}) collective-permute-start(bf16[3,72,2752]{2,1,0:T(8,128)(2,1)S(1)} %copy-done.57), channel_id=1, source_target_pairs={{0,4},{4,0},{8,12},{12,8},{16,24},{20,28},{24,16},{28,20},{1,5},{5... | collective-permute-start | bytes 3566600 | tf_op jit(solution)/shard_map/ppermute | solution.py:38
  250.8 27.9 %collective-permute-start.33 = (bf16[184,1152]{1,0:T(8,128)(2,1)}, bf16[184,1152]{1,0:T(8,128)(2,1)}, u32[]{:S(2)}, u32[]{:S(2)}) collective-permute-start(bf16[184,1152]{1,0:T(8,128)(2,1)} %get-tuple-element.491), channel_id=1, source_target_pairs={{16,20},{20,16},{24,28},{28,24},{17,21},{21,17},{25,29},{29,25},{1... | collective-permute-start | bytes 1271816 | tf_op jit(solution)/shard_map/ppermute | solution.py:38
  252.3 26.4 %collective-permute-start.34 = (bf16[184,1152]{1,0:T(8,128)(2,1)}, bf16[184,1152]{1,0:T(8,128)(2,1)}, u32[]{:S(2)}, u32[]{:S(2)}) collective-permute-start(bf16[184,1152]{1,0:T(8,128)(2,1)} %get-tuple-element.492), channel_id=1, source_target_pairs={{16,24},{20,28},{24,16},{28,20},{17,25},{21,29},{25,17},{29,21},{1... | collective-permute-start | bytes 1271816 | tf_op jit(solution)/shard_map/ppermute | solution.py:38
  278.7 26.9 %collective-permute-start.35 = (bf16[3,72,2752]{2,1,0:T(8,128)(2,1)}, bf16[3,72,2752]{2,1,0:T(8,128)(2,1)S(1)}, u32[]{:S(2)}, u32[]{:S(2)}) collective-permute-start(bf16[3,72,2752]{2,1,0:T(8,128)(2,1)} %collective-permute-done.32.second_ref), channel_id=1, source_target_pairs={{0,4},{4,0},{8,12},{12,8},{16,24},{20,28},{24,16},{28,20},{1,5},{5... | collective-permute-start | bytes 3566600 | tf_op jit(solution)/shard_map/ppermute | solution.py:38
  280.2 39.5 %collective-permute-start.37 = (bf16[3,136,1152]{2,1,0:T(8,128)(2,1)}, bf16[3,136,1152]{2,1,0:T(8,128)(2,1)}, u32[]{:S(2)}, u32[]{:S(2)}) collective-permute-start(bf16[3,136,1152]{2,1,0:T(8,128)(2,1)} %fusion.2.near_ref), channel_id=1, source_target_pairs={{0,8},{4,12},{8,0},{12,4},{16,20},{20,16},{24,28},{28,24},{1,9},{5... | collective-permute-start | bytes 2820104 | tf_op jit(solution)/shard_map/ppermute | solution.py:38
  280.7 39.7 %collective-permute-start.36 = (bf16[3,136,1152]{2,1,0:T(8,128)(2,1)}, bf16[3,136,1152]{2,1,0:T(8,128)(2,1)}, u32[]{:S(2)}, u32[]{:S(2)}) collective-permute-start(bf16[3,136,1152]{2,1,0:T(8,128)(2,1)} %fusion.2.near_ref), channel_id=1, source_target_pairs={{0,4},{4,0},{8,12},{12,8},{16,24},{20,28},{24,16},{28,20},{1,5},{5... | collective-permute-start | bytes 2820104 | tf_op jit(solution)/shard_map/ppermute | solution.py:38
  281.3 38.3 %collective-permute-start.38 = (bf16[184,1152]{1,0:T(8,128)(2,1)}, bf16[184,1152]{1,0:T(8,128)(2,1)}, u32[]{:S(2)}, u32[]{:S(2)}) collective-permute-start(bf16[184,1152]{1,0:T(8,128)(2,1)} %get-tuple-element.509), channel_id=1, source_target_pairs={{16,28},{20,24},{24,20},{28,16},{17,29},{21,25},{25,21},{29,17},{1... | collective-permute-start | bytes 1271816 | tf_op jit(solution)/shard_map/ppermute | solution.py:38
  325.7 28.6 %collective-permute-start.42 = (bf16[736,1152]{1,0:T(8,128)(2,1)}, bf16[736,1152]{1,0:T(8,128)(2,1)}, u32[]{:S(2)}, u32[]{:S(2)}) collective-permute-start(bf16[736,1152]{1,0:T(8,128)(2,1)} %constant_dynamic-update-slice_fusion.4), channel_id=1, source_target_pairs={{0,16},{16,0},{1,17},{17,1},{2,18},{18,2},{3,19},{19,3},{4,20},{20... | collective-permute-start | bytes 5087240 | tf_op jit(solution)/shard_map/ppermute | solution.py:26
  328.6 27.4 %collective-permute-start.41 = (bf16[3,136,1152]{2,1,0:T(8,128)(2,1)}, bf16[3,136,1152]{2,1,0:T(8,128)(2,1)}, u32[]{:S(2)}, u32[]{:S(2)}) collective-permute-start(bf16[3,136,1152]{2,1,0:T(8,128)(2,1)} %collective-permute-done.37.second_ref), channel_id=1, source_target_pairs={{0,4},{4,0},{8,12},{12,8},{16,24},{20,28},{24,16},{28,20},{1,5},{5... | collective-permute-start | bytes 2820104 | tf_op jit(solution)/shard_map/ppermute | solution.py:38
  365.5 31.3 %collective-permute-start.45 = (bf16[4,2,136,1152]{3,2,1,0:T(8,128)(2,1)}, bf16[4,2,136,1152]{3,2,1,0:T(8,128)(2,1)}, u32[]{:S(2)}, u32[]{:S(2)}) collective-permute-start(bf16[4,2,136,1152]{3,2,1,0:T(8,128)(2,1)} %get-tuple-element.548), channel_id=1, source_target_pairs={{0,4},{4,0},{8,12},{12,8},{16,24},{20,28},{24,16},{28,20},{1,5},{5... | collective-permute-start | bytes 7520264 | tf_op jit(solution)/shard_map/ppermute | solution.py:38
  390.8 56.2 %collective-permute-start.46 = (bf16[4,2,72,2176]{3,2,1,0:T(8,128)(2,1)}, bf16[4,2,72,2176]{3,2,1,0:T(8,128)(2,1)}, u32[]{:S(2)}, u32[]{:S(2)}) collective-permute-start(bf16[4,2,72,2176]{3,2,1,0:T(8,128)(2,1)} %get-tuple-element.576), channel_id=1, source_target_pairs={{0,4},{4,0},{8,12},{12,8},{16,24},{20,28},{24,16},{28,20},{1,5},{5... | collective-permute-start | bytes 7520264 | tf_op jit(solution)/shard_map/ppermute | solution.py:38
  405.2 39.0 %collective-permute-start.47 = (bf16[4,136,1152]{2,1,0:T(8,128)(2,1)}, bf16[4,136,1152]{2,1,0:T(8,128)(2,1)}, u32[]{:S(2)}, u32[]{:S(2)}) collective-permute-start(bf16[4,136,1152]{2,1,0:T(8,128)(2,1)} %get-tuple-element.578), channel_id=1, source_target_pairs={{0,8},{4,12},{8,0},{12,4},{16,20},{20,16},{24,28},{28,24},{1,9},{5... | collective-permute-start | bytes 3760136 | tf_op jit(solution)/shard_map/ppermute | solution.py:38
  446.9 113.0 %reduce-scatter.27.cloned.1.call-start = ((), (), s32[]{:S(2)}) async-start(), calls=%async_computation.17 | async-start | bytes 1566720
  467.8 26.0 %collective-permute-start.53 = (bf16[4,2,72,1728]{3,2,1,0:T(8,128)(2,1)}, bf16[4,2,72,1728]{3,2,1,0:T(8,128)(2,1)}, u32[]{:S(2)}, u32[]{:S(2)}) collective-permute-start(bf16[4,2,72,1728]{3,2,1,0:T(8,128)(2,1)} %get-tuple-element.613), channel_id=1, source_target_pairs={{0,4},{4,0},{8,12},{12,8},{16,24},{20,28},{24,16},{28,20},{1,5},{5... | collective-permute-start | bytes 5971976 | tf_op jit(solution)/shard_map/ppermute | solution.py:38
  472.2 135.6 %reduce-scatter.17.cloned.1.call-start = ((), (), s32[]{:S(2)}) async-start(), calls=%async_computation.8 | async-start | bytes 1290240 | tf_op jit(solution)/shard_map/reduce_scatter | solution.py:345
  504.5 34.5 %collective-permute-start.57 = (bf16[4,2,136,1152]{3,2,1,0:T(8,128)(2,1)}, bf16[4,2,136,1152]{3,2,1,0:T(8,128)(2,1)}, u32[]{:S(2)}, u32[]{:S(2)}) collective-permute-start(bf16[4,2,136,1152]{3,2,1,0:T(8,128)(2,1)} %get-tuple-element.648), channel_id=1, source_target_pairs={{0,4},{4,0},{8,12},{12,8},{16,24},{20,28},{24,16},{28,20},{1,5},{5... | collective-permute-start | bytes 7520264 | tf_op jit(solution)/shard_map/ppermute | solution.py:38
  524.5 116.1 %reduce-scatter.19.cloned.1.call-start = ((), (), s32[]{:S(2)}) async-start(), calls=%async_computation.9 | async-start | bytes 1843200 | tf_op jit(solution)/shard_map/reduce_scatter | solution.py:909
  535.3 55.0 %collective-permute-start.59 = (bf16[4,2,72,2176]{3,2,1,0:T(8,128)(2,1)}, bf16[4,2,72,2176]{3,2,1,0:T(8,128)(2,1)}, u32[]{:S(2)}, u32[]{:S(2)}) collective-permute-start(bf16[4,2,72,2176]{3,2,1,0:T(8,128)(2,1)} %copy-done.135), channel_id=1, source_target_pairs={{0,4},{4,0},{8,12},{12,8},{16,24},{20,28},{24,16},{28,20},{1,5},{5... | collective-permute-start | bytes 7520264 | tf_op jit(solution)/shard_map/ppermute | solution.py:38
  559.9 93.9 %reduce-scatter.29.cloned.1.call-start = ((), (), s32[]{:S(2)}) async-start(), calls=%async_computation.18 | async-start | bytes 1566720
  560.0 36.0 %collective-permute-start.58 = (bf16[4,136,1152]{2,1,0:T(8,128)(2,1)}, bf16[4,136,1152]{2,1,0:T(8,128)(2,1)S(1)}, u32[]{:S(2)}, u32[]{:S(2)}) collective-permute-start(bf16[4,136,1152]{2,1,0:T(8,128)(2,1)} %copy-done.136), channel_id=1, source_target_pairs={{0,8},{4,12},{8,0},{12,4},{16,20},{20,16},{24,28},{28,24},{1,9},{5... | collective-permute-start | bytes 3760136 | tf_op jit(solution)/shard_map/ppermute | solution.py:38
  562.7 27.5 %collective-permute-start.62 = (bf16[184,1152]{1,0:T(8,128)(2,1)S(1)}, bf16[184,1152]{1,0:T(8,128)(2,1)S(1)}, u32[]{:S(2)}, u32[]{:S(2)}) collective-permute-start(bf16[184,1152]{1,0:T(8,128)(2,1)S(1)} %get-tuple-element.818), channel_id=1, source_target_pairs={{16,28},{20,24},{24,20},{28,16},{17,29},{21,25},{25,21},{29,17},{1... | collective-permute-start | bytes 1271816 | tf_op jit(solution)/shard_map/ppermute | solution.py:38
  563.4 26.8 %collective-permute-start.61 = (bf16[184,1152]{1,0:T(8,128)(2,1)S(1)}, bf16[184,1152]{1,0:T(8,128)(2,1)S(1)}, u32[]{:S(2)}, u32[]{:S(2)}) collective-permute-start(bf16[184,1152]{1,0:T(8,128)(2,1)S(1)} %get-tuple-element.819), channel_id=1, source_target_pairs={{16,24},{20,28},{24,16},{28,20},{17,25},{21,29},{25,17},{29,21},{1... | collective-permute-start | bytes 1271816 | tf_op jit(solution)/shard_map/ppermute | solution.py:38
  564.1 26.2 %collective-permute-start.60 = (bf16[184,1152]{1,0:T(8,128)(2,1)S(1)}, bf16[184,1152]{1,0:T(8,128)(2,1)S(1)}, u32[]{:S(2)}, u32[]{:S(2)}) collective-permute-start(bf16[184,1152]{1,0:T(8,128)(2,1)S(1)} %get-tuple-element.820), channel_id=1, source_target_pairs={{16,20},{20,16},{24,28},{28,24},{17,21},{21,17},{25,29},{29,25},{1... | collective-permute-start | bytes 1271816 | tf_op jit(solution)/shard_map/ppermute | solution.py:38
  597.4 74.4 %reduce-scatter.31.cloned.1.call-start = ((), (), s32[]{:S(2)}) async-start(), calls=%async_computation.19 | async-start | bytes 1566720
  597.4 30.8 %collective-permute-start.65 = (bf16[4,72,2176]{2,1,0:T(8,128)(2,1)}, bf16[4,72,2176]{2,1,0:T(8,128)(2,1)}, u32[]{:S(2)}, u32[]{:S(2)}) collective-permute-start(bf16[4,72,2176]{2,1,0:T(8,128)(2,1)} %copy-done.137), channel_id=1, source_target_pairs={{0,8},{4,12},{8,0},{12,4},{16,20},{20,16},{24,28},{28,24},{1,9},{5... | collective-permute-start | bytes 3760136 | tf_op jit(solution)/shard_map/ppermute | solution.py:38
  623.2 26.0 %collective-permute-start.66 = (bf16[4,2,72,1728]{3,2,1,0:T(8,128)(2,1)}, bf16[4,2,72,1728]{3,2,1,0:T(8,128)(2,1)}, u32[]{:S(2)}, u32[]{:S(2)}) collective-permute-start(bf16[4,2,72,1728]{3,2,1,0:T(8,128)(2,1)} %get-tuple-element.729), channel_id=1, source_target_pairs={{0,4},{4,0},{8,12},{12,8},{16,24},{20,28},{24,16},{28,20},{1,5},{5... | collective-permute-start | bytes 5971976 | tf_op jit(solution)/shard_map/ppermute | solution.py:38
  630.9 68.5 %reduce-scatter.21.cloned.1.call-start = ((), (), s32[]{:S(2)}) async-start(), calls=%async_computation.10 | async-start | bytes 1290240 | tf_op jit(solution)/shard_map/reduce_scatter | solution.py:345
  669.8 81.4 %reduce-scatter.23.cloned.1.call-start = ((), (), s32[]{:S(2)}) async-start(), calls=%async_computation.11 | async-start | bytes 1843200 | tf_op jit(solution)/shard_map/reduce_scatter | solution.py:909
  (220 other events, 1563.5 us)
Sparse Core Ops, SparseCore 0:
  54.8 36.2 all-gather.8
  92.6 30.5 all-gather.10
  153.6 41.1 all-gather.12
  225.8 35.0 all-gather.14
  447.0 33.8 reduce-scatter.24
  483.1 29.1 reduce-scatter.26
  524.6 29.7 reduce-scatter.16
  560.1 37.6 reduce-scatter.18
  600.1 37.3 reduce-scatter.28
  640.3 29.1 reduce-scatter.30
  672.4 26.9 reduce-scatter.20
  702.3 32.3 reduce-scatter.22
